TPU v7x, 256 devices: a whole 4x4x8 slice. The times are simulated.
256 devices in a mesh: layer: 4 (over x), row: 4 (over y), col: 16 (over z, core).
Axes of the slice: x: 4, y: 4, z: 8, core: 2. Of those that a mesh axis runs over, the one named last changes fastest.
Arguments:
- values: bfloat16 [768, 20, 128, 128], P(('row', 'col')), may hold values from -1.1953125 to 1.1953125
- columns: int32 [768, 20], replicated, may hold values from 0 to 767, as said below
- counts: int32 [768], replicated, may hold values from 10 to 20, as said below
Outputs:
- square: bfloat16 [768, 20, 128, 128], P(('row', 'col'), 'layer')
Inputs may be any that keep to these rules, and one draw needn't show every extreme that they name: Row i names 20 distinct block columns, each at cyclic distance at most 12 from i modulo 768; only the first counts[i] slots are nonzero blocks. `counts`: some block row has all 20 slots live.
All inputs are finite; a program needn't handle non-finite values.
Results may differ from a plain program's by a relative error of at most 0.001.
Values may be sent and summed in bfloat16 or wider, within the bound.
No kernel may reach another device: no remote copies, remote signals or barrier semaphores. Data moves between devices by JAX's collectives and lax.ppermute only.
A program may use at most 128 MiB of HBM per device.

v0:
```python
import jax
import jax.numpy as jnp
from jax import lax
from jax.sharding import PartitionSpec as P

BAND = 12


def with_halo(block, sides, width):
    for axis, dim in sides:
        count = lax.axis_size(axis)
        forward = [(i, i + 1) for i in range(count - 1)]
        forward.append((count - 1, 0))
        backward = [(target, source) for source, target in forward]
        low = lax.ppermute(
            lax.slice_in_dim(block, block.shape[dim] - width, None, axis=dim), axis, forward
        )
        high = lax.ppermute(lax.slice_in_dim(block, 0, width, axis=dim), axis, backward)
        block = jnp.concatenate([low, block, high], axis=dim)
    return block


def lookup_terms(
    flat_blocks,
    slots_all,
    a_part,
    out_cols,
    out_live,
    term_cols,
    term_live,
    columns,
    live_mask,
    slot_ids,
    to_local,
):
    near_rows = to_local(term_cols)
    cols_far = jnp.take(columns, term_cols, axis=0)
    live_far = jnp.take(live_mask, term_cols, axis=0) & term_live[:, None]
    match = (
        (cols_far[None, :, :] == out_cols[:, None, None])
        & live_far[None, :, :]
        & out_live[:, None, None]
    )
    found = jnp.any(match, axis=2)
    which = jnp.sum(jnp.where(match, slot_ids[None, None, :], 0), axis=2)
    flat_index = near_rows[None, :] * slots_all + which
    picked = jnp.take(flat_blocks, flat_index, axis=0)
    picked = jnp.where(found[:, :, None, None], picked, jnp.zeros((), picked.dtype))
    return jnp.einsum("mab,pmbc->pac", a_part, picked, preferred_element_type=jnp.float32)


def per_device(values, columns, counts):
    rows_dev = values.shape[0]
    slots_all = values.shape[1]
    edge = values.shape[2]
    quarter = slots_all // lax.axis_size("layer")
    start_slot = lax.axis_index("layer") * quarter
    total_rows = columns.shape[0]
    first_row = lax.axis_index(("row", "col")) * rows_dev
    slot_ids = jnp.arange(slots_all, dtype=jnp.int32)
    live_mask = slot_ids[None, :] < counts[:, None]
    my_cols = lax.dynamic_slice_in_dim(columns, first_row, rows_dev, 0)
    my_live = lax.dynamic_slice_in_dim(live_mask, first_row, rows_dev, 0)

    def to_local(cols_list):
        return (cols_list - first_row + BAND) % total_rows

    padded = with_halo(values, ((("row", "col"), 0),), BAND)
    flat_blocks = padded.reshape((-1, edge, edge))

    def row_outputs(items):
        a_row, cols_row, live_row = items
        out_cols = lax.dynamic_slice_in_dim(cols_row, start_slot, quarter, 0)
        out_live = lax.dynamic_slice_in_dim(live_row, start_slot, quarter, 0)
        total = lookup_terms(
            flat_blocks,
            slots_all,
            a_row,
            out_cols,
            out_live,
            cols_row,
            live_row,
            columns,
            live_mask,
            slot_ids,
            to_local,
        )
        return total.astype(jnp.bfloat16)

    return lax.map(row_outputs, (values, my_cols, my_live))


def solution(mesh):
    return jax.shard_map(
        per_device,
        mesh=mesh,
        in_specs=(P(("row", "col"), None, None, None), P(), P()),
        out_specs=P(("row", "col"), "layer", None, None),
        check_vma=False,
    )
```

profile of v0, /device:TPU:2, one launch (start us, length us, event | category | flops | bytes accessed | tf_op | source)
XLA Modules:
  0.0 349.7 jit_solution(18320159407196092716)
XLA Ops:
  0.0 7.7 %collective-permute-start.1 = (bf16[12,20,128,128]{3,2,1,0:T(8,128)(2,1)}, bf16[12,20,128,128]{3,2,1,0:T(8,128)(2,1)}, u32[]{:S(2)}, u32[]{:S(2)}) collective-permute-start(bf16[12,20,128,128]{3,2,1,0:T(8,128)(2,1)} %param.5), channel_id=1, source_target_pairs={{1,0},{2,1},{3,2},{4,3},{5,4},{6,5},{7,6},{8,7},{9,8},{10,9},{11,1... | collective-permute-start | bytes 23592968 | tf_op jit(solution)/shard_map/ppermute | solution.py:18
  11.1 82.5 %collective-permute-done = bf16[12,20,128,128]{3,2,1,0:T(8,128)(2,1)} collective-permute-done((bf16[12,20,128,128]{3,2,1,0:T(8,128)(2,1)}, bf16[12,20,128,128]{3,2,1,0:T(8,128)(2,1)}, u32[]{:S(2)}, u32[]{:S(2)}) %collective-permute-start) | collective-permute-done | bytes 7864352 | tf_op jit(solution)/shard_map/ppermute | solution.py:15
  93.6 20.1 %pad_maximum_fusion = bf16[36,20,128,128]{3,2,1,0:T(8,128)(2,1)} fusion(bf16[12,20,128,128]{3,2,1,0:T(8,128)(2,1)} %collective-permute-done.1, bf16[12,20,128,128]{3,2,1,0:T(8,128)(2,1)} %param.5, bf16[12,20,128,128]{3,2,1,0:T(8,128)(2,1)} %collective-permute-done), kind=kLoop, calls=%fused_computation.45 | loop fusion | flops 23592960 | bytes 47185920 | tf_op jit(solution)/shard_map/concatenate | solution.py:19
  113.6 236.1 %while.14 = (s32[]{:T(128)}, bf16[12,5,128,128]{3,2,1,0:T(8,128)(2,1)}, s32[12,20]{1,0:T(8,128)S(1)}, s32[768,20]{1,0:T(8,128)}, s32[]{:T(128)}, /*index=5*/pred...) while((s32[]{:T(128)}, ...), condition=%wide.region_3.4_spmd.clone, body=%wide.region_0.3_spmd.clone.sunk | while | flops 422826976 | bytes 17903004 | solution.py:90
  116.7 8.9 %gather_fusion.2 = bf16[100,128,128]{2,1,0:T(8,128)(2,1)S(1)} fusion(bf16[720,128,128]{2,1,0:T(8,128)(2,1)} %get-tuple-element.365, s32[1024]{0:T(1024)S(1)} %pad_clamp_fusion.5), kind=kCustom, calls=%fused_computation.2.clone.clone.1 | custom fusion | bytes 6554000 | tf_op jit(solution)/shard_map/while/body/eval_jaxpr/jit(_take)/gather | solution.py:47
  125.6 3.4 copy.21
  129.3 3.1 fusion.43
  136.4 8.9 %gather_fusion.2 = bf16[100,128,128]{2,1,0:T(8,128)(2,1)S(1)} fusion(bf16[720,128,128]{2,1,0:T(8,128)(2,1)} %get-tuple-element.365, s32[1024]{0:T(1024)S(1)} %pad_clamp_fusion.5), kind=kCustom, calls=%fused_computation.2.clone.clone.1 | custom fusion | bytes 6554000 | tf_op jit(solution)/shard_map/while/body/eval_jaxpr/jit(_take)/gather | solution.py:47
  145.3 3.4 copy.21
  156.1 8.9 %gather_fusion.2 = bf16[100,128,128]{2,1,0:T(8,128)(2,1)S(1)} fusion(bf16[720,128,128]{2,1,0:T(8,128)(2,1)} %get-tuple-element.365, s32[1024]{0:T(1024)S(1)} %pad_clamp_fusion.5), kind=kCustom, calls=%fused_computation.2.clone.clone.1 | custom fusion | bytes 6554000 | tf_op jit(solution)/shard_map/while/body/eval_jaxpr/jit(_take)/gather | solution.py:47
  164.9 3.4 copy.21
  168.7 3.1 fusion.43
  175.7 8.9 %gather_fusion.2 = bf16[100,128,128]{2,1,0:T(8,128)(2,1)S(1)} fusion(bf16[720,128,128]{2,1,0:T(8,128)(2,1)} %get-tuple-element.365, s32[1024]{0:T(1024)S(1)} %pad_clamp_fusion.5), kind=kCustom, calls=%fused_computation.2.clone.clone.1 | custom fusion | bytes 6554000 | tf_op jit(solution)/shard_map/while/body/eval_jaxpr/jit(_take)/gather | solution.py:47
  184.6 3.4 copy.21
  188.3 3.1 fusion.43
  195.4 8.9 %gather_fusion.2 = bf16[100,128,128]{2,1,0:T(8,128)(2,1)S(1)} fusion(bf16[720,128,128]{2,1,0:T(8,128)(2,1)} %get-tuple-element.365, s32[1024]{0:T(1024)S(1)} %pad_clamp_fusion.5), kind=kCustom, calls=%fused_computation.2.clone.clone.1 | custom fusion | bytes 6554000 | tf_op jit(solution)/shard_map/while/body/eval_jaxpr/jit(_take)/gather | solution.py:47
  204.3 3.4 copy.21
  215.1 8.9 %gather_fusion.2 = bf16[100,128,128]{2,1,0:T(8,128)(2,1)S(1)} fusion(bf16[720,128,128]{2,1,0:T(8,128)(2,1)} %get-tuple-element.365, s32[1024]{0:T(1024)S(1)} %pad_clamp_fusion.5), kind=kCustom, calls=%fused_computation.2.clone.clone.1 | custom fusion | bytes 6554000 | tf_op jit(solution)/shard_map/while/body/eval_jaxpr/jit(_take)/gather | solution.py:47
  224.0 3.4 copy.21
  234.7 8.9 %gather_fusion.2 = bf16[100,128,128]{2,1,0:T(8,128)(2,1)S(1)} fusion(bf16[720,128,128]{2,1,0:T(8,128)(2,1)} %get-tuple-element.365, s32[1024]{0:T(1024)S(1)} %pad_clamp_fusion.5), kind=kCustom, calls=%fused_computation.2.clone.clone.1 | custom fusion | bytes 6554000 | tf_op jit(solution)/shard_map/while/body/eval_jaxpr/jit(_take)/gather | solution.py:47
  243.6 3.4 copy.21
  254.4 8.9 %gather_fusion.2 = bf16[100,128,128]{2,1,0:T(8,128)(2,1)S(1)} fusion(bf16[720,128,128]{2,1,0:T(8,128)(2,1)} %get-tuple-element.365, s32[1024]{0:T(1024)S(1)} %pad_clamp_fusion.5), kind=kCustom, calls=%fused_computation.2.clone.clone.1 | custom fusion | bytes 6554000 | tf_op jit(solution)/shard_map/while/body/eval_jaxpr/jit(_take)/gather | solution.py:47
  263.3 3.4 copy.21
  274.1 8.9 %gather_fusion.2 = bf16[100,128,128]{2,1,0:T(8,128)(2,1)S(1)} fusion(bf16[720,128,128]{2,1,0:T(8,128)(2,1)} %get-tuple-element.365, s32[1024]{0:T(1024)S(1)} %pad_clamp_fusion.5), kind=kCustom, calls=%fused_computation.2.clone.clone.1 | custom fusion | bytes 6554000 | tf_op jit(solution)/shard_map/while/body/eval_jaxpr/jit(_take)/gather | solution.py:47
  283.0 3.4 copy.21
  286.7 3.1 fusion.43
  293.8 8.9 %gather_fusion.2 = bf16[100,128,128]{2,1,0:T(8,128)(2,1)S(1)} fusion(bf16[720,128,128]{2,1,0:T(8,128)(2,1)} %get-tuple-element.365, s32[1024]{0:T(1024)S(1)} %pad_clamp_fusion.5), kind=kCustom, calls=%fused_computation.2.clone.clone.1 | custom fusion | bytes 6554000 | tf_op jit(solution)/shard_map/while/body/eval_jaxpr/jit(_take)/gather | solution.py:47
  302.7 3.4 copy.21
  313.4 8.9 %gather_fusion.2 = bf16[100,128,128]{2,1,0:T(8,128)(2,1)S(1)} fusion(bf16[720,128,128]{2,1,0:T(8,128)(2,1)} %get-tuple-element.365, s32[1024]{0:T(1024)S(1)} %pad_clamp_fusion.5), kind=kCustom, calls=%fused_computation.2.clone.clone.1 | custom fusion | bytes 6554000 | tf_op jit(solution)/shard_map/while/body/eval_jaxpr/jit(_take)/gather | solution.py:47
  322.3 3.4 copy.21
  333.1 8.9 %gather_fusion.2 = bf16[100,128,128]{2,1,0:T(8,128)(2,1)S(1)} fusion(bf16[720,128,128]{2,1,0:T(8,128)(2,1)} %get-tuple-element.365, s32[1024]{0:T(1024)S(1)} %pad_clamp_fusion.5), kind=kCustom, calls=%fused_computation.2.clone.clone.1 | custom fusion | bytes 6554000 | tf_op jit(solution)/shard_map/while/body/eval_jaxpr/jit(_take)/gather | solution.py:47
  342.0 3.4 copy.21
  (257 shorter events, 78.3 us)
Async XLA Ops:
  0.0 93.6 %collective-permute-start = (bf16[12,20,128,128]{3,2,1,0:T(8,128)(2,1)}, bf16[12,20,128,128]{3,2,1,0:T(8,128)(2,1)}, u32[]{:S(2)}, u32[]{:S(2)}) collective-permute-start(bf16[12,20,128,128]{3,2,1,0:T(8,128)(2,1)} %param.5), channel_id=1, source_target_pairs={{0,1},{1,2},{2,3},{3,4},{4,5},{5,6},{6,7},{7,8},{8,9},{9,10},{10,1... | collective-permute-start | bytes 23592968 | tf_op jit(solution)/shard_map/ppermute | solution.py:15
  0.0 93.6 %collective-permute-start.1 = (bf16[12,20,128,128]{3,2,1,0:T(8,128)(2,1)}, bf16[12,20,128,128]{3,2,1,0:T(8,128)(2,1)}, u32[]{:S(2)}, u32[]{:S(2)}) collective-permute-start(bf16[12,20,128,128]{3,2,1,0:T(8,128)(2,1)} %param.5), channel_id=1, source_target_pairs={{1,0},{2,1},{3,2},{4,3},{5,4},{6,5},{7,6},{8,7},{9,8},{10,9},{11,1... | collective-permute-start | bytes 23592968 | tf_op jit(solution)/shard_map/ppermute | solution.py:18
  11.1 102.5 %copy-start = (s32[768]{0:T(1024)S(1)}, s32[768]{0:T(1024)}, u32[]{:S(2)}) copy-start(s32[768]{0:T(1024)} %param.7) | copy-start | bytes 9220
where the time goes:
time: 351 us; the launch traced here: 350 us
  local copies, waits for them, and re-layouts  190 us (54%)
  waiting for transfers between devices  82.5 us (24%)
  matrix products  37.8 us (11%)
  other arithmetic  31 us (9%)
  starting transfers between devices  7.75 us (2%)
    gather x24, local copies, waits for them, and re-layouts, lookup_terms(): picked = jnp.take(flat_blocks, flat_index, axis=0)  148 us
    ppermute x1, waiting for transfers between devices, with_halo(): lax.ppermute(lax.slice_in_dim(block, block.shape[dim] - width, None, axis...  82.5 us
    dot_general x12, matrix products, lookup_terms(): jnp.einsum('mab,pmbc->pac', a_part, picked, preferred_element_type=jnp.fl...  37.8 us
    concatenate x1, other arithmetic, with_halo(): block = jnp.concatenate([low, block, high], axis=dim)  20.1 us
    gather x12, local copies, waits for them, and re-layouts, lookup_terms(): cols_far = jnp.take(columns, term_cols, axis=0)  18.7 us
    dynamic_update_slice x24, local copies, waits for them, and re-layouts, per_device(): return lax.map(row_outputs, (values, my_cols, my_live))  10.3 us
    ppermute x1, starting transfers between devices, with_halo(): lax.ppermute(lax.slice_in_dim(block, 0, width, axis=dim), axis, backward)  7.75 us
  transfers between devices with their start and end apart: 2, of which 1 were waited for; matrix products, arithmetic and copies ran while one was open for 1% of the time, Pallas kernels for 0%

commit v1 on v0

v1 whole, which is shorter than its diff:
```python
import functools

import jax
import jax.numpy as jnp
from jax import lax
from jax.experimental import pallas as pl
from jax.experimental.pallas import tpu as pltpu
from jax.sharding import PartitionSpec as P

BAND = 12
STRIDE = 64
UNROLL = 4
FIRST = 104
ANY = pl.BlockSpec(memory_space=pl.ANY)
SMEM = pl.BlockSpec(memory_space=pltpu.SMEM)
VMEM = pl.BlockSpec(memory_space=pltpu.VMEM)


def pack_kernel(start, size, idx_ref, blocks_ref, out_ref, held, read_sem, write_sem):
    group = 8

    def read(g, carry):
        for u in range(group):
            p = g * group + u
            pltpu.make_async_copy(
                blocks_ref.at[idx_ref[start + p]], held.at[p], read_sem.at[g]
            ).start()
        return carry

    lax.fori_loop(0, size // group, read, 0)

    def write(g, carry):
        part = pl.ds(g * group, group)
        pltpu.make_async_copy(
            blocks_ref.at[pl.ds(0, group)], held.at[part], read_sem.at[g]
        ).wait()
        pltpu.make_async_copy(held.at[part], out_ref.at[part], write_sem).start()
        return carry

    lax.fori_loop(0, size // group, write, 0)
    pltpu.make_async_copy(held, out_ref, write_sem).wait()


def pack(idx, blocks, start, size):
    shape = (size,) + blocks.shape[1:]
    return pl.pallas_call(
        functools.partial(pack_kernel, start, size),
        out_shape=jax.ShapeDtypeStruct(shape, blocks.dtype),
        in_specs=[SMEM, ANY],
        out_specs=ANY,
        scratch_shapes=[
            pltpu.VMEM(shape, blocks.dtype),
            pltpu.SemaphoreType.DMA((size // 8,)),
            pltpu.SemaphoreType.DMA,
        ],
        compiler_params=pltpu.CompilerParams(vmem_limit_bytes=8 << 20),
        name="pack",
    )(idx, blocks)


def run_list(entries, length, a_ref, v_ref, acc_ref):
    def step(t, carry):
        parts = []
        for u in range(UNROLL):
            e0 = entries[(t * UNROLL + u) * 2]
            e1 = entries[(t * UNROLL + u) * 2 + 1]
            lhs = jnp.concatenate(
                [a_ref[(e0 >> 10) & 255], a_ref[(e1 >> 10) & 255]], axis=1
            )
            rhs = jnp.concatenate([v_ref[e0 & 1023], v_ref[e1 & 1023]], axis=0)
            parts.append(
                (e0 >> 18, jnp.dot(lhs, rhs, preferred_element_type=jnp.float32))
            )
        for out, part in parts:
            acc_ref[out] += part
        return carry

    lax.fori_loop(0, length // (2 * UNROLL), step, 0)


def local_kernel(
    rows,
    slots,
    quarter,
    first,
    params_ref,
    table_ref,
    place_ref,
    blocks_ref,
    inner_ref,
    acc_ref,
    near_ref,
    extra_ref,
    sizes_ref,
    own_ref,
    v_ref,
    sem,
):
    count = rows * slots
    zero_at = 2 * count
    outs = rows * quarter
    loads = [
        pltpu.make_async_copy(ref, v_ref.at[pl.ds(at, count)], sem.at[n])
        for n, (ref, at) in enumerate(((blocks_ref, 0), (inner_ref, count)))
    ]
    for load in loads:
        load.start()
    v_ref[zero_at] = jnp.zeros(v_ref.shape[1:], v_ref.dtype)

    def clear(o, carry):
        acc_ref[o] = jnp.zeros(acc_ref.shape[1:], acc_ref.dtype)
        return carry

    lax.fori_loop(0, outs + 1, clear, 0)
    start_slot = params_ref[0]

    def one_output(o, ends):
        i = o // quarter
        p = start_slot + o % quarter
        j_at = place_ref[i * slots + p]
        alive = j_at < 3 * rows

        def terms(ends):
            e_own, e_near, e_extra = ends
            for m in range(slots):
                k_at = place_ref[i * slots + m]
                b = table_ref[k_at * STRIDE + j_at - k_at + 2 * BAND]
                tag = (o << 18) | ((i * slots + m) << 10)
                kind = b >> 10
                entry = tag | (b & 1023)
                own_ref[e_own] = entry
                near_ref[e_near] = entry
                extra_ref[e_extra] = entry
                e_own += jnp.where(kind == 1, 1, 0)
                e_near += jnp.where(kind == 2, 1, 0)
                e_extra += jnp.where(kind == 3, 1, 0)
            tag = (o << 18) | ((i * slots) << 10)
            own_ref[e_own] = tag | zero_at
            near_ref[e_near] = tag | first
            extra_ref[e_extra] = tag | (BOUND - first)
            return (
                e_own + (e_own & 1),
                e_near + (e_near & 1),
                e_extra + (e_extra & 1),
            )

        return lax.cond(alive, terms, lambda ends: ends, ends)

    zero = jnp.int32(0)
    e_own, e_near, e_extra = lax.fori_loop(0, outs, one_output, (zero, zero, zero))
    for u in range(2 * UNROLL):
        own_ref[e_own + u] = (outs << 18) | zero_at
        near_ref[e_near + u] = (outs << 18) | first
        extra_ref[e_extra + u] = (outs << 18) | (BOUND - first)
    size = 2 * UNROLL
    sizes_ref[0] = (e_near + size - 1) // size * size
    sizes_ref[1] = (e_extra + size - 1) // size * size
    for load in loads:
        load.wait()
    run_list(own_ref, (e_own + size - 1) // size * size, v_ref, v_ref, acc_ref)


BOUND = 200


def local_products(params, table, place, blocks, inner, rows, slots, quarter):
    edge = blocks.shape[-1]
    outs = rows * quarter
    length = outs * slots + 4 * UNROLL
    int_list = jax.ShapeDtypeStruct((length,), jnp.int32)
    return pl.pallas_call(
        functools.partial(local_kernel, rows, slots, quarter, FIRST),
        out_shape=(
            jax.ShapeDtypeStruct((outs + 1, edge, edge), jnp.float32),
            int_list,
            int_list,
            jax.ShapeDtypeStruct((8,), jnp.int32),
        ),
        in_specs=[SMEM, SMEM, SMEM, ANY, ANY],
        out_specs=(VMEM, SMEM, SMEM, SMEM),
        scratch_shapes=[
            pltpu.SMEM((length,), jnp.int32),
            pltpu.VMEM((2 * rows * slots + 1, edge, edge), blocks.dtype),
            pltpu.SemaphoreType.DMA((2,)),
        ],
        compiler_params=pltpu.CompilerParams(vmem_limit_bytes=26 << 20),
        cost_estimate=pl.CostEstimate(
            flops=10 * 10**9, bytes_accessed=24 * 10**6, transcendentals=0
        ),
        name="local_products",
    )(params, table, place, blocks, inner)


def remote_kernel(chunks, outs, *refs):
    sizes_ref = refs[0]
    lists = refs[1 : 1 + chunks]
    acc_in, blocks_ref = refs[1 + chunks : 3 + chunks]
    halos = refs[3 + chunks : 3 + 2 * chunks]
    out_ref = refs[3 + 2 * chunks]
    a_ref, acc_ref = refs[4 + 2 * chunks : 6 + 2 * chunks]
    stores = refs[6 + 2 * chunks : 6 + 3 * chunks]
    sem = refs[6 + 3 * chunks]
    pairs = [(acc_in, acc_ref), (blocks_ref, a_ref)]
    for halo, store in zip(halos, stores):
        pairs.append((halo, store.at[pl.ds(0, halo.shape[0])]))
    copies = [
        pltpu.make_async_copy(source, target, sem.at[n])
        for n, (source, target) in enumerate(pairs)
    ]
    for copy in copies:
        copy.start()
    for halo, store in zip(halos, stores):
        store[halo.shape[0]] = jnp.zeros(store.shape[1:], store.dtype)
    for copy in copies:
        copy.wait()
    for c in range(chunks):
        run_list(lists[c], sizes_ref[c], a_ref, stores[c], acc_ref)

    def finish(o, carry):
        out_ref[o] = acc_ref[o].astype(out_ref.dtype)
        return carry

    lax.fori_loop(0, outs, finish, 0, unroll=2)


def remote_products(sizes, lists, acc, blocks, halos, outs):
    chunks = len(lists)
    edge = blocks.shape[-1]
    return pl.pallas_call(
        functools.partial(remote_kernel, chunks, outs),
        out_shape=jax.ShapeDtypeStruct((outs, edge, edge), blocks.dtype),
        in_specs=[SMEM] * (1 + chunks) + [ANY] * (2 + chunks),
        out_specs=VMEM,
        scratch_shapes=[
            pltpu.VMEM(blocks.shape, blocks.dtype),
            pltpu.VMEM((outs + 1, edge, edge), jnp.float32),
        ]
        + [
            pltpu.VMEM((halo.shape[0] + 1, edge, edge), blocks.dtype) for halo in halos
        ]
        + [pltpu.SemaphoreType.DMA((2 + chunks,))],
        compiler_params=pltpu.CompilerParams(vmem_limit_bytes=26 << 20),
        name="remote_products",
    )(sizes, *lists, acc, blocks, *halos)


def or_reduce(x, axis):
    return lax.reduce(x, jnp.uint32(0), lax.bitwise_or, (axis,))


def bit_masks(off, live):
    bits = jnp.where(live, jnp.uint32(1) << off.astype(jnp.uint32), jnp.uint32(0))
    return or_reduce(bits, 1), bits


def needed(k_mask, i_mask, i_part, later):
    rows = k_mask.shape[-1]
    kk = lax.broadcasted_iota(jnp.int32, (rows, rows), 0)
    ii = lax.broadcasted_iota(jnp.int32, (rows, rows), 1)
    ahead = ii - kk if later else kk - ii
    valid = ahead <= 0
    shift = jnp.where(valid, rows + ahead, 0).astype(jnp.uint32)
    at = BAND - shift if later else BAND + shift
    has = valid & (((i_mask[..., None, :] >> at) & 1) == 1)
    moved = i_part[..., None, :] << shift if later else i_part[..., None, :] >> shift
    return k_mask & or_reduce(jnp.where(has, moved, jnp.uint32(0)), moved.ndim - 1)


def most_needed(columns, counts, layers):
    total_rows, slots = columns.shape
    quarter = slots // layers
    rows_id = jnp.arange(total_rows, dtype=jnp.int32)
    off = (columns - rows_id[:, None] + BAND) % total_rows
    slot_ids = jnp.arange(slots, dtype=jnp.int32)
    live = slot_ids[None, :] < counts[:, None]
    mask, bits = bit_masks(off, live)
    part = jnp.stack(
        [or_reduce(bits[:, q * quarter : (q + 1) * quarter], 1) for q in range(layers)]
    )
    mask_wrap = jnp.concatenate([mask[-BAND:], mask, mask[:BAND]])
    part_wrap = jnp.concatenate([part[:, -BAND:], part, part[:, :BAND]], axis=1)
    kk = rows_id % BAND
    up = jnp.zeros_like(part)
    down = jnp.zeros_like(part)
    for s in range(1, BAND + 1):
        i_mask = mask_wrap[BAND + s : BAND + s + total_rows]
        i_part = part_wrap[:, BAND + s : BAND + s + total_rows]
        has = (((i_mask >> (BAND - s)) & 1) == 1) & (kk + s >= BAND)
        up = up | jnp.where(has, i_part << s, jnp.uint32(0))
        i_mask = mask_wrap[BAND - s : BAND - s + total_rows]
        i_part = part_wrap[:, BAND - s : BAND - s + total_rows]
        has = (((i_mask >> (BAND + s)) & 1) == 1) & (kk - s < 0)
        down = down | jnp.where(has, i_part >> s, jnp.uint32(0))
    odd = (rows_id // BAND) % 2 == 1
    asked = jnp.where(odd, up, down) & mask
    per_row = lax.population_count(asked).astype(jnp.int32)
    return jnp.max(jnp.sum(per_row.reshape(layers, -1, BAND), axis=2))


def per_device(values, columns, counts):
    rows, slots, edge, _ = values.shape
    layers = lax.axis_size("layer")
    quarter = slots // layers
    start_slot = lax.axis_index("layer") * quarter
    total_rows = columns.shape[0]
    group = lax.axis_index(("row", "col"))
    groups = lax.axis_size(("row", "col"))
    even = group % 2 == 0
    first_row = group * rows
    blocks = values.reshape((-1, edge, edge))
    span = rows * slots

    inner = lax.ppermute(blocks, ("row", "col"), [(g, g ^ 1) for g in range(groups)])

    all_cols = jnp.concatenate([columns[-rows:], columns, columns[:rows]], axis=0)
    all_counts = jnp.concatenate([counts[-rows:], counts, counts[:rows]], axis=0)
    cols = lax.dynamic_slice_in_dim(all_cols, first_row, 3 * rows, 0)
    cnts = lax.dynamic_slice_in_dim(all_counts, first_row, 3 * rows, 0)
    row_ids = first_row - rows + jnp.arange(3 * rows, dtype=jnp.int32)
    off = (cols - row_ids[:, None] + BAND) % total_rows
    slot_ids = jnp.arange(slots, dtype=jnp.int32)[None, :]
    live = slot_ids < cnts[:, None]
    mask, bits = bit_masks(off, live)
    mine = (slot_ids >= start_slot) & (slot_ids < start_slot + quarter)
    part = or_reduce(jnp.where(mine, bits, jnp.uint32(0)), 1)
    mask = mask.reshape(3, rows)
    part = part.reshape(3, rows)
    off = off.reshape(3, rows, slots)
    live = live.reshape(3, rows, slots)

    def pair(x):
        return jnp.where(even, x[:2], x[1:])

    mask2, part2, off2, live2 = pair(mask), pair(part), pair(off), pair(live)
    ask = jnp.stack(
        [
            needed(mask2[0], mask2[1], part2[1], True),
            needed(mask2[1], mask2[0], part2[0], False),
        ]
    )
    need = (((ask[:, :, None] >> off2.astype(jnp.uint32)) & 1) == 1) & live2
    need = jnp.stack([need[0, ::-1], need[1]]).reshape(2, span)
    before = (
        lax.broadcasted_iota(jnp.int32, (span, span), 0)
        < lax.broadcasted_iota(jnp.int32, (span, span), 1)
    ).astype(jnp.bfloat16)
    pos = jnp.dot(
        need.astype(jnp.bfloat16), before, preferred_element_type=jnp.float32
    ).astype(jnp.int32)
    ids = jnp.arange(span, dtype=jnp.int32)
    ids_up = (rows - 1 - ids // slots) * slots + ids % slots
    give, give_pos = jnp.where(even, need[1], need[0]), jnp.where(even, pos[1], pos[0])
    give_ids = jnp.where(even, ids, ids_up)
    get, get_pos = jnp.where(even, need[0], need[1]), jnp.where(even, pos[0], pos[1])
    hit = give[:, None] & (
        give_pos[:, None] == jnp.arange(BOUND, dtype=jnp.int32)[None, :]
    )
    send_idx = jnp.sum(jnp.where(hit, give_ids[:, None], 0), axis=0)

    outer_pairs = [
        (g, (g - 1) % groups if g % 2 == 0 else (g + 1) % groups) for g in range(groups)
    ]
    outer = lax.ppermute(pack(send_idx, blocks, 0, FIRST), ("row", "col"), outer_pairs)

    code = jnp.where(get_pos < FIRST, (2 << 10) + get_pos, (3 << 10) + get_pos - FIRST)
    code = jnp.where(get, code, 0).reshape(rows, slots)
    code = jnp.where(even, code[::-1], code)
    ids = ids.reshape(rows, slots)
    own = jnp.where(live[1], (1 << 10) + ids, 0)
    near = jnp.where(even, live[2], live[0])
    near = jnp.where(near, (1 << 10) + span + ids, 0)
    codes = jnp.concatenate(
        [jnp.where(even, code, near), own, jnp.where(even, near, code)], axis=0
    )
    off3 = off.reshape(3 * rows, slots)
    at = lax.broadcasted_iota(jnp.int32, (1, 1, STRIDE), 2)
    table = jnp.sum(
        jnp.where(off3[:, :, None] + BAND == at, codes[:, :, None], 0), axis=1
    ).reshape(-1)
    table = jnp.concatenate([table, jnp.zeros((STRIDE,), jnp.int32)])
    place = jnp.where(
        live[1], jnp.arange(rows, dtype=jnp.int32)[:, None] + off[1], 3 * rows
    ).reshape(-1)
    params = jnp.full((8,), start_slot, jnp.int32)

    acc, near, extra, sizes = local_products(
        params, table, place, blocks, inner, rows, slots, quarter
    )
    outs = rows * quarter
    more = most_needed(columns, counts, layers) > FIRST

    def with_extra():
        late = pack(send_idx, blocks, FIRST, BOUND - FIRST)
        late = lax.ppermute(late, ("row", "col"), outer_pairs)
        return remote_products(sizes, [near, extra], acc, blocks, [outer, late], outs)

    def without():
        return remote_products(sizes, [near], acc, blocks, [outer], outs)

    square = lax.cond(more, with_extra, without)
    return square.reshape(rows, quarter, edge, edge)


def solution(mesh):
    return jax.shard_map(
        per_device,
        mesh=mesh,
        in_specs=(P(("row", "col"), None, None, None), P(), P()),
        out_specs=P(("row", "col"), "layer", None, None),
        check_vma=False,
    )
```

time: 351 us -> 65.7 us (0.19)
  local copies, waits for them, and re-layouts: 190 us -> 5.39 us
  waiting for transfers between devices: 82.5 us -> 4.99 us
  Pallas kernels: 0 us -> 38.3 us
  matrix products: 37.8 us -> 0.15 us
  other arithmetic: 31 us -> 6.41 us
    gather x48 -> x0, local copies, waits for them, and re-layouts: 174 us -> none  [the longest x24 148 us: lookup_terms(): picked = jnp.take(flat_blocks, flat_index, axis=0)]
    ppermute x2, waiting for transfers between devices: 82.5 us -> 4.99 us  [the longest x1 4.99 us: per_device(): lax.ppermute(pack(send_idx, blocks, 0, FIRST), ('row', 'col'), outer_pairs)]
    pallas_call x0 -> x3, Pallas kernels: none -> 38.3 us  [the longest x1 26.7 us: local_products(): pl.pallas_call(functools.partial(local_kernel, rows, slots, quarter, FIRS...]
    dot_general x12 -> x1, matrix products: 37.8 us -> 0.15 us  [per_device(): jnp.dot(need.astype(jnp.bfloat16), before, preferred_element_type=jnp.flo...]
    concatenate x1 -> x4, other arithmetic: 20.1 us -> 1.02 us  [the longest x1 0.76 us: per_device(): jnp.concatenate([counts[-rows:], counts, counts[:rows]], axis=0)]
    dynamic_update_slice x24 -> x0, local copies, waits for them, and re-layouts: 10.3 us -> none  [per_device(): return lax.map(row_outputs, (values, my_cols, my_live))]
  transfers between devices with their start and end apart: 2 -> 2, of which waited for: 1 -> 1; matrix products, arithmetic and copies ran while one was open for 1% -> 16% of each run, Pallas kernels for 0% -> 46%
where the time goes in v1:
time: 65.7 us; the launch traced here: 64.9 us
  Pallas kernels  38.3 us (58%)
  starting transfers between devices  8.71 us (13%)
  other arithmetic  6.41 us (10%)
  local copies, waits for them, and re-layouts  5.39 us (8%)
  waiting for transfers between devices  4.99 us (8%)
  between operations  0.96 us (1%)
    pallas_call x1, Pallas kernels, local_products(): pl.pallas_call(functools.partial(local_kernel, rows, slots, quarter, FIRS...  26.7 us
    ppermute x1, starting transfers between devices, per_device(): lax.ppermute(pack(send_idx, blocks, 0, FIRST), ('row', 'col'), outer_pairs)  8.7 us
    pallas_call x1, Pallas kernels, remote_products(): pl.pallas_call(functools.partial(remote_kernel, chunks, outs), out_shape=...  8.2 us
    ppermute x1, waiting for transfers between devices, per_device(): lax.ppermute(pack(send_idx, blocks, 0, FIRST), ('row', 'col'), outer_pairs)  4.99 us
    pallas_call x1, Pallas kernels, pack(): pl.pallas_call(functools.partial(pack_kernel, start, size), out_shape=jax...  3.4 us
    reduce_max x1, other arithmetic, most_needed(): return jnp.max(jnp.sum(per_row.reshape(layers, -1, BAND), axis=2))  1.39 us
  transfers between devices with their start and end apart: 2, of which 1 were waited for; matrix products, arithmetic and copies ran while one was open for 16% of the time, Pallas kernels for 46%

profile of v1, /device:TPU:2, one launch (start us, length us, event | category | flops | bytes accessed | tf_op | source)
XLA Modules:
  0.0 64.9 jit_solution(4987500738686858175)
XLA Ops:
  0.0 0.8 %fusion.162 = (s32[12]{0:T(128)S(1)}, s32[12]{0:T(128)S(1)}) fusion(s32[768]{0:T(1024)} %param.7), kind=kLoop, calls=%fused_computation.282 | loop fusion | bytes 192 | tf_op jit(solution)/shard_map/slice | solution.py:316
  0.8 0.8 %pad_add_fusion.5 = s32[792]{0:T(1024)S(1)} fusion(s32[12]{0:T(128)S(1)} %get-tuple-element.75, s32[768]{0:T(1024)} %param.7, s32[12]{0:T(128)S(1)} %get-tuple-element.74), kind=kLoop, calls=%fused_computation.205 | loop fusion | flops 1584 | bytes 6336 | tf_op jit(solution)/shard_map/concatenate | solution.py:316
  1.7 0.8 %fusion.161 = (s32[12,20]{0,1:T(8,128)S(1)}, s32[12,20]{0,1:T(8,128)S(1)}) fusion(s32[768,20]{0,1:T(8,128)} %param.6), kind=kLoop, calls=%fused_computation.281 | loop fusion | bytes 3840 | tf_op jit(solution)/shard_map/slice | solution.py:315
  2.5 0.8 %broadcast_add_fusion = (s32[36,20]{0,1:T(8,128)S(1)}, s32[36,20]{0,1:T(8,128)S(1)}) fusion(s32[36]{0:T(128)S(1)} %iota_add_fusion, s32[]{:T(128)S(6)} %select_n.378, s32[12,20]{0,1:T(8,128)S(1)} %get-tuple-element.65, s32[768,20]{0,1:T(8,128)} %param.6, s32[12,20]{0,1:T(8,128)S(1)} %get-tuple-element.64), kind=kLoop, calls=%fused_computation.143 | loop fusion | flops 7920 | bytes 69268 | tf_op jit(solution)/shard_map/add | solution.py:378
  3.6 0.1 copy.25
  3.7 0.1 copy.26
  3.8 0.1 fusion.66
  4.1 0.1 select_reduce_fusion.3
  4.3 0.1 select_reduce_fusion.4
  4.6 0.1 copy.27
  4.7 0.1 reshape.193
  4.8 0.1 copy.30
  4.9 0.1 select_n.412
  5.0 0.1 convolution_convert_fusion
  5.2 0.1 select_reduce_fusion.1.idx_ref
  5.4 3.4 %pack.3 = bf16[104,128,128]{2,1,0:T(8,128)(2,1)S(1)} custom-call(s32[200]{0:T(256)S(1)} %select_reduce_fusion.1.idx_ref, bf16[240,128,128]{2,1,0:T(8,128)(2,1)} %bitcast.14), custom_call_target="tpu_custom_call" | custom-call | tf_op jit(solution)/shard_map/pack/pallas_call | solution.py:46
  8.8 8.7 %collective-permute-start.2 = (bf16[104,128,128]{2,1,0:T(8,128)(2,1)S(1)}, bf16[104,128,128]{2,1,0:T(8,128)(2,1)}, u32[]{:S(2)}, u32[]{:S(2)}) collective-permute-start(bf16[104,128,128]{2,1,0:T(8,128)(2,1)S(1)} %pack.3), channel_id=1, source_target_pairs={{0,63},{1,2},{2,1},{3,4},{4,3},{5,6},{6,5},{7,8},{8,7},{9,10},{10,... | collective-permute-start | bytes 10223624 | tf_op jit(solution)/shard_map/ppermute | solution.py:363
  17.6 0.1 copy.28
  17.9 0.3 select_reduce_fusion
  18.3 0.1 copy.29
  18.9 0.1 pad_add_fusion.1
  19.0 0.1 fusion.151
  19.1 0.1 fusion.139
  19.2 0.8 %fusion.19 = s32[4,768]{1,0:T(4,128)} fusion(u32[4,780]{1,0:T(4,128)S(1)} %get-tuple-element.69, u32[4,780]{1,0:T(4,128)S(1)} %get-tuple-element.68, u32[768]{0:T(1024)S(1)} %get-tuple-element.62, pred[768]{0:T(1024)(128)(4,1)S(1)} %get-tuple-element.93, pred[768]{0:T(1024)(128)(4,1)S(1)} %get-tuple-element.94, pred[768]{0:T(1024)(128)(4,1)S(1)} %get-tuple-element.95, ...), kind=kLoop, calls=%fused_computation.43 | loop fusion | flops 227328 | bytes 329472 | tf_op jit(solution)/shard_map/convert_element_type | solution.py:296
  20.0 0.8 %reshape.192 = s32[4,64,12]{2,1,0:T(8,128)S(1)} reshape(s32[4,768]{1,0:T(4,128)} %fusion.19) | data formatting | bytes 24576 | tf_op jit(solution)/shard_map/reshape | solution.py:297
  20.9 0.7 %reduce_sum.27 = s32[4,64]{1,0:T(4,128)} reduce(s32[4,64,12]{2,1,0:T(8,128)S(1)} %reshape.192, s32[]{:T(128)} %constant.64.clone.1), dimensions={2}, to_apply=%region_5.6 | reduce | flops 2816 | bytes 13316 | tf_op jit(solution)/shard_map/reduce_sum | solution.py:297
  21.6 1.4 %reduce_max.9 = s32[]{:T(128)} reduce(s32[4,64]{1,0:T(4,128)} %reduce_sum.27, s32[]{:T(128)} %constant.214.clone.1), dimensions={0,1}, to_apply=%region_6.7 | reduce | flops 255 | bytes 1032 | tf_op jit(solution)/shard_map/reduce_max | solution.py:297
  23.7 26.7 %local_products.1 = (f32[61,128,128]{2,1,0:T(8,128)S(1)}, s32[1216]{0:T(1024)S(1)}, s32[1216]{0:T(1024)S(1)}, s32[8]{0:T(128)S(1)}) custom-call(s32[8]{0:T(128)S(1)} %broadcast_in_dim.211.params_ref, s32[2368]{0:T(1024)S(1)} %concatenate.77.table_ref, s32[240]{0:T(256)S(1)} %reshape.198.place_ref, bf16[240,128,128]{2,1,0:T(8,128)(2,1)} %bitcast.15, ...), custom_call_target="tpu_custom_call" | custom-call | flops 10000000000 | bytes 24000000 | tf_op jit(solution)/shard_map/local_products/pallas_call | solution.py:171
  50.4 5.0 %collective-permute-done.2 = bf16[104,128,128]{2,1,0:T(8,128)(2,1)} collective-permute-done((bf16[104,128,128]{2,1,0:T(8,128)(2,1)S(1)}, bf16[104,128,128]{2,1,0:T(8,128)(2,1)}, u32[]{:S(2)}, u32[]{:S(2)}) %collective-permute-start.2) | collective-permute-done | bytes 3407904 | tf_op jit(solution)/shard_map/ppermute | solution.py:363
  55.4 8.2 %conditional.1 = (bf16[12,5,128,128]{3,2,1,0:T(8,128)(2,1)S(1)}) conditional(s32[]{:T(128)} %convert_element_type.35, (s32[8]{0:T(128)S(1)}, s32[1216]{0:T(1024)S(1)}, f32[61,128,128]{2,1,0:T(8,128)S(1)}, bf16[240,128,128]{2,1,0:T(8,128)(2,1)}, bf16[104,128,128]{2,1,0:T(8,128)(2,1)}) %tuple.64, (s32[200]{0:T(256)S(1)}, ...), branch_computations={%region_13.14_spmd, %region_14.15_spmd} | conditional | bytes 44040268 | solution.py:400
  55.4 8.2 %remote_products.2 = bf16[60,128,128]{2,1,0:T(8,128)(2,1)S(1)} custom-call(s32[8]{0:T(128)S(1)} %get-tuple-element.33.refs_0_, s32[1216]{0:T(1024)S(1)} %get-tuple-element.34.refs_1_, f32[61,128,128]{2,1,0:T(8,128)S(1)} %get-tuple-element.35.refs_2_, bf16[240,128,128]{2,1,0:T(8,128)(2,1)} %get-tuple-element.36.refs_3_, ...), custom_call_target="tpu_custom_call" | custom-call | tf_op jit(solution)/shard_map/cond/branch_0_fun/remote_products/pallas_call | solution.py:229
  63.6 1.3 %copy-done.1 = bf16[12,5,128,128]{3,2,1,0:T(8,128)(2,1)} copy-done((bf16[12,5,128,128]{3,2,1,0:T(8,128)(2,1)}, bf16[12,5,128,128]{3,2,1,0:T(8,128)(2,1)S(1)}, u32[]{:S(2)}) %copy-start.1) | copy-done | bytes 1966104
  (49 shorter events, 1.7 us)
Async XLA Ops:
  0.0 23.7 %collective-permute-start.1 = (bf16[240,128,128]{2,1,0:T(8,128)(2,1)}, bf16[240,128,128]{2,1,0:T(8,128)(2,1)}, u32[]{:S(2)}, u32[]{:S(2)}) collective-permute-start(bf16[240,128,128]{2,1,0:T(8,128)(2,1)} %bitcast.13), channel_id=1, source_target_pairs={{0,1},{1,0},{2,3},{3,2},{4,5},{5,4},{6,7},{7,6},{8,9},{9,8},{10,11... | collective-permute-start | bytes 23592968 | tf_op jit(solution)/shard_map/ppermute | solution.py:313
  5.3 3.4 %copy-start.4 = (s32[200]{0:T(256)}, s32[200]{0:T(256)S(1)}, u32[]{:S(2)}) copy-start(s32[200]{0:T(256)S(1)} %select_reduce_fusion.1.idx_ref) | copy-start | bytes 2404
  5.4 13.1 %copy-start.2 = (s32[768,20]{0,1:T(8,128)S(1)}, s32[768,20]{0,1:T(8,128)}, u32[]{:S(2)}) copy-start(s32[768,20]{0,1:T(8,128)} %param.6) | copy-start | bytes 184324
  5.4 13.1 %copy-start.3 = (s32[768]{0:T(1024)S(1)}, s32[768]{0:T(1024)}, u32[]{:S(2)}) copy-start(s32[768]{0:T(1024)} %param.7) | copy-start | bytes 9220
  8.8 46.6 %collective-permute-start.2 = (bf16[104,128,128]{2,1,0:T(8,128)(2,1)S(1)}, bf16[104,128,128]{2,1,0:T(8,128)(2,1)}, u32[]{:S(2)}, u32[]{:S(2)}) collective-permute-start(bf16[104,128,128]{2,1,0:T(8,128)(2,1)S(1)} %pack.3), channel_id=1, source_target_pairs={{0,63},{1,2},{2,1},{3,4},{4,3},{5,6},{6,5},{7,8},{8,7},{9,10},{10,... | collective-permute-start | bytes 10223624 | tf_op jit(solution)/shard_map/ppermute | solution.py:363
  23.7 31.7 %copy-start.5 = (s32[200]{0:T(256)S(1)}, s32[200]{0:T(256)}, u32[]{:S(2)}) copy-start(s32[200]{0:T(256)} %copy-done.4) | copy-start | bytes 2404
  63.6 1.3 %copy-start.1 = (bf16[12,5,128,128]{3,2,1,0:T(8,128)(2,1)}, bf16[12,5,128,128]{3,2,1,0:T(8,128)(2,1)S(1)}, u32[]{:S(2)}) copy-start(bf16[12,5,128,128]{3,2,1,0:T(8,128)(2,1)S(1)} %get-tuple-element.125) | copy-start | bytes 5898244

commit v2 on v1

v2 whole, which is shorter than its diff:
```python
import functools

import jax
import jax.numpy as jnp
from jax import lax
from jax.experimental import pallas as pl
from jax.experimental.pallas import tpu as pltpu
from jax.sharding import PartitionSpec as P

BAND = 12
STRIDE = 64
WIDE = 16
UNROLL = 4
NEAR_ROWS = 6
NEAR_SLOTS = 12
FIRST = 60
BOUND = 132
ANY = pl.BlockSpec(memory_space=pl.ANY)
SMEM = pl.BlockSpec(memory_space=pltpu.SMEM)
VMEM = pl.BlockSpec(memory_space=pltpu.VMEM)


def pack_kernel(start, size, idx_ref, blocks_ref, out_ref, held, read_sem, write_sem):
    group = 4

    def read(g, carry):
        for u in range(group):
            p = g * group + u
            pltpu.make_async_copy(
                blocks_ref.at[idx_ref[start + p]], held.at[p], read_sem.at[g]
            ).start()
        return carry

    lax.fori_loop(0, size // group, read, 0)

    def write(g, carry):
        part = pl.ds(g * group, group)
        pltpu.make_async_copy(
            blocks_ref.at[pl.ds(0, group)], held.at[part], read_sem.at[g]
        ).wait()
        pltpu.make_async_copy(held.at[part], out_ref.at[part], write_sem).start()
        return carry

    lax.fori_loop(0, size // group, write, 0)
    pltpu.make_async_copy(held, out_ref, write_sem).wait()


def pack(idx, blocks, start, size):
    shape = (size,) + blocks.shape[1:]
    return pl.pallas_call(
        functools.partial(pack_kernel, start, size),
        out_shape=jax.ShapeDtypeStruct(shape, blocks.dtype),
        in_specs=[SMEM, ANY],
        out_specs=ANY,
        scratch_shapes=[
            pltpu.VMEM(shape, blocks.dtype),
            pltpu.SemaphoreType.DMA((size // 4,)),
            pltpu.SemaphoreType.DMA,
        ],
        compiler_params=pltpu.CompilerParams(vmem_limit_bytes=8 << 20),
        name="pack",
    )(idx, blocks)


def run_list(entries, length, a_ref, v_ref, acc_ref):
    def steps(begin, count, carry):
        parts = []
        for u in range(count):
            e0 = entries[(begin + u) * 2]
            e1 = entries[(begin + u) * 2 + 1]
            lhs = jnp.concatenate(
                [a_ref[(e0 >> 10) & 255], a_ref[(e1 >> 10) & 255]], axis=1
            )
            rhs = jnp.concatenate([v_ref[e0 & 1023], v_ref[e1 & 1023]], axis=0)
            parts.append(
                (e0 >> 18, jnp.dot(lhs, rhs, preferred_element_type=jnp.float32))
            )
        for out, part in parts:
            acc_ref[out] += part
        return carry

    pairs = length // 2
    wide = pairs // WIDE
    lax.fori_loop(0, wide, lambda t, c: steps(t * WIDE, WIDE, c), 0)
    rest = (pairs - wide * WIDE) // UNROLL
    lax.fori_loop(0, rest, lambda t, c: steps(wide * WIDE + t * UNROLL, UNROLL, c), 0)


def local_kernel(
    rows,
    slots,
    quarter,
    start_ref,
    table_ref,
    place_ref,
    blocks_ref,
    inner_ref,
    acc_ref,
    far_ref,
    size_ref,
    own_ref,
    inner_v,
    sem,
):
    count = rows * slots
    outs = rows * quarter
    size = 2 * UNROLL
    load = pltpu.make_async_copy(inner_ref, inner_v.at[pl.ds(1 + count, count)], sem.at[0])
    load.start()
    load_own = pltpu.make_async_copy(blocks_ref, inner_v.at[pl.ds(1, count)], sem.at[1])
    load_own.start()
    inner_v[0] = jnp.zeros(inner_v.shape[1:], inner_v.dtype)

    def clear(o, carry):
        acc_ref[o] = jnp.zeros(acc_ref.shape[1:], acc_ref.dtype)
        return carry

    lax.fori_loop(0, outs + 1, clear, 0)
    start_slot = start_ref[0]

    def one_row(i, ends):
        base = i * slots
        row_tag = base << 10
        terms_at = [place_ref[base + m] * (STRIDE - 1) for m in range(slots)]

        def one_output(p, ends):
            j_at = place_ref[base + start_slot + p]
            tag = row_tag + ((i * quarter + p) << 18)

            def terms(ends):
                e_own, e_far = ends
                for m in range(slots):
                    code = table_ref[terms_at[m] + (j_at + 2 * BAND)]
                    entry = (code & 1023) + (tag + (m << 10))
                    own_ref[e_own] = entry
                    far_ref[e_far] = entry
                    e_own += (code >> 10) & 1
                    e_far += code >> 11
                own_ref[e_own] = tag
                far_ref[e_far] = tag
                return e_own + (e_own & 1), e_far + (e_far & 1)

            return lax.cond(j_at < 3 * rows, terms, lambda ends: ends, ends)

        return lax.fori_loop(0, quarter, one_output, ends)

    zero = jnp.int32(0)
    e_own, e_far = lax.fori_loop(0, rows, one_row, (zero, zero))
    for u in range(size):
        own_ref[e_own + u] = outs << 18
        far_ref[e_far + u] = outs << 18
    size_ref[0] = (e_far + size - 1) // size * size
    load_own.wait()
    load.wait()
    run_list(own_ref, (e_own + size - 1) // size * size, inner_v.at[pl.ds(1, count)], inner_v, acc_ref)


def local_products(start, table, place, blocks, inner, rows, slots, quarter):
    edge = blocks.shape[-1]
    outs = rows * quarter
    length = outs * slots + 4 * UNROLL
    return pl.pallas_call(
        functools.partial(local_kernel, rows, slots, quarter),
        out_shape=(
            jax.ShapeDtypeStruct((outs + 1, edge, edge), jnp.float32),
            jax.ShapeDtypeStruct((length,), jnp.int32),
            jax.ShapeDtypeStruct((8,), jnp.int32),
        ),
        in_specs=[SMEM, SMEM, SMEM, ANY, ANY],
        out_specs=(VMEM, SMEM, SMEM),
        scratch_shapes=[
            pltpu.SMEM((length,), jnp.int32),
            pltpu.VMEM((2 * rows * slots + 1, edge, edge), blocks.dtype),
            pltpu.SemaphoreType.DMA((2,)),
        ],
        compiler_params=pltpu.CompilerParams(vmem_limit_bytes=26 << 20),
        cost_estimate=pl.CostEstimate(
            flops=10 * 10**9, bytes_accessed=24 * 10**6, transcendentals=0
        ),
        name="local_products",
    )(start, table, place, blocks, inner)


def far_kernel(
    rows,
    quarter,
    more_ref,
    size_ref,
    list_ref,
    acc_in,
    blocks_ref,
    near0_ref,
    near1_ref,
    near2_ref,
    near3_ref,
    first_ref,
    late_ref,
    out_ref,
    a_ref,
    acc_ref,
    v_ref,
    held,
    sem,
):
    nears = (near0_ref, near1_ref, near2_ref, near3_ref)
    near, first, late = near0_ref.shape[0], first_ref.shape[0], late_ref.shape[0]
    at = 1 + len(nears) * near
    late_copy = pltpu.make_async_copy(
        late_ref, v_ref.at[pl.ds(at + first, late)], sem.at[3]
    )
    pairs = [(first_ref, v_ref.at[pl.ds(at, first)]), (acc_in, acc_ref), (blocks_ref, a_ref)]
    copies = [
        pltpu.make_async_copy(source, target, sem.at[n])
        for n, (source, target) in enumerate(pairs)
    ]
    me = more_ref[1]
    for away, ref in enumerate(nears):
        source = lax.rem(me + len(nears) - away, len(nears))
        copies.append(
            pltpu.make_async_copy(
                ref, v_ref.at[pl.ds(1 + source * near, near)], sem.at[5 + away]
            )
        )
    for copy in copies:
        copy.start()
    v_ref[0] = jnp.zeros(v_ref.shape[1:], v_ref.dtype)

    @pl.when(more_ref[0] > 0)
    def _():
        late_copy.start()
        late_copy.wait()

    for copy in copies:
        copy.wait()
    run_list(list_ref, size_ref[0], a_ref, v_ref, acc_ref)

    def finish(i, carry):
        part = pl.ds(i * quarter, quarter)
        held[part] = acc_ref[part].astype(held.dtype)
        pltpu.make_async_copy(held.at[part], out_ref.at[part], sem.at[4]).start()
        return carry

    lax.fori_loop(0, rows, finish, 0)
    pltpu.make_async_copy(held, out_ref, sem.at[4]).wait()


def far_products(flags, size, entries, acc, blocks, nears, first, late, rows, quarter):
    edge = blocks.shape[-1]
    outs = rows * quarter
    held = 1 + len(nears) * nears[0].shape[0] + first.shape[0] + late.shape[0]
    return pl.pallas_call(
        functools.partial(far_kernel, rows, quarter),
        out_shape=jax.ShapeDtypeStruct((outs, edge, edge), blocks.dtype),
        in_specs=[SMEM] * 3 + [ANY] * (4 + len(nears)),
        out_specs=ANY,
        scratch_shapes=[
            pltpu.VMEM(blocks.shape, blocks.dtype),
            pltpu.VMEM((outs + 1, edge, edge), jnp.float32),
            pltpu.VMEM((held, edge, edge), blocks.dtype),
            pltpu.VMEM((outs, edge, edge), blocks.dtype),
            pltpu.SemaphoreType.DMA((5 + len(nears),)),
        ],
        compiler_params=pltpu.CompilerParams(vmem_limit_bytes=26 << 20),
        name="far_products",
    )(flags, size, entries, acc, blocks, *nears, first, late)


def blank(shape, dtype):
    return pl.pallas_call(
        lambda out_ref: None,
        out_shape=jax.ShapeDtypeStruct(shape, dtype),
        out_specs=ANY,
        name="blank",
    )()


def or_reduce(x, axis):
    return lax.reduce(x, jnp.uint32(0), lax.bitwise_or, (axis,))


def bit_masks(off, live):
    bits = jnp.where(live, jnp.uint32(1) << off.astype(jnp.uint32), jnp.uint32(0))
    return or_reduce(bits, 1), bits


def needed(k_mask, i_mask, i_part, later):
    rows = k_mask.shape[-1]
    kk = lax.broadcasted_iota(jnp.int32, (rows, rows), 0)
    ii = lax.broadcasted_iota(jnp.int32, (rows, rows), 1)
    ahead = ii - kk if later else kk - ii
    valid = ahead <= 0
    shift = jnp.where(valid, rows + ahead, 0).astype(jnp.uint32)
    at = BAND - shift if later else BAND + shift
    has = valid & (((i_mask[..., None, :] >> at) & 1) == 1)
    moved = i_part[..., None, :] << shift if later else i_part[..., None, :] >> shift
    return k_mask & or_reduce(jnp.where(has, moved, jnp.uint32(0)), moved.ndim - 1)


def most_needed(columns, counts, layers):
    total_rows, slots = columns.shape
    quarter = slots // layers
    rows_id = jnp.arange(total_rows, dtype=jnp.int32)
    off = (columns - rows_id[:, None] + BAND) % total_rows
    slot_ids = jnp.arange(slots, dtype=jnp.int32)
    live = slot_ids[None, :] < counts[:, None]
    mask, bits = bit_masks(off, live)
    part = jnp.stack(
        [or_reduce(bits[:, q * quarter : (q + 1) * quarter], 1) for q in range(layers)]
    )
    mask_wrap = jnp.concatenate([mask[-BAND:], mask, mask[:BAND]])
    part_wrap = jnp.concatenate([part[:, -BAND:], part, part[:, :BAND]], axis=1)
    kk = rows_id % BAND
    up = jnp.zeros_like(part)
    down = jnp.zeros_like(part)
    for s in range(1, BAND + 1):
        i_mask = mask_wrap[BAND + s : BAND + s + total_rows]
        i_part = part_wrap[:, BAND + s : BAND + s + total_rows]
        has = (((i_mask >> (BAND - s)) & 1) == 1) & (kk + s >= BAND)
        up = up | jnp.where(has, i_part << s, jnp.uint32(0))
        i_mask = mask_wrap[BAND - s : BAND - s + total_rows]
        i_part = part_wrap[:, BAND - s : BAND - s + total_rows]
        has = (((i_mask >> (BAND + s)) & 1) == 1) & (kk - s < 0)
        down = down | jnp.where(has, i_part >> s, jnp.uint32(0))
    odd = (rows_id // BAND) % 2 == 1
    fixed = or_reduce(bits[:, :NEAR_SLOTS], 1)
    close = jnp.where(odd, kk >= BAND - NEAR_ROWS, kk < NEAR_ROWS)
    asked = jnp.where(odd, up, down) & mask & jnp.where(close, ~fixed, ~jnp.uint32(0))
    per_row = lax.population_count(asked).astype(jnp.bfloat16)
    member = rows_id[:, None] // BAND == jnp.arange(total_rows // BAND)[None, :]
    per_group = jnp.dot(
        per_row, member.astype(jnp.bfloat16), preferred_element_type=jnp.float32
    )
    return jnp.max(per_group)


def per_device(values, columns, counts):
    rows, slots, edge, _ = values.shape
    layers = lax.axis_size("layer")
    quarter = slots // layers
    start_slot = lax.axis_index("layer") * quarter
    total_rows = columns.shape[0]
    group = lax.axis_index(("row", "col"))
    groups = lax.axis_size(("row", "col"))
    even = group % 2 == 0
    first_row = group * rows
    blocks = values.reshape((-1, edge, edge))
    span = rows * slots

    inner = lax.ppermute(blocks, ("row", "col"), [(g, g ^ 1) for g in range(groups)])

    share = NEAR_SLOTS // layers
    layer = lax.axis_index("layer")
    outer_pairs = [
        (g, (g - 1) % groups if g % 2 == 0 else (g + 1) % groups) for g in range(groups)
    ]
    near_rows = lax.dynamic_slice(
        values,
        (jnp.where(even, 0, rows - NEAR_ROWS), layer * share, 0, 0),
        (NEAR_ROWS, share, edge, edge),
    ).reshape(-1, edge, edge)
    near_mine = lax.ppermute(near_rows, ("row", "col"), outer_pairs)
    all_cols = jnp.concatenate([columns[-rows:], columns, columns[:rows]], axis=0)
    all_counts = jnp.concatenate([counts[-rows:], counts, counts[:rows]], axis=0)
    cols = lax.dynamic_slice_in_dim(all_cols, first_row, 3 * rows, 0)
    cnts = lax.dynamic_slice_in_dim(all_counts, first_row, 3 * rows, 0)
    row_ids = first_row - rows + jnp.arange(3 * rows, dtype=jnp.int32)
    off = (cols - row_ids[:, None] + BAND) % total_rows
    slot_ids = jnp.arange(slots, dtype=jnp.int32)[None, :]
    live = slot_ids < cnts[:, None]
    mask, bits = bit_masks(off, live)
    mine = (slot_ids >= start_slot) & (slot_ids < start_slot + quarter)
    part = or_reduce(jnp.where(mine, bits, jnp.uint32(0)), 1)
    mask = mask.reshape(3, rows)
    part = part.reshape(3, rows)
    off = off.reshape(3, rows, slots)
    live = live.reshape(3, rows, slots)

    def pair(x):
        return jnp.where(even, x[:2], x[1:])

    mask2, part2, off2, live2 = pair(mask), pair(part), pair(off), pair(live)
    ask = jnp.stack(
        [
            needed(mask2[0], mask2[1], part2[1], True),
            needed(mask2[1], mask2[0], part2[0], False),
        ]
    )
    need = (((ask[:, :, None] >> off2.astype(jnp.uint32)) & 1) == 1) & live2
    fixed = (jnp.arange(rows)[:, None] < NEAR_ROWS) & (slot_ids < NEAR_SLOTS)
    need = jnp.stack([need[0, ::-1], need[1]]) & ~fixed
    need = need.reshape(2, span)
    before = (
        lax.broadcasted_iota(jnp.int32, (span, span), 0)
        < lax.broadcasted_iota(jnp.int32, (span, span), 1)
    ).astype(jnp.bfloat16)
    pos = jnp.dot(
        need.astype(jnp.bfloat16), before, preferred_element_type=jnp.float32
    ).astype(jnp.int32)
    ids = jnp.arange(span, dtype=jnp.int32)
    ids_up = (rows - 1 - ids // slots) * slots + ids % slots
    give, give_pos = jnp.where(even, need[1], need[0]), jnp.where(even, pos[1], pos[0])
    give_ids = jnp.where(even, ids, ids_up)
    get, get_pos = jnp.where(even, need[0], need[1]), jnp.where(even, pos[0], pos[1])
    hit = give[:, None] & (
        give_pos[:, None] == jnp.arange(BOUND, dtype=jnp.int32)[None, :]
    )
    send_idx = jnp.sum(jnp.where(hit, give_ids[:, None], 0), axis=0)

    columns, counts, send_idx, near_mine = lax.optimization_barrier(
        (columns, counts, send_idx, near_mine)
    )
    nears = [near_mine] + [
        lax.ppermute(near_mine, "layer", [(x, (x + d) % layers) for x in range(layers)])
        for d in range(1, layers)
    ]
    packed = pack(send_idx, blocks, 0, FIRST)
    outer = lax.ppermute(packed, ("row", "col"), outer_pairs)

    code = jnp.where(get, (2 << 10) + 1 + NEAR_ROWS * NEAR_SLOTS + get_pos, 0)
    code = jnp.where(even, code.reshape(rows, slots)[::-1], code.reshape(rows, slots))
    row_at = jnp.arange(rows, dtype=jnp.int32)[:, None] - jnp.where(even, rows - NEAR_ROWS, 0)
    sent = (row_at >= 0) & (row_at < NEAR_ROWS) & (slot_ids < NEAR_SLOTS)
    sent_at = (slot_ids // share * NEAR_ROWS + row_at) * share + slot_ids % share
    far_live = jnp.where(even, live[0], live[2])
    code = jnp.where(sent & far_live, (2 << 10) + 1 + sent_at, code)
    ids = ids.reshape(rows, slots)
    own = jnp.where(live[1], (1 << 10) + 1 + ids, 0)
    near = jnp.where(even, live[2], live[0])
    near = jnp.where(near, (1 << 10) + 1 + span + ids, 0)
    codes = jnp.concatenate(
        [jnp.where(even, code, near), own, jnp.where(even, near, code)], axis=0
    )
    off3 = off.reshape(3 * rows, slots)
    at = lax.broadcasted_iota(jnp.int32, (1, 1, STRIDE), 2)
    table = jnp.sum(
        jnp.where(off3[:, :, None] + BAND == at, codes[:, :, None], 0), axis=1
    ).reshape(-1)
    table = jnp.concatenate([table, jnp.zeros((STRIDE,), jnp.int32)])
    place = jnp.where(
        live[1], jnp.arange(rows, dtype=jnp.int32)[:, None] + off[1], 3 * rows
    ).reshape(-1)
    start = jnp.full((8,), start_slot, jnp.int32)

    more = most_needed(columns, counts, layers) > FIRST
    acc, entries, size = local_products(
        start, table, place, blocks, inner, rows, slots, quarter
    )

    def second():
        late = pack(send_idx, blocks, FIRST, BOUND - FIRST)
        return lax.ppermute(late, ("row", "col"), outer_pairs)

    late = lax.cond(
        more, second, lambda: blank((BOUND - FIRST, edge, edge), values.dtype)
    )
    flags = jnp.stack([more.astype(jnp.int32), layer])
    square = far_products(
        flags, size, entries, acc, blocks, nears, outer, late, rows, quarter
    )
    return square.reshape(rows, quarter, edge, edge)


def solution(mesh):
    return jax.shard_map(
        per_device,
        mesh=mesh,
        in_specs=(P(("row", "col"), None, None, None), P(), P()),
        out_specs=P(("row", "col"), "layer", None, None),
        check_vma=False,
    )
```

time: 65.7 us -> 58.4 us (0.89)
  Pallas kernels: 38.3 us -> 24.1 us
  starting transfers between devices: 8.71 us -> 17.9 us
  other arithmetic: 6.41 us -> 3.79 us
  matrix products: 0.15 us -> 1.27 us
    pallas_call x2 -> x3, Pallas kernels: 34.9 us -> 20 us  [the longest x1 13.7 us: local_products(): pl.pallas_call(functools.partial(local_kernel, rows, slots, quarter), out...]
    ppermute x1 -> x5, starting transfers between devices: 8.7 us -> 17.9 us  [the longest x1 8.5 us: per_device(): near_mine = lax.ppermute(near_rows, ('row', 'col'), outer_pairs)]
    reduce_max x1 -> x0, other arithmetic: 1.39 us -> none  [most_needed(): return jnp.max(jnp.sum(per_row.reshape(layers, -1, BAND), axis=2))]
    unnamed x10 -> x8, local copies, waits for them, and re-layouts: 1.29 us -> 0.02 us
    dot_general x0 -> x1, matrix products: none -> 1.12 us  [most_needed(): jnp.dot(per_row, member.astype(jnp.bfloat16), preferred_element_type=jnp....]
    dynamic_slice x0 -> x1, local copies, waits for them, and re-layouts: none -> 1.11 us  [per_device(): lax.dynamic_slice(values, (jnp.where(even, 0, rows - NEAR_ROWS), layer *...]
    reshape x2 -> x0, local copies, waits for them, and re-layouts: 0.94 us -> none  [the longest x1 0.85 us: most_needed(): return jnp.max(jnp.sum(per_row.reshape(layers, -1, BAND), axis=2))]
    convert_element_type x1 -> x0, other arithmetic: 0.84 us -> none  [most_needed(): per_row = lax.population_count(asked).astype(jnp.int32)]
  transfers between devices with their start and end apart: 2 -> 6, of which waited for: 1 -> 2; matrix products, arithmetic and copies ran while one was open for 16% -> 17% of each run, Pallas kernels for 46% -> 31%
where the time goes in v2:
time: 58.4 us; the launch traced here: 57.8 us
  Pallas kernels  24.1 us (41%)
  starting transfers between devices  17.9 us (31%)
  waiting for transfers between devices  4.92 us (8%)
  local copies, waits for them, and re-layouts  4.82 us (8%)
  other arithmetic  3.79 us (6%)
  matrix products  1.27 us (2%)
  between operations  0.96 us (2%)
    pallas_call x1, Pallas kernels, local_products(): pl.pallas_call(functools.partial(local_kernel, rows, slots, quarter), out...  13.7 us
    ppermute x1, starting transfers between devices, per_device(): near_mine = lax.ppermute(near_rows, ('row', 'col'), outer_pairs)  8.5 us
    pallas_call x1, Pallas kernels, far_products(): pl.pallas_call(functools.partial(far_kernel, rows, quarter), out_shape=ja...  6.29 us
    ppermute x3, starting transfers between devices, per_device(): lax.ppermute(near_mine, 'layer', [(x, (x + d) % layers) for x in range(la...  4.91 us
    ppermute x1, starting transfers between devices, per_device(): outer = lax.ppermute(packed, ('row', 'col'), outer_pairs)  4.5 us
    ppermute x1, waiting for transfers between devices, per_device(): outer = lax.ppermute(packed, ('row', 'col'), outer_pairs)  4.44 us
    pallas_call x1, Pallas kernels, pack(): pl.pallas_call(functools.partial(pack_kernel, start, size), out_shape=jax...  4.09 us
  transfers between devices with their start and end apart: 6, of which 2 were waited for; matrix products, arithmetic and copies ran while one was open for 17% of the time, Pallas kernels for 31%

profile of v2, /device:TPU:2, one launch (start us, length us, event | category | flops | bytes accessed | tf_op | source)
XLA Modules:
  0.0 57.8 jit_solution(9672872697273756796)
XLA Ops:
  0.0 1.1 %constant_dynamic-slice_fusion = bf16[6,3,128,128]{3,2,1,0:T(8,128)(2,1)S(1)} fusion(bf16[12,20,128,128]{3,2,1,0:T(8,128)(2,1)} %param.5, s32[]{:T(128)S(6)} %select_n.454, s32[]{:T(128)S(6)} %select_n.455), kind=kLoop, calls=%fused_computation.296 | loop fusion | bytes 1179656 | tf_op jit(solution)/shard_map/dynamic_slice | solution.py:356
  1.1 8.5 %collective-permute-start.1 = (bf16[18,128,128]{2,1,0:T(8,128)(2,1)S(1)}, bf16[18,128,128]{2,1,0:T(8,128)(2,1)S(1)}, u32[]{:S(2)}, u32[]{:S(2)}) collective-permute-start(bf16[18,128,128]{2,1,0:T(8,128)(2,1)S(1)} %bitcast.23), channel_id=1, source_target_pairs={{0,63},{1,2},{2,1},{3,4},{4,3},{5,6},{6,5},{7,8},{8,7},{9,10},{10,... | collective-permute-start | bytes 1769480 | tf_op jit(solution)/shard_map/ppermute | solution.py:361
  9.6 0.8 %fusion.186 = (s32[12,20]{0,1:T(8,128)S(1)}, s32[12,20]{0,1:T(8,128)S(1)}) fusion(s32[768,20]{0,1:T(8,128)} %param.6), kind=kLoop, calls=%fused_computation.322 | loop fusion | bytes 3840 | tf_op jit(solution)/shard_map/slice | solution.py:362
  10.4 0.8 %fusion.189 = (s32[12]{0:T(128)S(1)}, s32[12]{0:T(128)S(1)}) fusion(s32[768]{0:T(1024)} %param.7), kind=kLoop, calls=%fused_computation.325 | loop fusion | bytes 192 | tf_op jit(solution)/shard_map/slice | solution.py:363
  11.3 0.8 %broadcast_add_fusion = (s32[36,20]{0,1:T(8,128)S(1)}, s32[36,20]{0,1:T(8,128)S(1)}) fusion(s32[36]{0:T(128)S(1)} %iota_add_fusion, s32[]{:T(128)S(6)} %select_n.430, s32[12,20]{0,1:T(8,128)S(1)} %get-tuple-element.41, s32[768,20]{0,1:T(8,128)} %param.6, s32[12,20]{0,1:T(8,128)S(1)} %get-tuple-element.40), kind=kLoop, calls=%fused_computation.151 | loop fusion | flops 7920 | bytes 69268 | tf_op jit(solution)/shard_map/add | solution.py:436
  12.1 0.8 %pad_add_fusion.2 = s32[792]{0:T(1024)S(1)} fusion(s32[12]{0:T(128)S(1)} %get-tuple-element.77, s32[768]{0:T(1024)} %param.7, s32[12]{0:T(128)S(1)} %get-tuple-element.76), kind=kLoop, calls=%fused_computation.211 | loop fusion | flops 1584 | bytes 6336 | tf_op jit(solution)/shard_map/concatenate | solution.py:363
  13.2 0.1 copy.27
  13.3 0.1 copy.28
  13.4 0.1 fusion.68
  13.8 0.1 select_reduce_fusion.3
  13.9 0.1 select_reduce_fusion.4
  14.2 0.1 copy.30
  14.4 0.1 copy.31
  14.5 0.1 stack.41
  14.9 0.2 convolution_convert_fusion
  15.2 0.1 copy.33
  15.8 0.3 select_reduce_fusion
  16.3 0.1 copy.29
  16.6 0.1 select_reduce_fusion.1.idx_ref
  16.7 0.5 collective-permute-done.1.near0_ref
  17.2 4.1 %pack.3 = bf16[60,128,128]{2,1,0:T(8,128)(2,1)S(1)} custom-call(s32[132]{0:T(256)S(1)} %select_reduce_fusion.1.idx_ref, bf16[240,128,128]{2,1,0:T(8,128)(2,1)} %bitcast.17), custom_call_target="tpu_custom_call" | custom-call | tf_op jit(solution)/shard_map/pack/pallas_call | solution.py:50
  21.3 1.6 %collective-permute-start.3 = (bf16[18,128,128]{2,1,0:T(8,128)(2,1)S(1)}, bf16[18,128,128]{2,1,0:T(8,128)(2,1)S(1)}, u32[]{:S(2)}, u32[]{:S(2)}) collective-permute-start(bf16[18,128,128]{2,1,0:T(8,128)(2,1)S(1)} %collective-permute-done.1.near0_ref), channel_id=1, source_target_pairs={{0,64},{64,128},{128,192},{192,0},{1,65},{65,129},{129,193},{193,1... | collective-permute-start | bytes 1769480 | tf_op jit(solution)/shard_map/ppermute | solution.py:413
  22.9 1.1 %collective-permute-start.4 = (bf16[18,128,128]{2,1,0:T(8,128)(2,1)S(1)}, bf16[18,128,128]{2,1,0:T(8,128)(2,1)}, u32[]{:S(2)}, u32[]{:S(2)}) collective-permute-start(bf16[18,128,128]{2,1,0:T(8,128)(2,1)S(1)} %collective-permute-done.1.near0_ref), channel_id=1, source_target_pairs={{0,128},{64,192},{128,0},{192,64},{1,129},{65,193},{129,1},{193,65... | collective-permute-start | bytes 1769480 | tf_op jit(solution)/shard_map/ppermute | solution.py:413
  24.0 4.5 %collective-permute-start.6 = (bf16[60,128,128]{2,1,0:T(8,128)(2,1)S(1)}, bf16[60,128,128]{2,1,0:T(8,128)(2,1)}, u32[]{:S(2)}, u32[]{:S(2)}) collective-permute-start(bf16[60,128,128]{2,1,0:T(8,128)(2,1)S(1)} %pack.3), channel_id=1, source_target_pairs={{0,63},{1,2},{2,1},{3,4},{4,3},{5,6},{6,5},{7,8},{8,7},{9,10},{10,... | collective-permute-start | bytes 5898248 | tf_op jit(solution)/shard_map/ppermute | solution.py:417
  28.7 0.1 pad_add_fusion
  29.0 0.1 fusion.156
  29.1 0.1 fusion.144
  29.2 1.1 %convolution_reduce_fusion = f32[]{:T(128)} fusion(s32[768]{0:T(1024)S(1)} %add_select_fusion.7, u32[4,780]{1,0:T(4,128)S(1)} %get-tuple-element.43, u32[4,780]{1,0:T(4,128)S(1)} %get-tuple-element.42, u32[768]{0:T(1024)S(1)} %not_select_fusion, u32[768]{0:T(1024)S(1)} %get-tuple-element.38, pred[768]{0:T(1024)(128)(4,1)S(1)} %get-tuple-element.65, ...), kind=kOutput, calls=%fused_computation.1 | convolution fusion | flops 673023 | bytes 332804 | tf_op jit(solution)/shard_map/dot_general | solution.py:330
  31.0 2.2 %collective-permute-start.5 = (bf16[18,128,128]{2,1,0:T(8,128)(2,1)S(1)}, bf16[18,128,128]{2,1,0:T(8,128)(2,1)S(1)}, u32[]{:S(2)}, u32[]{:S(2)}) collective-permute-start(bf16[18,128,128]{2,1,0:T(8,128)(2,1)S(1)} %collective-permute-done.1.near0_ref), channel_id=1, source_target_pairs={{0,192},{64,0},{128,64},{192,128},{1,193},{65,1},{129,65},{193,129... | collective-permute-start | bytes 1769480 | tf_op jit(solution)/shard_map/ppermute | solution.py:413
  33.3 13.7 %local_products.1 = (f32[61,128,128]{2,1,0:T(8,128)S(1)}, s32[1216]{0:T(1024)S(1)}, s32[8]{0:T(128)S(1)}) custom-call(s32[8]{0:T(128)S(1)} %broadcast_in_dim.223.start_ref, s32[2368]{0:T(1024)S(1)} %concatenate.78.table_ref, s32[240]{0:T(256)S(1)} %reshape.340.place_ref, bf16[240,128,128]{2,1,0:T(8,128)(2,1)} %bitcast.19, ...), custom_call_target="tpu_custom_call" | custom-call | flops 10000000000 | bytes 24000000 | tf_op jit(solution)/shard_map/local_products/pallas_call | solution.py:162
  47.0 4.4 %collective-permute-done.6.first_ref = bf16[60,128,128]{2,1,0:T(8,128)(2,1)} collective-permute-done((bf16[60,128,128]{2,1,0:T(8,128)(2,1)S(1)}, bf16[60,128,128]{2,1,0:T(8,128)(2,1)}, u32[]{:S(2)}, u32[]{:S(2)}) %collective-permute-start.6) | collective-permute-done | bytes 1966112 | tf_op jit(solution)/shard_map/ppermute | solution.py:417
  51.5 6.3 %far_products.1 = bf16[60,128,128]{2,1,0:T(8,128)(2,1)} custom-call(s32[2]{0:T(128)S(1)} %pad_add_fusion.10.more_ref, s32[8]{0:T(128)S(1)} %get-tuple-element.23.size_ref, s32[1216]{0:T(1024)S(1)} %get-tuple-element.24.list_ref, f32[61,128,128]{2,1,0:T(8,128)S(1)} %get-tuple-element.25.acc_in, bf16[240,128,128]{2,1,0:T(8,128)(2,1)S(1)} %bitcast.22, ...), custom_call_target="tpu_custom_call" | custom-call | tf_op jit(solution)/shard_map/far_products/pallas_call | solution.py:251
  (74 shorter events, 2.6 us)
Async XLA Ops:
  0.0 33.3 %collective-permute-start.2 = (bf16[240,128,128]{2,1,0:T(8,128)(2,1)}, bf16[240,128,128]{2,1,0:T(8,128)(2,1)}, u32[]{:S(2)}, u32[]{:S(2)}) collective-permute-start(bf16[240,128,128]{2,1,0:T(8,128)(2,1)} %bitcast.16), channel_id=1, source_target_pairs={{0,1},{1,0},{2,3},{3,2},{4,5},{5,4},{6,7},{7,6},{8,9},{9,8},{10,11... | collective-permute-start | bytes 23592968 | tf_op jit(solution)/shard_map/ppermute | solution.py:349
  1.1 16.1 %collective-permute-start.1 = (bf16[18,128,128]{2,1,0:T(8,128)(2,1)S(1)}, bf16[18,128,128]{2,1,0:T(8,128)(2,1)S(1)}, u32[]{:S(2)}, u32[]{:S(2)}) collective-permute-start(bf16[18,128,128]{2,1,0:T(8,128)(2,1)S(1)} %bitcast.23), channel_id=1, source_target_pairs={{0,63},{1,2},{2,1},{3,4},{4,3},{5,6},{6,5},{7,8},{8,7},{9,10},{10,... | collective-permute-start | bytes 1769480 | tf_op jit(solution)/shard_map/ppermute | solution.py:361
  16.7 11.8 %copy-start = (s32[768,20]{0,1:T(8,128)S(1)}, s32[768,20]{0,1:T(8,128)}, u32[]{:S(2)}) copy-start(s32[768,20]{0,1:T(8,128)} %param.6) | copy-start | bytes 184324
  16.7 11.8 %copy-start.1 = (s32[768]{0:T(1024)S(1)}, s32[768]{0:T(1024)}, u32[]{:S(2)}) copy-start(s32[768]{0:T(1024)} %param.7) | copy-start | bytes 9220
  21.3 25.7 %collective-permute-start.3 = (bf16[18,128,128]{2,1,0:T(8,128)(2,1)S(1)}, bf16[18,128,128]{2,1,0:T(8,128)(2,1)S(1)}, u32[]{:S(2)}, u32[]{:S(2)}) collective-permute-start(bf16[18,128,128]{2,1,0:T(8,128)(2,1)S(1)} %collective-permute-done.1.near0_ref), channel_id=1, source_target_pairs={{0,64},{64,128},{128,192},{192,0},{1,65},{65,129},{129,193},{193,1... | collective-permute-start | bytes 1769480 | tf_op jit(solution)/shard_map/ppermute | solution.py:413
  22.9 24.1 %collective-permute-start.4 = (bf16[18,128,128]{2,1,0:T(8,128)(2,1)S(1)}, bf16[18,128,128]{2,1,0:T(8,128)(2,1)}, u32[]{:S(2)}, u32[]{:S(2)}) collective-permute-start(bf16[18,128,128]{2,1,0:T(8,128)(2,1)S(1)} %collective-permute-done.1.near0_ref), channel_id=1, source_target_pairs={{0,128},{64,192},{128,0},{192,64},{1,129},{65,193},{129,1},{193,65... | collective-permute-start | bytes 1769480 | tf_op jit(solution)/shard_map/ppermute | solution.py:413
  24.0 27.5 %collective-permute-start.6 = (bf16[60,128,128]{2,1,0:T(8,128)(2,1)S(1)}, bf16[60,128,128]{2,1,0:T(8,128)(2,1)}, u32[]{:S(2)}, u32[]{:S(2)}) collective-permute-start(bf16[60,128,128]{2,1,0:T(8,128)(2,1)S(1)} %pack.3), channel_id=1, source_target_pairs={{0,63},{1,2},{2,1},{3,4},{4,3},{5,6},{6,5},{7,8},{8,7},{9,10},{10,... | collective-permute-start | bytes 5898248 | tf_op jit(solution)/shard_map/ppermute | solution.py:417
  31.0 16.0 %collective-permute-start.5 = (bf16[18,128,128]{2,1,0:T(8,128)(2,1)S(1)}, bf16[18,128,128]{2,1,0:T(8,128)(2,1)S(1)}, u32[]{:S(2)}, u32[]{:S(2)}) collective-permute-start(bf16[18,128,128]{2,1,0:T(8,128)(2,1)S(1)} %collective-permute-done.1.near0_ref), channel_id=1, source_target_pairs={{0,192},{64,0},{128,64},{192,128},{1,193},{65,1},{129,65},{193,129... | collective-permute-start | bytes 1769480 | tf_op jit(solution)/shard_map/ppermute | solution.py:413
  33.3 18.2 %slice-start = ((s8[7864320]{0:T(1024)(128)(4,1)}), s8[4194304]{0:T(1024)(128)(4,1)S(1)}, s32[]{:S(2)}) async-start(s8[7864320]{0:T(1024)(128)(4,1)} %bitcast.20), calls=%async_computation | async-start | bytes 8388608
  33.3 18.2 %slice-start.1 = ((s8[7864320]{0:T(1024)(128)(4,1)}), s8[3670016]{0:T(1024)(128)(4,1)S(1)}, s32[]{:S(2)}) async-start(s8[7864320]{0:T(1024)(128)(4,1)} %bitcast.20), calls=%async_computation.1 | async-start | bytes 7340032

commit v3 on v2

--- a/solution.py
+++ b/solution.py
@@ -20,29 +20,15 @@
 VMEM = pl.BlockSpec(memory_space=pltpu.VMEM)
 
 
-def pack_kernel(start, size, idx_ref, blocks_ref, out_ref, held, read_sem, write_sem):
-    group = 4
-
-    def read(g, carry):
-        for u in range(group):
-            p = g * group + u
-            pltpu.make_async_copy(
-                blocks_ref.at[idx_ref[start + p]], held.at[p], read_sem.at[g]
-            ).start()
+def pack_kernel(start, size, idx_ref, blocks_ref, out_ref, sem):
+    def read(p, carry):
+        pltpu.make_async_copy(
+            blocks_ref.at[idx_ref[start + p]], out_ref.at[p], sem
+        ).start()
         return carry
 
-    lax.fori_loop(0, size // group, read, 0)
-
-    def write(g, carry):
-        part = pl.ds(g * group, group)
-        pltpu.make_async_copy(
-            blocks_ref.at[pl.ds(0, group)], held.at[part], read_sem.at[g]
-        ).wait()
-        pltpu.make_async_copy(held.at[part], out_ref.at[part], write_sem).start()
-        return carry
-
-    lax.fori_loop(0, size // group, write, 0)
-    pltpu.make_async_copy(held, out_ref, write_sem).wait()
+    lax.fori_loop(0, size, read, 0, unroll=4)
+    pltpu.make_async_copy(blocks_ref.at[pl.ds(0, size)], out_ref, sem).wait()
 
 
 def pack(idx, blocks, start, size):
@@ -51,12 +37,8 @@
         functools.partial(pack_kernel, start, size),
         out_shape=jax.ShapeDtypeStruct(shape, blocks.dtype),
         in_specs=[SMEM, ANY],
-        out_specs=ANY,
-        scratch_shapes=[
-            pltpu.VMEM(shape, blocks.dtype),
-            pltpu.SemaphoreType.DMA((size // 4,)),
-            pltpu.SemaphoreType.DMA,
-        ],
+        out_specs=VMEM,
+        scratch_shapes=[pltpu.SemaphoreType.DMA],
         compiler_params=pltpu.CompilerParams(vmem_limit_bytes=8 << 20),
         name="pack",
     )(idx, blocks)
@@ -96,6 +78,8 @@
     blocks_ref,
     inner_ref,
     acc_ref,
+    a_ref,
+    near_ref,
     far_ref,
     size_ref,
     own_ref,
@@ -109,6 +93,8 @@
     load.start()
     load_own = pltpu.make_async_copy(blocks_ref, inner_v.at[pl.ds(1, count)], sem.at[1])
     load_own.start()
+    load_a = pltpu.make_async_copy(blocks_ref, a_ref, sem.at[2])
+    load_a.start()
     inner_v[0] = jnp.zeros(inner_v.shape[1:], inner_v.dtype)
 
     def clear(o, carry):
@@ -128,31 +114,37 @@
             tag = row_tag + ((i * quarter + p) << 18)
 
             def terms(ends):
-                e_own, e_far = ends
+                e_own, e_near, e_far = ends
                 for m in range(slots):
                     code = table_ref[terms_at[m] + (j_at + 2 * BAND)]
                     entry = (code & 1023) + (tag + (m << 10))
                     own_ref[e_own] = entry
+                    near_ref[e_near] = entry
                     far_ref[e_far] = entry
                     e_own += (code >> 10) & 1
-                    e_far += code >> 11
+                    e_near += (code >> 11) & 1
+                    e_far += code >> 12
                 own_ref[e_own] = tag
+                near_ref[e_near] = tag
                 far_ref[e_far] = tag
-                return e_own + (e_own & 1), e_far + (e_far & 1)
+                return e_own + (e_own & 1), e_near + (e_near & 1), e_far + (e_far & 1)
 
             return lax.cond(j_at < 3 * rows, terms, lambda ends: ends, ends)
 
         return lax.fori_loop(0, quarter, one_output, ends)
 
     zero = jnp.int32(0)
-    e_own, e_far = lax.fori_loop(0, rows, one_row, (zero, zero))
+    e_own, e_near, e_far = lax.fori_loop(0, rows, one_row, (zero, zero, zero))
     for u in range(size):
         own_ref[e_own + u] = outs << 18
+        near_ref[e_near + u] = outs << 18
         far_ref[e_far + u] = outs << 18
-    size_ref[0] = (e_far + size - 1) // size * size
+    size_ref[0] = (e_near + size - 1) // size * size
+    size_ref[1] = (e_far + size - 1) // size * size
     load_own.wait()
+    load_a.wait()
     load.wait()
-    run_list(own_ref, (e_own + size - 1) // size * size, inner_v.at[pl.ds(1, count)], inner_v, acc_ref)
+    run_list(own_ref, (e_own + size - 1) // size * size, a_ref, inner_v, acc_ref)
 
 
 def local_products(start, table, place, blocks, inner, rows, slots, quarter):
@@ -163,22 +155,74 @@
         functools.partial(local_kernel, rows, slots, quarter),
         out_shape=(
             jax.ShapeDtypeStruct((outs + 1, edge, edge), jnp.float32),
+            jax.ShapeDtypeStruct(blocks.shape, blocks.dtype),
+            jax.ShapeDtypeStruct((length,), jnp.int32),
             jax.ShapeDtypeStruct((length,), jnp.int32),
             jax.ShapeDtypeStruct((8,), jnp.int32),
         ),
         in_specs=[SMEM, SMEM, SMEM, ANY, ANY],
-        out_specs=(VMEM, SMEM, SMEM),
+        out_specs=(VMEM, VMEM, SMEM, SMEM, SMEM),
         scratch_shapes=[
             pltpu.SMEM((length,), jnp.int32),
             pltpu.VMEM((2 * rows * slots + 1, edge, edge), blocks.dtype),
-            pltpu.SemaphoreType.DMA((2,)),
+            pltpu.SemaphoreType.DMA((3,)),
         ],
-        compiler_params=pltpu.CompilerParams(vmem_limit_bytes=26 << 20),
+        compiler_params=pltpu.CompilerParams(vmem_limit_bytes=32 << 20),
         cost_estimate=pl.CostEstimate(
             flops=10 * 10**9, bytes_accessed=24 * 10**6, transcendentals=0
         ),
         name="local_products",
     )(start, table, place, blocks, inner)
+
+
+def near_kernel(
+    layer_ref,
+    size_ref,
+    list_ref,
+    acc_in,
+    a_ref,
+    near0_ref,
+    near1_ref,
+    near2_ref,
+    near3_ref,
+    acc_ref,
+    v_ref,
+    sem,
+):
+    nears = (near0_ref, near1_ref, near2_ref, near3_ref)
+    near = near0_ref.shape[0]
+    copies = []
+    for away, ref in enumerate(nears):
+        source = lax.rem(layer_ref[0] + len(nears) - away, len(nears))
+        copies.append(
+            pltpu.make_async_copy(
+                ref, v_ref.at[pl.ds(1 + source * near, near)], sem.at[away]
+            )
+        )
+    for copy in copies:
+        copy.start()
+    v_ref[0] = jnp.zeros(v_ref.shape[1:], v_ref.dtype)
+    for copy in copies:
+        copy.wait()
+    run_list(list_ref, size_ref[0], a_ref, v_ref, acc_ref)
+
+
+def near_products(layer, size, entries, acc, blocks, nears):
+    edge = blocks.shape[-1]
+    held = 1 + len(nears) * nears[0].shape[0]
+    return pl.pallas_call(
+        near_kernel,
+        out_shape=jax.ShapeDtypeStruct(acc.shape, acc.dtype),
+        in_specs=[SMEM] * 3 + [VMEM, VMEM] + [ANY] * len(nears),
+        out_specs=VMEM,
+        scratch_shapes=[
+            pltpu.VMEM((held, edge, edge), blocks.dtype),
+            pltpu.SemaphoreType.DMA((len(nears),)),
+        ],
+        input_output_aliases={3: 0},
+        compiler_params=pltpu.CompilerParams(vmem_limit_bytes=24 << 20),
+        name="near_products",
+    )(layer, size, entries, acc, blocks, *nears)
 
 
 def far_kernel(
@@ -188,81 +232,63 @@
     size_ref,
     list_ref,
     acc_in,
-    blocks_ref,
-    near0_ref,
-    near1_ref,
-    near2_ref,
-    near3_ref,
+    a_ref,
     first_ref,
     late_ref,
     out_ref,
-    a_ref,
     acc_ref,
     v_ref,
     held,
     sem,
 ):
-    nears = (near0_ref, near1_ref, near2_ref, near3_ref)
-    near, first, late = near0_ref.shape[0], first_ref.shape[0], late_ref.shape[0]
-    at = 1 + len(nears) * near
-    late_copy = pltpu.make_async_copy(
-        late_ref, v_ref.at[pl.ds(at + first, late)], sem.at[3]
-    )
-    pairs = [(first_ref, v_ref.at[pl.ds(at, first)]), (acc_in, acc_ref), (blocks_ref, a_ref)]
-    copies = [
-        pltpu.make_async_copy(source, target, sem.at[n])
-        for n, (source, target) in enumerate(pairs)
-    ]
-    me = more_ref[1]
-    for away, ref in enumerate(nears):
-        source = lax.rem(me + len(nears) - away, len(nears))
-        copies.append(
-            pltpu.make_async_copy(
-                ref, v_ref.at[pl.ds(1 + source * near, near)], sem.at[5 + away]
-            )
-        )
-    for copy in copies:
-        copy.start()
+    first, late = first_ref.shape[0], late_ref.shape[0]
+    load = pltpu.make_async_copy(first_ref, v_ref.at[pl.ds(1, first)], sem.at[0])
+    load.start()
     v_ref[0] = jnp.zeros(v_ref.shape[1:], v_ref.dtype)
 
     @pl.when(more_ref[0] > 0)
     def _():
+        late_copy = pltpu.make_async_copy(
+            late_ref, v_ref.at[pl.ds(1 + first, late)], sem.at[1]
+        )
         late_copy.start()
         late_copy.wait()
 
-    for copy in copies:
-        copy.wait()
-    run_list(list_ref, size_ref[0], a_ref, v_ref, acc_ref)
+    load.wait()
+    run_list(list_ref, size_ref[1], a_ref, v_ref, acc_ref)
 
     def finish(i, carry):
         part = pl.ds(i * quarter, quarter)
         held[part] = acc_ref[part].astype(held.dtype)
-        pltpu.make_async_copy(held.at[part], out_ref.at[part], sem.at[4]).start()
+        pltpu.make_async_copy(held.at[part], out_ref.at[part], sem.at[2]).start()
         return carry
 
     lax.fori_loop(0, rows, finish, 0)
-    pltpu.make_async_copy(held, out_ref, sem.at[4]).wait()
-
-
-def far_products(flags, size, entries, acc, blocks, nears, first, late, rows, quarter):
+    pltpu.make_async_copy(held, out_ref, sem.at[2]).wait()
+
+
+def far_products(more, size, entries, acc, blocks, first, late, rows, quarter):
     edge = blocks.shape[-1]
     outs = rows * quarter
-    held = 1 + len(nears) * nears[0].shape[0] + first.shape[0] + late.shape[0]
-    return pl.pallas_call(
+    held = 1 + first.shape[0] + late.shape[0]
+    square, _ = pl.pallas_call(
         functools.partial(far_kernel, rows, quarter),
-        out_shape=jax.ShapeDtypeStruct((outs, edge, edge), blocks.dtype),
-        in_specs=[SMEM] * 3 + [ANY] * (4 + len(nears)),
-        out_specs=ANY,
+        out_shape=(
+            jax.ShapeDtypeStruct((outs, edge, edge), blocks.dtype),
+            jax.ShapeDtypeStruct(acc.shape, acc.dtype),
+        ),
+        in_specs=[SMEM] * 3 + [VMEM, VMEM, ANY, ANY],
+        out_specs=(ANY, VMEM),
         scratch_shapes=[
-            pltpu.VMEM(blocks.shape, blocks.dtype),
-            pltpu.VMEM((outs + 1, edge, edge), jnp.float32),
             pltpu.VMEM((held, edge, edge), blocks.dtype),
             pltpu.VMEM((outs, edge, edge), blocks.dtype),
-            pltpu.SemaphoreType.DMA((5 + len(nears),)),
+            pltpu.SemaphoreType.DMA((3,)),
         ],
-        compiler_params=pltpu.CompilerParams(vmem_limit_bytes=26 << 20),
+        input_output_aliases={3: 1},
+        compiler_params=pltpu.CompilerParams(vmem_limit_bytes=24 << 20),
         name="far_products",
-    )(flags, size, entries, acc, blocks, *nears, first, late)
+    )(more, size, entries, acc, blocks, first, late)
+    return square
 
 
 def blank(shape, dtype):
@@ -359,10 +385,11 @@
         (NEAR_ROWS, share, edge, edge),
     ).reshape(-1, edge, edge)
     near_mine = lax.ppermute(near_rows, ("row", "col"), outer_pairs)
-    all_cols = jnp.concatenate([columns[-rows:], columns, columns[:rows]], axis=0)
-    all_counts = jnp.concatenate([counts[-rows:], counts, counts[:rows]], axis=0)
-    cols = lax.dynamic_slice_in_dim(all_cols, first_row, 3 * rows, 0)
-    cnts = lax.dynamic_slice_in_dim(all_counts, first_row, 3 * rows, 0)
+    both = jnp.concatenate([columns.T, counts[None, :]], axis=0)
+    both = lax.optimization_barrier(both)
+    both = jnp.concatenate([both[:, -rows:], both, both[:, :rows]], axis=1)
+    both = lax.dynamic_slice_in_dim(both, first_row, 3 * rows, 1)
+    cols, cnts = both[:slots].T, both[slots]
     row_ids = first_row - rows + jnp.arange(3 * rows, dtype=jnp.int32)
     off = (cols - row_ids[:, None] + BAND) % total_rows
     slot_ids = jnp.arange(slots, dtype=jnp.int32)[None, :]
@@ -406,9 +433,7 @@
     )
     send_idx = jnp.sum(jnp.where(hit, give_ids[:, None], 0), axis=0)
 
-    columns, counts, send_idx, near_mine = lax.optimization_barrier(
-        (columns, counts, send_idx, near_mine)
-    )
+    send_idx, near_mine = lax.optimization_barrier((send_idx, near_mine))
     nears = [near_mine] + [
         lax.ppermute(near_mine, "layer", [(x, (x + d) % layers) for x in range(layers)])
         for d in range(1, layers)
@@ -416,7 +441,7 @@
     packed = pack(send_idx, blocks, 0, FIRST)
     outer = lax.ppermute(packed, ("row", "col"), outer_pairs)
 
-    code = jnp.where(get, (2 << 10) + 1 + NEAR_ROWS * NEAR_SLOTS + get_pos, 0)
+    code = jnp.where(get, (4 << 10) + 1 + get_pos, 0)
     code = jnp.where(even, code.reshape(rows, slots)[::-1], code.reshape(rows, slots))
     row_at = jnp.arange(rows, dtype=jnp.int32)[:, None] - jnp.where(even, rows - NEAR_ROWS, 0)
     sent = (row_at >= 0) & (row_at < NEAR_ROWS) & (slot_ids < NEAR_SLOTS)
@@ -441,10 +466,11 @@
     ).reshape(-1)
     start = jnp.full((8,), start_slot, jnp.int32)
 
+    acc, held, near_list, far_list, size = local_products(
+        start, table, place, blocks, inner, rows, slots, quarter
+    )
+    columns, counts, size = lax.optimization_barrier((columns, counts, size))
     more = most_needed(columns, counts, layers) > FIRST
-    acc, entries, size = local_products(
-        start, table, place, blocks, inner, rows, slots, quarter
-    )
 
     def second():
         late = pack(send_idx, blocks, FIRST, BOUND - FIRST)
@@ -453,10 +479,9 @@
     late = lax.cond(
         more, second, lambda: blank((BOUND - FIRST, edge, edge), values.dtype)
     )
-    flags = jnp.stack([more.astype(jnp.int32), layer])
-    square = far_products(
-        flags, size, entries, acc, blocks, nears, outer, late, rows, quarter
-    )
+    acc = near_products(jnp.full((8,), layer, jnp.int32), size, near_list, acc, held, nears)
+    more = jnp.full((8,), more, jnp.int32)
+    square = far_products(more, size, far_list, acc, held, outer, late, rows, quarter)
     return square.reshape(rows, quarter, edge, edge)
 
 

time: 58.4 us -> 67.3 us (1.15)
  local copies, waits for them, and re-layouts: 4.82 us -> 14.3 us
  Pallas kernels: 24.1 us -> 27.9 us
  waiting for transfers between devices: 4.92 us -> 2.01 us
  other arithmetic: 3.79 us -> 3.11 us
    unnamed x8 -> x14, local copies, waits for them, and re-layouts: 0.02 us -> 10.4 us
    ppermute x1, waiting for transfers between devices: 4.44 us -> 0.01 us  [per_device(): outer = lax.ppermute(packed, ('row', 'col'), outer_pairs)]
    pallas_call x1, Pallas kernels: 13.7 us -> 17.2 us  [local_products(): pl.pallas_call(functools.partial(local_kernel, rows, slots, quarter), out...]
    pallas_call x1 -> x2, Pallas kernels: 6.29 us -> 8.09 us  [the longest x1 4.37 us: far_products(): pl.pallas_call(functools.partial(far_kernel, rows, quarter), out_shape=(j...]
    slice x2 -> x1, local copies, waits for them, and re-layouts: 1.63 us -> 0.07 us  [per_device(): both = jnp.concatenate([both[:, -rows:], both, both[:, :rows]], axis=1)]
    ppermute x1, waiting for transfers between devices: 0.47 us -> 2 us  [per_device(): near_mine = lax.ppermute(near_rows, ('row', 'col'), outer_pairs)]
    pallas_call x1, Pallas kernels: 4.09 us -> 2.64 us  [pack(): pl.pallas_call(functools.partial(pack_kernel, start, size), out_shape=jax...]
    add x1, other arithmetic: 0.83 us -> 0.02 us  [per_device(): off3[:, :, None] + BAND == at]
  transfers between devices with their start and end apart: 6 -> 6, of which waited for: 2 -> 1; matrix products, arithmetic and copies ran while one was open for 17% -> 12% of each run, Pallas kernels for 31% -> 35%
where the time goes in v3:
time: 67.3 us; the launch traced here: 67.1 us
  Pallas kernels  27.9 us (41%)
  starting transfers between devices  17.4 us (26%)
  local copies, waits for them, and re-layouts  14.3 us (21%)
  other arithmetic  3.11 us (5%)
  waiting for transfers between devices  2.01 us (3%)
  matrix products  1.21 us (2%)
  between operations  1.05 us (2%)
    pallas_call x1, Pallas kernels, local_products(): pl.pallas_call(functools.partial(local_kernel, rows, slots, quarter), out...  17.2 us
    unnamed x14, local copies, waits for them, and re-layouts  10.4 us
    ppermute x1, starting transfers between devices, per_device(): near_mine = lax.ppermute(near_rows, ('row', 'col'), outer_pairs)  8.5 us
    ppermute x3, starting transfers between devices, per_device(): lax.ppermute(near_mine, 'layer', [(x, (x + d) % layers) for x in range(la...  4.76 us
    pallas_call x1, Pallas kernels, far_products(): pl.pallas_call(functools.partial(far_kernel, rows, quarter), out_shape=(j...  4.37 us
    ppermute x1, starting transfers between devices, per_device(): outer = lax.ppermute(packed, ('row', 'col'), outer_pairs)  4.16 us
    pallas_call x1, Pallas kernels, near_products(): pl.pallas_call(near_kernel, out_shape=jax.ShapeDtypeStruct(acc.shape, acc...  3.72 us
    pallas_call x1, Pallas kernels, pack(): pl.pallas_call(functools.partial(pack_kernel, start, size), out_shape=jax...  2.64 us
  transfers between devices with their start and end apart: 6, of which 1 were waited for; matrix products, arithmetic and copies ran while one was open for 12% of the time, Pallas kernels for 35%

profile of v3, /device:TPU:2, one launch (start us, length us, event | category | flops | bytes accessed | tf_op | source)
XLA Modules:
  0.0 67.1 jit_solution(14855946879064546651)
XLA Ops:
  0.0 1.1 %constant_dynamic-slice_fusion = bf16[6,3,128,128]{3,2,1,0:T(8,128)(2,1)S(1)} fusion(bf16[12,20,128,128]{3,2,1,0:T(8,128)(2,1)} %param.5, s32[]{:T(128)S(6)} %select_n.501, s32[]{:T(128)S(6)} %select_n.502), kind=kLoop, calls=%fused_computation.297 | loop fusion | bytes 1179656 | tf_op jit(solution)/shard_map/dynamic_slice | solution.py:382
  1.1 8.5 %collective-permute-start.2 = (bf16[18,128,128]{2,1,0:T(8,128)(2,1)S(1)}, bf16[18,128,128]{2,1,0:T(8,128)(2,1)S(1)}, u32[]{:S(2)}, u32[]{:S(2)}) collective-permute-start(bf16[18,128,128]{2,1,0:T(8,128)(2,1)S(1)} %bitcast.26), channel_id=1, source_target_pairs={{0,63},{1,2},{2,1},{3,4},{4,3},{5,6},{6,5},{7,8},{8,7},{9,10},{10,... | collective-permute-start | bytes 1769480 | tf_op jit(solution)/shard_map/ppermute | solution.py:387
  9.6 0.7 %broadcast_in_dim.204 = s32[1,768]{1,0:T(1,128)S(1)} reshape(s32[768]{0:T(1024)} %param.7) | data formatting | bytes 6144 | tf_op jit(solution)/shard_map/broadcast_in_dim | solution.py:388
  10.3 0.9 %pad_add_fusion = s32[21,768]{1,0:T(8,128)S(1)} fusion(s32[1,768]{1,0:T(1,128)S(1)} %broadcast_in_dim.204, s32[20,768]{1,0:T(8,128)} %bitcast.27), kind=kLoop, calls=%fused_computation.17 | loop fusion | flops 16128 | bytes 129024 | tf_op jit(solution)/shard_map/concatenate | solution.py:388
  11.7 0.1 copy.29
  11.8 0.1 copy.30
  11.9 0.1 fusion.68
  12.2 0.1 select_reduce_fusion.3
  12.4 0.1 select_reduce_fusion.4
  12.7 0.1 copy.31
  12.9 0.1 copy.32
  13.0 0.1 stack.32
  13.4 0.2 convolution_convert_fusion
  13.7 0.1 copy.34
  14.2 0.3 select_reduce_fusion
  14.8 0.1 copy.36
  15.1 0.1 select_reduce_fusion.1.idx_ref
  15.2 2.0 %collective-permute-done.2.near0_ref = bf16[18,128,128]{2,1,0:T(8,128)(2,1)S(1)} collective-permute-done((bf16[18,128,128]{2,1,0:T(8,128)(2,1)S(1)}, bf16[18,128,128]{2,1,0:T(8,128)(2,1)S(1)}, u32[]{:S(2)}, u32[]{:S(2)}) %collective-permute-start.2) | collective-permute-done | bytes 589856 | tf_op jit(solution)/shard_map/ppermute | solution.py:387
  17.2 1.5 %collective-permute-start.3 = (bf16[18,128,128]{2,1,0:T(8,128)(2,1)S(1)}, bf16[18,128,128]{2,1,0:T(8,128)(2,1)S(1)}, u32[]{:S(2)}, u32[]{:S(2)}) collective-permute-start(bf16[18,128,128]{2,1,0:T(8,128)(2,1)S(1)} %collective-permute-done.2.near0_ref), channel_id=1, source_target_pairs={{0,64},{64,128},{128,192},{192,0},{1,65},{65,129},{129,193},{193,1... | collective-permute-start | bytes 1769480 | tf_op jit(solution)/shard_map/ppermute | solution.py:438
  18.7 1.1 %collective-permute-start.4 = (bf16[18,128,128]{2,1,0:T(8,128)(2,1)S(1)}, bf16[18,128,128]{2,1,0:T(8,128)(2,1)}, u32[]{:S(2)}, u32[]{:S(2)}) collective-permute-start(bf16[18,128,128]{2,1,0:T(8,128)(2,1)S(1)} %collective-permute-done.2.near0_ref), channel_id=1, source_target_pairs={{0,128},{64,192},{128,0},{192,64},{1,129},{65,193},{129,1},{193,65... | collective-permute-start | bytes 1769480 | tf_op jit(solution)/shard_map/ppermute | solution.py:438
  19.8 2.2 %collective-permute-start.5 = (bf16[18,128,128]{2,1,0:T(8,128)(2,1)S(1)}, bf16[18,128,128]{2,1,0:T(8,128)(2,1)}, u32[]{:S(2)}, u32[]{:S(2)}) collective-permute-start(bf16[18,128,128]{2,1,0:T(8,128)(2,1)S(1)} %collective-permute-done.2.near0_ref), channel_id=1, source_target_pairs={{0,192},{64,0},{128,64},{192,128},{1,193},{65,1},{129,65},{193,129... | collective-permute-start | bytes 1769480 | tf_op jit(solution)/shard_map/ppermute | solution.py:438
  21.9 2.6 %pack.3 = bf16[60,128,128]{2,1,0:T(8,128)(2,1)S(1)} custom-call(s32[132]{0:T(256)S(1)} %select_reduce_fusion.1.idx_ref, bf16[240,128,128]{2,1,0:T(8,128)(2,1)} %bitcast.23), custom_call_target="tpu_custom_call" | custom-call | tf_op jit(solution)/shard_map/pack/pallas_call | solution.py:36
  24.6 4.2 %collective-permute-start.6 = (bf16[60,128,128]{2,1,0:T(8,128)(2,1)S(1)}, bf16[60,128,128]{2,1,0:T(8,128)(2,1)}, u32[]{:S(2)}, u32[]{:S(2)}) collective-permute-start(bf16[60,128,128]{2,1,0:T(8,128)(2,1)S(1)} %pack.3), channel_id=1, source_target_pairs={{0,63},{1,2},{2,1},{3,4},{4,3},{5,6},{6,5},{7,8},{8,7},{9,10},{10,... | collective-permute-start | bytes 5898248 | tf_op jit(solution)/shard_map/ppermute | solution.py:442
  28.8 17.2 %local_products.1 = (f32[61,128,128]{2,1,0:T(8,128)S(1)}, bf16[240,128,128]{2,1,0:T(8,128)(2,1)S(1)}, s32[1216]{0:T(1024)S(1)}, s32[1216]{0:T(1024)S(1)}, s32[8]{0:T(128)S(1)}) custom-call(s32[8]{0:T(128)S(1)} %broadcast_in_dim.203.start_ref, s32[2368]{0:T(1024)S(1)} %concatenate.74.table_ref, s32[240]{0:T(256)S(1)} %reshape.339.place_ref, ...), custom_call_target="tpu_custom_call" | custom-call | flops 10000000000 | bytes 24000000 | tf_op jit(solution)/shard_map/local_products/pallas_call | solution.py:154
  46.0 3.1 %copy-done = bf16[240,128,128]{2,1,0:T(8,128)(2,1)} copy-done((bf16[240,128,128]{2,1,0:T(8,128)(2,1)}, bf16[240,128,128]{2,1,0:T(8,128)(2,1)S(1)}, u32[]{:S(2)}) %copy-start) | copy-done | bytes 7864344
  49.1 2.0 %copy-done.2 = f32[61,128,128]{2,1,0:T(8,128)} copy-done((f32[61,128,128]{2,1,0:T(8,128)}, f32[61,128,128]{2,1,0:T(8,128)S(1)}, u32[]{:S(2)}) %copy-start.2) | copy-done | bytes 3997720
  51.3 0.1 pad_add_fusion.1
  51.8 1.1 %convolution_reduce_fusion = f32[]{:T(128)} fusion(s32[768]{0:T(1024)S(1)} %add_select_fusion.7, u32[4,780]{1,0:T(4,128)S(1)} %get-tuple-element.51, u32[4,780]{1,0:T(4,128)S(1)} %get-tuple-element.50, u32[768]{0:T(1024)S(1)} %not_select_fusion, u32[768]{0:T(1024)S(1)} %get-tuple-element.42, pred[768]{0:T(1024)(128)(4,1)S(1)} %get-tuple-element.73, ...), kind=kOutput, calls=%fused_computation.1 | convolution fusion | flops 673023 | bytes 332804 | tf_op jit(solution)/shard_map/dot_general | solution.py:356
  53.6 3.2 %copy-done.1 = bf16[240,128,128]{2,1,0:T(8,128)(2,1)S(1)} copy-done((bf16[240,128,128]{2,1,0:T(8,128)(2,1)S(1)}, bf16[240,128,128]{2,1,0:T(8,128)(2,1)}, u32[]{:S(2)}) %copy-start.1) | copy-done | bytes 7864344
  56.8 2.1 %copy-done.3 = f32[61,128,128]{2,1,0:T(8,128)S(1)} copy-done((f32[61,128,128]{2,1,0:T(8,128)S(1)}, f32[61,128,128]{2,1,0:T(8,128)}, u32[]{:S(2)}) %copy-start.3) | copy-done | bytes 3997720
  58.9 3.7 %near_products.1.acc_in = f32[61,128,128]{2,1,0:T(8,128)S(1)} custom-call(s32[8]{0:T(128)S(1)} %broadcast_in_dim.240.layer_ref, s32[8]{0:T(128)S(1)} %get-tuple-element.28.size_ref, s32[1216]{0:T(1024)S(1)} %get-tuple-element.30.list_ref, f32[61,128,128]{2,1,0:T(8,128)S(1)} %copy-done.3, ...), custom_call_target="tpu_custom_call", output_to_operand_aliasing={{}: (3, {})} | custom-call | tf_op jit(solution)/shard_map/near_products/pallas_call | solution.py:213
  62.7 4.4 %far_products.1 = (bf16[60,128,128]{2,1,0:T(8,128)(2,1)}, f32[61,128,128]{2,1,0:T(8,128)S(1)}) custom-call(s32[8]{0:T(128)S(1)} %broadcast_in_dim.239.more_ref, s32[8]{0:T(128)S(1)} %get-tuple-element.28.size_ref, s32[1216]{0:T(1024)S(1)} %get-tuple-element.29.list_ref, f32[61,128,128]{2,1,0:T(8,128)S(1)} %near_products.1.acc_in, ...), custom_call_target="tpu_custom_call", output_to_operand_aliasing={{1}: (3, {})} | custom-call | tf_op jit(solution)/shard_map/far_products/pallas_call | solution.py:274
  (82 shorter events, 2.8 us)
Async XLA Ops:
  0.0 28.8 %collective-permute-start.1 = (bf16[240,128,128]{2,1,0:T(8,128)(2,1)}, bf16[240,128,128]{2,1,0:T(8,128)(2,1)}, u32[]{:S(2)}, u32[]{:S(2)}) collective-permute-start(bf16[240,128,128]{2,1,0:T(8,128)(2,1)} %bitcast.22), channel_id=1, source_target_pairs={{0,1},{1,0},{2,3},{3,2},{4,5},{5,4},{6,7},{7,6},{8,9},{9,8},{10,11... | collective-permute-start | bytes 23592968 | tf_op jit(solution)/shard_map/ppermute | solution.py:375
  1.1 16.1 %collective-permute-start.2 = (bf16[18,128,128]{2,1,0:T(8,128)(2,1)S(1)}, bf16[18,128,128]{2,1,0:T(8,128)(2,1)S(1)}, u32[]{:S(2)}, u32[]{:S(2)}) collective-permute-start(bf16[18,128,128]{2,1,0:T(8,128)(2,1)S(1)} %bitcast.26), channel_id=1, source_target_pairs={{0,63},{1,2},{2,1},{3,4},{4,3},{5,6},{6,5},{7,8},{8,7},{9,10},{10,... | collective-permute-start | bytes 1769480 | tf_op jit(solution)/shard_map/ppermute | solution.py:387
  17.2 36.3 %collective-permute-start.3 = (bf16[18,128,128]{2,1,0:T(8,128)(2,1)S(1)}, bf16[18,128,128]{2,1,0:T(8,128)(2,1)S(1)}, u32[]{:S(2)}, u32[]{:S(2)}) collective-permute-start(bf16[18,128,128]{2,1,0:T(8,128)(2,1)S(1)} %collective-permute-done.2.near0_ref), channel_id=1, source_target_pairs={{0,64},{64,128},{128,192},{192,0},{1,65},{65,129},{129,193},{193,1... | collective-permute-start | bytes 1769480 | tf_op jit(solution)/shard_map/ppermute | solution.py:438
  18.7 34.9 %collective-permute-start.4 = (bf16[18,128,128]{2,1,0:T(8,128)(2,1)S(1)}, bf16[18,128,128]{2,1,0:T(8,128)(2,1)}, u32[]{:S(2)}, u32[]{:S(2)}) collective-permute-start(bf16[18,128,128]{2,1,0:T(8,128)(2,1)S(1)} %collective-permute-done.2.near0_ref), channel_id=1, source_target_pairs={{0,128},{64,192},{128,0},{192,64},{1,129},{65,193},{129,1},{193,65... | collective-permute-start | bytes 1769480 | tf_op jit(solution)/shard_map/ppermute | solution.py:438
  19.8 33.8 %collective-permute-start.5 = (bf16[18,128,128]{2,1,0:T(8,128)(2,1)S(1)}, bf16[18,128,128]{2,1,0:T(8,128)(2,1)}, u32[]{:S(2)}, u32[]{:S(2)}) collective-permute-start(bf16[18,128,128]{2,1,0:T(8,128)(2,1)S(1)} %collective-permute-done.2.near0_ref), channel_id=1, source_target_pairs={{0,192},{64,0},{128,64},{192,128},{1,193},{65,1},{129,65},{193,129... | collective-permute-start | bytes 1769480 | tf_op jit(solution)/shard_map/ppermute | solution.py:438
  21.9 6.8 %copy-start.4 = (bf16[12,20,128,128]{3,2,1,0:T(8,128)(2,1)S(1)}, bf16[12,20,128,128]{3,2,1,0:T(8,128)(2,1)}, u32[]{:S(2)}) copy-start(bf16[12,20,128,128]{3,2,1,0:T(8,128)(2,1)} %param.5) | copy-start | bytes 23592964
  24.6 38.1 %collective-permute-start.6 = (bf16[60,128,128]{2,1,0:T(8,128)(2,1)S(1)}, bf16[60,128,128]{2,1,0:T(8,128)(2,1)}, u32[]{:S(2)}, u32[]{:S(2)}) collective-permute-start(bf16[60,128,128]{2,1,0:T(8,128)(2,1)S(1)} %pack.3), channel_id=1, source_target_pairs={{0,63},{1,2},{2,1},{3,4},{4,3},{5,6},{6,5},{7,8},{8,7},{9,10},{10,... | collective-permute-start | bytes 5898248 | tf_op jit(solution)/shard_map/ppermute | solution.py:442
  28.8 22.3 %copy-start.5 = (s32[768,20]{0,1:T(8,128)S(1)}, s32[768,20]{0,1:T(8,128)}, u32[]{:S(2)}) copy-start(s32[768,20]{0,1:T(8,128)} %param.6) | copy-start | bytes 184324
  28.8 22.3 %copy-start.6 = (s32[768]{0:T(1024)S(1)}, s32[768]{0:T(1024)}, u32[]{:S(2)}) copy-start(s32[768]{0:T(1024)} %param.7) | copy-start | bytes 9220
  46.0 3.1 %copy-start = (bf16[240,128,128]{2,1,0:T(8,128)(2,1)}, bf16[240,128,128]{2,1,0:T(8,128)(2,1)S(1)}, u32[]{:S(2)}) copy-start(bf16[240,128,128]{2,1,0:T(8,128)(2,1)S(1)} %get-tuple-element.32.a_ref) | copy-start | bytes 23592964
  49.1 2.0 %copy-start.2 = (f32[61,128,128]{2,1,0:T(8,128)}, f32[61,128,128]{2,1,0:T(8,128)S(1)}, u32[]{:S(2)}) copy-start(f32[61,128,128]{2,1,0:T(8,128)S(1)} %get-tuple-element.31.acc_in) | copy-start | bytes 11993092
  53.6 3.2 %copy-start.1 = (bf16[240,128,128]{2,1,0:T(8,128)(2,1)S(1)}, bf16[240,128,128]{2,1,0:T(8,128)(2,1)}, u32[]{:S(2)}) copy-start(bf16[240,128,128]{2,1,0:T(8,128)(2,1)} %copy-done) | copy-start | bytes 23592964
  56.8 2.1 %copy-start.3 = (f32[61,128,128]{2,1,0:T(8,128)S(1)}, f32[61,128,128]{2,1,0:T(8,128)}, u32[]{:S(2)}) copy-start(f32[61,128,128]{2,1,0:T(8,128)} %copy-done.2) | copy-start | bytes 11993092

commit v4 on v3

--- a/solution.py
+++ b/solution.py
@@ -464,12 +464,7 @@
     place = jnp.where(
         live[1], jnp.arange(rows, dtype=jnp.int32)[:, None] + off[1], 3 * rows
     ).reshape(-1)
-    start = jnp.full((8,), start_slot, jnp.int32)
-
-    acc, held, near_list, far_list, size = local_products(
-        start, table, place, blocks, inner, rows, slots, quarter
-    )
-    columns, counts, size = lax.optimization_barrier((columns, counts, size))
+    columns, counts, packed = lax.optimization_barrier((columns, counts, packed))
     more = most_needed(columns, counts, layers) > FIRST
 
     def second():
@@ -478,6 +473,11 @@
 
     late = lax.cond(
         more, second, lambda: blank((BOUND - FIRST, edge, edge), values.dtype)
+    )
+    start = jnp.full((8,), start_slot, jnp.int32)
+
+    acc, held, near_list, far_list, size = local_products(
+        start, table, place, blocks, inner, rows, slots, quarter
     )
     acc = near_products(jnp.full((8,), layer, jnp.int32), size, near_list, acc, held, nears)
     more = jnp.full((8,), more, jnp.int32)

time: 67.3 us -> 55.8 us (0.83)
  local copies, waits for them, and re-layouts: 14.3 us -> 3.88 us
  Pallas kernels: 27.9 us -> 25.8 us
    unnamed x14 -> x4, local copies, waits for them, and re-layouts: 10.4 us -> 0.01 us
    pallas_call x1, Pallas kernels: 17.2 us -> 15 us  [local_products(): pl.pallas_call(functools.partial(local_kernel, rows, slots, quarter), out...]
  transfers between devices with their start and end apart: 6 -> 6, of which waited for: 1 -> 1; matrix products, arithmetic and copies ran while one was open for 12% -> 15% of each run, Pallas kernels for 35% -> 38%
where the time goes in v4:
time: 55.8 us; the launch traced here: 54.9 us
  Pallas kernels  25.8 us (46%)
  starting transfers between devices  17.9 us (32%)
  local copies, waits for them, and re-layouts  3.88 us (7%)
  other arithmetic  3.12 us (6%)
  waiting for transfers between devices  2.01 us (4%)
  matrix products  1.22 us (2%)
  between operations  1.02 us (2%)
    pallas_call x1, Pallas kernels, local_products(): pl.pallas_call(functools.partial(local_kernel, rows, slots, quarter), out...  15 us
    ppermute x1, starting transfers between devices, per_device(): near_mine = lax.ppermute(near_rows, ('row', 'col'), outer_pairs)  8.5 us
    ppermute x3, starting transfers between devices, per_device(): lax.ppermute(near_mine, 'layer', [(x, (x + d) % layers) for x in range(la...  4.88 us
    pallas_call x1, Pallas kernels, far_products(): pl.pallas_call(functools.partial(far_kernel, rows, quarter), out_shape=(j...  4.82 us
    ppermute x1, starting transfers between devices, per_device(): outer = lax.ppermute(packed, ('row', 'col'), outer_pairs)  4.47 us
    pallas_call x1, Pallas kernels, near_products(): pl.pallas_call(near_kernel, out_shape=jax.ShapeDtypeStruct(acc.shape, acc...  3.32 us
    pallas_call x1, Pallas kernels, pack(): pl.pallas_call(functools.partial(pack_kernel, start, size), out_shape=jax...  2.66 us
    ppermute x1, waiting for transfers between devices, per_device(): near_mine = lax.ppermute(near_rows, ('row', 'col'), outer_pairs)  1.99 us
  transfers between devices with their start and end apart: 6, of which 1 were waited for; matrix products, arithmetic and copies ran while one was open for 15% of the time, Pallas kernels for 38%

profile of v4, /device:TPU:2, one launch (start us, length us, event | category | flops | bytes accessed | tf_op | source)
XLA Modules:
  0.0 54.9 jit_solution(16690815458029560316)
XLA Ops:
  0.0 1.1 %constant_dynamic-slice_fusion = bf16[6,3,128,128]{3,2,1,0:T(8,128)(2,1)S(1)} fusion(bf16[12,20,128,128]{3,2,1,0:T(8,128)(2,1)} %param.5, s32[]{:T(128)S(6)} %select_n.453, s32[]{:T(128)S(6)} %select_n.454), kind=kLoop, calls=%fused_computation.297 | loop fusion | bytes 1179656 | tf_op jit(solution)/shard_map/dynamic_slice | solution.py:382
  1.1 8.5 %collective-permute-start.1 = (bf16[18,128,128]{2,1,0:T(8,128)(2,1)S(1)}, bf16[18,128,128]{2,1,0:T(8,128)(2,1)S(1)}, u32[]{:S(2)}, u32[]{:S(2)}) collective-permute-start(bf16[18,128,128]{2,1,0:T(8,128)(2,1)S(1)} %bitcast.26), channel_id=1, source_target_pairs={{0,63},{1,2},{2,1},{3,4},{4,3},{5,6},{6,5},{7,8},{8,7},{9,10},{10,... | collective-permute-start | bytes 1769480 | tf_op jit(solution)/shard_map/ppermute | solution.py:387
  9.6 0.7 %broadcast_in_dim.199 = s32[1,768]{1,0:T(1,128)S(1)} reshape(s32[768]{0:T(1024)} %param.7) | data formatting | bytes 6144 | tf_op jit(solution)/shard_map/broadcast_in_dim | solution.py:388
  10.3 0.9 %pad_add_fusion = s32[21,768]{1,0:T(8,128)S(1)} fusion(s32[1,768]{1,0:T(1,128)S(1)} %broadcast_in_dim.199, s32[20,768]{1,0:T(8,128)} %bitcast.27), kind=kLoop, calls=%fused_computation.17 | loop fusion | flops 16128 | bytes 129024 | tf_op jit(solution)/shard_map/concatenate | solution.py:388
  11.7 0.1 copy.29
  11.8 0.1 copy.30
  11.9 0.1 fusion.68
  12.2 0.1 select_reduce_fusion.3
  12.4 0.1 select_reduce_fusion.4
  12.7 0.1 copy.32
  12.9 0.1 copy.33
  13.0 0.1 stack.32
  13.3 0.1 and.434
  13.4 0.2 convolution_convert_fusion
  13.7 0.1 copy.35
  14.2 0.3 select_reduce_fusion
  14.6 0.1 copy.36
  14.8 0.1 copy.31
  15.1 0.1 select_reduce_fusion.1.idx_ref
  15.2 2.0 %collective-permute-done.1.near0_ref = bf16[18,128,128]{2,1,0:T(8,128)(2,1)S(1)} collective-permute-done((bf16[18,128,128]{2,1,0:T(8,128)(2,1)S(1)}, bf16[18,128,128]{2,1,0:T(8,128)(2,1)S(1)}, u32[]{:S(2)}, u32[]{:S(2)}) %collective-permute-start.1) | collective-permute-done | bytes 589856 | tf_op jit(solution)/shard_map/ppermute | solution.py:387
  17.2 1.5 %collective-permute-start.3 = (bf16[18,128,128]{2,1,0:T(8,128)(2,1)S(1)}, bf16[18,128,128]{2,1,0:T(8,128)(2,1)S(1)}, u32[]{:S(2)}, u32[]{:S(2)}) collective-permute-start(bf16[18,128,128]{2,1,0:T(8,128)(2,1)S(1)} %collective-permute-done.1.near0_ref), channel_id=1, source_target_pairs={{0,64},{64,128},{128,192},{192,0},{1,65},{65,129},{129,193},{193,1... | collective-permute-start | bytes 1769480 | tf_op jit(solution)/shard_map/ppermute | solution.py:438
  18.7 1.1 %collective-permute-start.4 = (bf16[18,128,128]{2,1,0:T(8,128)(2,1)S(1)}, bf16[18,128,128]{2,1,0:T(8,128)(2,1)}, u32[]{:S(2)}, u32[]{:S(2)}) collective-permute-start(bf16[18,128,128]{2,1,0:T(8,128)(2,1)S(1)} %collective-permute-done.1.near0_ref), channel_id=1, source_target_pairs={{0,128},{64,192},{128,0},{192,64},{1,129},{65,193},{129,1},{193,65... | collective-permute-start | bytes 1769480 | tf_op jit(solution)/shard_map/ppermute | solution.py:438
  19.8 2.7 %pack.3 = bf16[60,128,128]{2,1,0:T(8,128)(2,1)S(1)} custom-call(s32[132]{0:T(256)S(1)} %select_reduce_fusion.1.idx_ref, bf16[240,128,128]{2,1,0:T(8,128)(2,1)} %bitcast.23), custom_call_target="tpu_custom_call" | custom-call | tf_op jit(solution)/shard_map/pack/pallas_call | solution.py:36
  22.5 4.5 %collective-permute-start.6 = (bf16[60,128,128]{2,1,0:T(8,128)(2,1)S(1)}, bf16[60,128,128]{2,1,0:T(8,128)(2,1)}, u32[]{:S(2)}, u32[]{:S(2)}) collective-permute-start(bf16[60,128,128]{2,1,0:T(8,128)(2,1)S(1)} %pack.3), channel_id=1, source_target_pairs={{0,63},{1,2},{2,1},{3,4},{4,3},{5,6},{6,5},{7,8},{8,7},{9,10},{10,... | collective-permute-start | bytes 5898248 | tf_op jit(solution)/shard_map/ppermute | solution.py:442
  27.2 0.1 pad_add_fusion.1
  27.5 0.1 fusion.156
  27.6 0.1 fusion.144
  27.7 1.1 %convolution_reduce_fusion = f32[]{:T(128)} fusion(s32[768]{0:T(1024)S(1)} %add_select_fusion.7, u32[4,780]{1,0:T(4,128)S(1)} %get-tuple-element.49, u32[4,780]{1,0:T(4,128)S(1)} %get-tuple-element.48, u32[768]{0:T(1024)S(1)} %not_select_fusion, u32[768]{0:T(1024)S(1)} %get-tuple-element.44, pred[768]{0:T(1024)(128)(4,1)S(1)} %get-tuple-element.71, ...), kind=kOutput, calls=%fused_computation.1 | convolution fusion | flops 673023 | bytes 332804 | tf_op jit(solution)/shard_map/dot_general | solution.py:356
  29.4 2.3 %collective-permute-start.5 = (bf16[18,128,128]{2,1,0:T(8,128)(2,1)S(1)}, bf16[18,128,128]{2,1,0:T(8,128)(2,1)S(1)}, u32[]{:S(2)}, u32[]{:S(2)}) collective-permute-start(bf16[18,128,128]{2,1,0:T(8,128)(2,1)S(1)} %collective-permute-done.1.near0_ref), channel_id=1, source_target_pairs={{0,192},{64,0},{128,64},{192,128},{1,193},{65,1},{129,65},{193,129... | collective-permute-start | bytes 1769480 | tf_op jit(solution)/shard_map/ppermute | solution.py:438
  31.7 15.0 %local_products.1 = (f32[61,128,128]{2,1,0:T(8,128)S(1)}, bf16[240,128,128]{2,1,0:T(8,128)(2,1)S(1)}, s32[1216]{0:T(1024)S(1)}, s32[1216]{0:T(1024)S(1)}, s32[8]{0:T(128)S(1)}) custom-call(s32[8]{0:T(128)S(1)} %broadcast_in_dim.233.start_ref, s32[2368]{0:T(1024)S(1)} %concatenate.78.table_ref, s32[240]{0:T(256)S(1)} %reshape.341.place_ref, ...), custom_call_target="tpu_custom_call" | custom-call | flops 10000000000 | bytes 24000000 | tf_op jit(solution)/shard_map/local_products/pallas_call | solution.py:154
  46.7 3.3 %near_products.1.acc_in = f32[61,128,128]{2,1,0:T(8,128)S(1)} custom-call(s32[8]{0:T(128)S(1)} %broadcast_in_dim.237.layer_ref, s32[8]{0:T(128)S(1)} %get-tuple-element.27.size_ref, s32[1216]{0:T(1024)S(1)} %get-tuple-element.29.list_ref, f32[61,128,128]{2,1,0:T(8,128)S(1)} %get-tuple-element.30.acc_in, ...), custom_call_target="tpu_custom_call", output_to_operand_aliasing={{}: (3, {})} | custom-call | tf_op jit(solution)/shard_map/near_products/pallas_call | solution.py:213
  50.1 4.8 %far_products.1 = (bf16[60,128,128]{2,1,0:T(8,128)(2,1)}, f32[61,128,128]{2,1,0:T(8,128)S(1)}) custom-call(s32[8]{0:T(128)S(1)} %broadcast_in_dim.232.more_ref, s32[8]{0:T(128)S(1)} %get-tuple-element.27.size_ref, s32[1216]{0:T(1024)S(1)} %get-tuple-element.28.list_ref, f32[61,128,128]{2,1,0:T(8,128)S(1)} %near_products.1.acc_in, ...), custom_call_target="tpu_custom_call", output_to_operand_aliasing={{1}: (3, {})} | custom-call | tf_op jit(solution)/shard_map/far_products/pallas_call | solution.py:274
  (72 shorter events, 2.4 us)
Async XLA Ops:
  0.0 31.7 %collective-permute-start.2 = (bf16[240,128,128]{2,1,0:T(8,128)(2,1)}, bf16[240,128,128]{2,1,0:T(8,128)(2,1)}, u32[]{:S(2)}, u32[]{:S(2)}) collective-permute-start(bf16[240,128,128]{2,1,0:T(8,128)(2,1)} %bitcast.22), channel_id=1, source_target_pairs={{0,1},{1,0},{2,3},{3,2},{4,5},{5,4},{6,7},{7,6},{8,9},{9,8},{10,11... | collective-permute-start | bytes 23592968 | tf_op jit(solution)/shard_map/ppermute | solution.py:375
  1.1 16.1 %collective-permute-start.1 = (bf16[18,128,128]{2,1,0:T(8,128)(2,1)S(1)}, bf16[18,128,128]{2,1,0:T(8,128)(2,1)S(1)}, u32[]{:S(2)}, u32[]{:S(2)}) collective-permute-start(bf16[18,128,128]{2,1,0:T(8,128)(2,1)S(1)} %bitcast.26), channel_id=1, source_target_pairs={{0,63},{1,2},{2,1},{3,4},{4,3},{5,6},{6,5},{7,8},{8,7},{9,10},{10,... | collective-permute-start | bytes 1769480 | tf_op jit(solution)/shard_map/ppermute | solution.py:387
  15.2 11.8 %copy-start = (s32[768,20]{0,1:T(8,128)S(1)}, s32[768,20]{0,1:T(8,128)}, u32[]{:S(2)}) copy-start(s32[768,20]{0,1:T(8,128)} %param.6) | copy-start | bytes 184324
  15.2 11.7 %copy-start.1 = (s32[768]{0:T(1024)S(1)}, s32[768]{0:T(1024)}, u32[]{:S(2)}) copy-start(s32[768]{0:T(1024)} %param.7) | copy-start | bytes 9220
  17.2 29.5 %collective-permute-start.3 = (bf16[18,128,128]{2,1,0:T(8,128)(2,1)S(1)}, bf16[18,128,128]{2,1,0:T(8,128)(2,1)S(1)}, u32[]{:S(2)}, u32[]{:S(2)}) collective-permute-start(bf16[18,128,128]{2,1,0:T(8,128)(2,1)S(1)} %collective-permute-done.1.near0_ref), channel_id=1, source_target_pairs={{0,64},{64,128},{128,192},{192,0},{1,65},{65,129},{129,193},{193,1... | collective-permute-start | bytes 1769480 | tf_op jit(solution)/shard_map/ppermute | solution.py:438
  18.7 28.0 %collective-permute-start.4 = (bf16[18,128,128]{2,1,0:T(8,128)(2,1)S(1)}, bf16[18,128,128]{2,1,0:T(8,128)(2,1)}, u32[]{:S(2)}, u32[]{:S(2)}) collective-permute-start(bf16[18,128,128]{2,1,0:T(8,128)(2,1)S(1)} %collective-permute-done.1.near0_ref), channel_id=1, source_target_pairs={{0,128},{64,192},{128,0},{192,64},{1,129},{65,193},{129,1},{193,65... | collective-permute-start | bytes 1769480 | tf_op jit(solution)/shard_map/ppermute | solution.py:438
  22.5 27.6 %collective-permute-start.6 = (bf16[60,128,128]{2,1,0:T(8,128)(2,1)S(1)}, bf16[60,128,128]{2,1,0:T(8,128)(2,1)}, u32[]{:S(2)}, u32[]{:S(2)}) collective-permute-start(bf16[60,128,128]{2,1,0:T(8,128)(2,1)S(1)} %pack.3), channel_id=1, source_target_pairs={{0,63},{1,2},{2,1},{3,4},{4,3},{5,6},{6,5},{7,8},{8,7},{9,10},{10,... | collective-permute-start | bytes 5898248 | tf_op jit(solution)/shard_map/ppermute | solution.py:442
  29.4 17.3 %collective-permute-start.5 = (bf16[18,128,128]{2,1,0:T(8,128)(2,1)S(1)}, bf16[18,128,128]{2,1,0:T(8,128)(2,1)S(1)}, u32[]{:S(2)}, u32[]{:S(2)}) collective-permute-start(bf16[18,128,128]{2,1,0:T(8,128)(2,1)S(1)} %collective-permute-done.1.near0_ref), channel_id=1, source_target_pairs={{0,192},{64,0},{128,64},{192,128},{1,193},{65,1},{129,65},{193,129... | collective-permute-start | bytes 1769480 | tf_op jit(solution)/shard_map/ppermute | solution.py:438

commit v5 on v4

--- a/solution.py
+++ b/solution.py
@@ -2,6 +2,7 @@
 
 import jax
 import jax.numpy as jnp
+import numpy as np
 from jax import lax
 from jax.experimental import pallas as pl
 from jax.experimental.pallas import tpu as pltpu
@@ -89,13 +90,13 @@
     count = rows * slots
     outs = rows * quarter
     size = 2 * UNROLL
-    load = pltpu.make_async_copy(inner_ref, inner_v.at[pl.ds(1 + count, count)], sem.at[0])
+    load = pltpu.make_async_copy(inner_ref, inner_v.at[pl.ds(count, count)], sem.at[0])
     load.start()
-    load_own = pltpu.make_async_copy(blocks_ref, inner_v.at[pl.ds(1, count)], sem.at[1])
+    load_own = pltpu.make_async_copy(blocks_ref, inner_v.at[pl.ds(0, count)], sem.at[1])
     load_own.start()
-    load_a = pltpu.make_async_copy(blocks_ref, a_ref, sem.at[2])
+    load_a = pltpu.make_async_copy(blocks_ref, a_ref.at[pl.ds(0, count)], sem.at[2])
     load_a.start()
-    inner_v[0] = jnp.zeros(inner_v.shape[1:], inner_v.dtype)
+    a_ref[count] = jnp.zeros(a_ref.shape[1:], a_ref.dtype)
 
     def clear(o, carry):
         acc_ref[o] = jnp.zeros(acc_ref.shape[1:], acc_ref.dtype)
@@ -124,9 +125,10 @@
                     e_own += (code >> 10) & 1
                     e_near += (code >> 11) & 1
                     e_far += code >> 12
-                own_ref[e_own] = tag
-                near_ref[e_near] = tag
-                far_ref[e_far] = tag
+                none = ((i * quarter + p) << 18) | (count << 10)
+                own_ref[e_own] = none
+                near_ref[e_near] = none
+                far_ref[e_far] = none
                 return e_own + (e_own & 1), e_near + (e_near & 1), e_far + (e_far & 1)
 
             return lax.cond(j_at < 3 * rows, terms, lambda ends: ends, ends)
@@ -136,9 +138,10 @@
     zero = jnp.int32(0)
     e_own, e_near, e_far = lax.fori_loop(0, rows, one_row, (zero, zero, zero))
     for u in range(size):
-        own_ref[e_own + u] = outs << 18
-        near_ref[e_near + u] = outs << 18
-        far_ref[e_far + u] = outs << 18
+        none = (outs << 18) | (count << 10)
+        own_ref[e_own + u] = none
+        near_ref[e_near + u] = none
+        far_ref[e_far + u] = none
     size_ref[0] = (e_near + size - 1) // size * size
     size_ref[1] = (e_far + size - 1) // size * size
     load_own.wait()
@@ -155,7 +158,7 @@
         functools.partial(local_kernel, rows, slots, quarter),
         out_shape=(
             jax.ShapeDtypeStruct((outs + 1, edge, edge), jnp.float32),
-            jax.ShapeDtypeStruct(blocks.shape, blocks.dtype),
+            jax.ShapeDtypeStruct((rows * slots + 1, edge, edge), blocks.dtype),
             jax.ShapeDtypeStruct((length,), jnp.int32),
             jax.ShapeDtypeStruct((length,), jnp.int32),
             jax.ShapeDtypeStruct((8,), jnp.int32),
@@ -164,7 +167,7 @@
         out_specs=(VMEM, VMEM, SMEM, SMEM, SMEM),
         scratch_shapes=[
             pltpu.SMEM((length,), jnp.int32),
-            pltpu.VMEM((2 * rows * slots + 1, edge, edge), blocks.dtype),
+            pltpu.VMEM((2 * rows * slots, edge, edge), blocks.dtype),
             pltpu.SemaphoreType.DMA((3,)),
         ],
         compiler_params=pltpu.CompilerParams(vmem_limit_bytes=32 << 20),
@@ -196,12 +199,11 @@
         source = lax.rem(layer_ref[0] + len(nears) - away, len(nears))
         copies.append(
             pltpu.make_async_copy(
-                ref, v_ref.at[pl.ds(1 + source * near, near)], sem.at[away]
+                ref, v_ref.at[pl.ds(source * near, near)], sem.at[away]
             )
         )
     for copy in copies:
         copy.start()
-    v_ref[0] = jnp.zeros(v_ref.shape[1:], v_ref.dtype)
     for copy in copies:
         copy.wait()
     run_list(list_ref, size_ref[0], a_ref, v_ref, acc_ref)
@@ -209,7 +211,7 @@
 
 def near_products(layer, size, entries, acc, blocks, nears):
     edge = blocks.shape[-1]
-    held = 1 + len(nears) * nears[0].shape[0]
+    held = len(nears) * nears[0].shape[0]
     return pl.pallas_call(
         near_kernel,
         out_shape=jax.ShapeDtypeStruct(acc.shape, acc.dtype),
@@ -242,47 +244,52 @@
     sem,
 ):
     first, late = first_ref.shape[0], late_ref.shape[0]
-    load = pltpu.make_async_copy(first_ref, v_ref.at[pl.ds(1, first)], sem.at[0])
-    load.start()
-    v_ref[0] = jnp.zeros(v_ref.shape[1:], v_ref.dtype)
-
-    @pl.when(more_ref[0] > 0)
+
+    @pl.when(more_ref[0] == 0)
+    def _():
+        run_list(list_ref, size_ref[1], a_ref, first_ref, acc_ref)
+
+    @pl.when(more_ref[0] != 0)
     def _():
         late_copy = pltpu.make_async_copy(
-            late_ref, v_ref.at[pl.ds(1 + first, late)], sem.at[1]
+            late_ref, v_ref.at[pl.ds(first, late)], sem.at[0]
         )
         late_copy.start()
+
+        def move(b, carry):
+            v_ref[b] = first_ref[b]
+            return carry
+
+        lax.fori_loop(0, first, move, 0)
         late_copy.wait()
-
-    load.wait()
-    run_list(list_ref, size_ref[1], a_ref, v_ref, acc_ref)
+        run_list(list_ref, size_ref[1], a_ref, v_ref, acc_ref)
 
     def finish(i, carry):
         part = pl.ds(i * quarter, quarter)
         held[part] = acc_ref[part].astype(held.dtype)
-        pltpu.make_async_copy(held.at[part], out_ref.at[part], sem.at[2]).start()
+        pltpu.make_async_copy(held.at[part], out_ref.at[part], sem.at[1]).start()
         return carry
 
     lax.fori_loop(0, rows, finish, 0)
-    pltpu.make_async_copy(held, out_ref, sem.at[2]).wait()
+    pltpu.make_async_copy(held, out_ref, sem.at[1]).wait()
 
 
 def far_products(more, size, entries, acc, blocks, first, late, rows, quarter):
     edge = blocks.shape[-1]
     outs = rows * quarter
-    held = 1 + first.shape[0] + late.shape[0]
+    held = first.shape[0] + late.shape[0]
     square, _ = pl.pallas_call(
         functools.partial(far_kernel, rows, quarter),
         out_shape=(
             jax.ShapeDtypeStruct((outs, edge, edge), blocks.dtype),
             jax.ShapeDtypeStruct(acc.shape, acc.dtype),
         ),
-        in_specs=[SMEM] * 3 + [VMEM, VMEM, ANY, ANY],
+        in_specs=[SMEM] * 3 + [VMEM, VMEM, VMEM, ANY],
         out_specs=(ANY, VMEM),
         scratch_shapes=[
             pltpu.VMEM((held, edge, edge), blocks.dtype),
             pltpu.VMEM((outs, edge, edge), blocks.dtype),
-            pltpu.SemaphoreType.DMA((3,)),
+            pltpu.SemaphoreType.DMA((2,)),
         ],
         input_output_aliases={3: 1},
         compiler_params=pltpu.CompilerParams(vmem_limit_bytes=24 << 20),
@@ -352,9 +359,9 @@
     close = jnp.where(odd, kk >= BAND - NEAR_ROWS, kk < NEAR_ROWS)
     asked = jnp.where(odd, up, down) & mask & jnp.where(close, ~fixed, ~jnp.uint32(0))
     per_row = lax.population_count(asked).astype(jnp.bfloat16)
-    member = rows_id[:, None] // BAND == jnp.arange(total_rows // BAND)[None, :]
+    member = np.arange(total_rows)[:, None] // BAND == np.arange(total_rows // BAND)
     per_group = jnp.dot(
-        per_row, member.astype(jnp.bfloat16), preferred_element_type=jnp.float32
+        per_row, jnp.asarray(member, jnp.bfloat16), preferred_element_type=jnp.float32
     )
     return jnp.max(per_group)
 
@@ -433,25 +440,27 @@
     )
     send_idx = jnp.sum(jnp.where(hit, give_ids[:, None], 0), axis=0)
 
-    send_idx, near_mine = lax.optimization_barrier((send_idx, near_mine))
+    packed = pack(send_idx, blocks, 0, FIRST)
+    _, near_mine, columns, counts = lax.optimization_barrier(
+        (packed, near_mine, columns, counts)
+    )
     nears = [near_mine] + [
         lax.ppermute(near_mine, "layer", [(x, (x + d) % layers) for x in range(layers)])
         for d in range(1, layers)
     ]
-    packed = pack(send_idx, blocks, 0, FIRST)
     outer = lax.ppermute(packed, ("row", "col"), outer_pairs)
 
-    code = jnp.where(get, (4 << 10) + 1 + get_pos, 0)
+    code = jnp.where(get, (4 << 10) + get_pos, 0)
     code = jnp.where(even, code.reshape(rows, slots)[::-1], code.reshape(rows, slots))
     row_at = jnp.arange(rows, dtype=jnp.int32)[:, None] - jnp.where(even, rows - NEAR_ROWS, 0)
     sent = (row_at >= 0) & (row_at < NEAR_ROWS) & (slot_ids < NEAR_SLOTS)
     sent_at = (slot_ids // share * NEAR_ROWS + row_at) * share + slot_ids % share
     far_live = jnp.where(even, live[0], live[2])
-    code = jnp.where(sent & far_live, (2 << 10) + 1 + sent_at, code)
+    code = jnp.where(sent & far_live, (2 << 10) + sent_at, code)
     ids = ids.reshape(rows, slots)
-    own = jnp.where(live[1], (1 << 10) + 1 + ids, 0)
+    own = jnp.where(live[1], (1 << 10) + ids, 0)
     near = jnp.where(even, live[2], live[0])
-    near = jnp.where(near, (1 << 10) + 1 + span + ids, 0)
+    near = jnp.where(near, (1 << 10) + span + ids, 0)
     codes = jnp.concatenate(
         [jnp.where(even, code, near), own, jnp.where(even, near, code)], axis=0
     )
@@ -464,7 +473,6 @@
     place = jnp.where(
         live[1], jnp.arange(rows, dtype=jnp.int32)[:, None] + off[1], 3 * rows
     ).reshape(-1)
-    columns, counts, packed = lax.optimization_barrier((columns, counts, packed))
     more = most_needed(columns, counts, layers) > FIRST
 
     def second():

time: 55.8 us -> 51.9 us (0.930)
  the two profiles are of different devices: /device:TPU:2 before, /device:TPU:107 now
where the time goes in v5:
time: 51.9 us; the launch traced here: 51.5 us
  Pallas kernels  25.4 us (49%)
  waiting for transfers between devices  8.8 us (17%)
  starting transfers between devices  8.17 us (16%)
  local copies, waits for them, and re-layouts  3.88 us (7%)
  other arithmetic  3.11 us (6%)
  matrix products  1.12 us (2%)
  between operations  1.01 us (2%)
    pallas_call x1, Pallas kernels, local_products(): pl.pallas_call(functools.partial(local_kernel, rows, slots, quarter), out...  14.8 us
    ppermute x3, waiting for transfers between devices, per_device(): lax.ppermute(near_mine, 'layer', [(x, (x + d) % layers) for x in range(la...  8.79 us
    ppermute x3, starting transfers between devices, per_device(): lax.ppermute(near_mine, 'layer', [(x, (x + d) % layers) for x in range(la...  4.53 us
    pallas_call x1, Pallas kernels, far_products(): pl.pallas_call(functools.partial(far_kernel, rows, quarter), out_shape=(j...  4.02 us
    pallas_call x1, Pallas kernels, near_products(): pl.pallas_call(near_kernel, out_shape=jax.ShapeDtypeStruct(acc.shape, acc...  3.54 us
    pallas_call x1, Pallas kernels, pack(): pl.pallas_call(functools.partial(pack_kernel, start, size), out_shape=jax...  3 us
    ppermute x1, starting transfers between devices, per_device(): near_mine = lax.ppermute(near_rows, ('row', 'col'), outer_pairs)  2.82 us
    dynamic_slice x1, local copies, waits for them, and re-layouts, per_device(): lax.dynamic_slice(values, (jnp.where(even, 0, rows - NEAR_ROWS), layer *...  1.1 us
  transfers between devices with their start and end apart: 6, of which 1 were waited for; matrix products, arithmetic and copies ran while one was open for 16% of the time, Pallas kernels for 41%

profile of v5, /device:TPU:107, one launch (start us, length us, event | category | flops | bytes accessed | tf_op | source)
XLA Modules:
  0.0 51.5 jit_solution(11211340128612569594)
XLA Ops:
  0.0 0.7 %collective-permute-start.2 = (bf16[240,128,128]{2,1,0:T(8,128)(2,1)}, bf16[240,128,128]{2,1,0:T(8,128)(2,1)}, u32[]{:S(2)}, u32[]{:S(2)}) collective-permute-start(bf16[240,128,128]{2,1,0:T(8,128)(2,1)} %bitcast.23), channel_id=1, source_target_pairs={{0,1},{1,0},{2,3},{3,2},{4,5},{5,4},{6,7},{7,6},{8,9},{9,8},{10,11... | collective-permute-start | bytes 23592968 | tf_op jit(solution)/shard_map/ppermute | solution.py:382
  0.7 1.1 %constant_dynamic-slice_fusion = bf16[6,3,128,128]{3,2,1,0:T(8,128)(2,1)S(1)} fusion(bf16[12,20,128,128]{3,2,1,0:T(8,128)(2,1)} %param.6, s32[]{:T(128)S(6)} %select_n.443, s32[]{:T(128)S(6)} %select_n.444), kind=kLoop, calls=%fused_computation.295 | loop fusion | bytes 1179656 | tf_op jit(solution)/shard_map/dynamic_slice | solution.py:389
  1.8 2.8 %collective-permute-start.1 = (bf16[18,128,128]{2,1,0:T(8,128)(2,1)S(1)}, bf16[18,128,128]{2,1,0:T(8,128)(2,1)S(1)}, u32[]{:S(2)}, u32[]{:S(2)}) collective-permute-start(bf16[18,128,128]{2,1,0:T(8,128)(2,1)S(1)} %bitcast.27), channel_id=1, source_target_pairs={{0,63},{1,2},{2,1},{3,4},{4,3},{5,6},{6,5},{7,8},{8,7},{9,10},{10,... | collective-permute-start | bytes 1769480 | tf_op jit(solution)/shard_map/ppermute | solution.py:394
  4.6 0.7 %broadcast_in_dim.197 = s32[1,768]{1,0:T(1,128)S(1)} reshape(s32[768]{0:T(1024)} %param.8) | data formatting | bytes 6144 | tf_op jit(solution)/shard_map/broadcast_in_dim | solution.py:395
  5.3 0.9 %pad_add_fusion = s32[21,768]{1,0:T(8,128)S(1)} fusion(s32[1,768]{1,0:T(1,128)S(1)} %broadcast_in_dim.197, s32[20,768]{1,0:T(8,128)} %bitcast.28), kind=kLoop, calls=%fused_computation.15 | loop fusion | flops 16128 | bytes 129024 | tf_op jit(solution)/shard_map/concatenate | solution.py:395
  6.7 0.1 copy.30
  6.8 0.1 copy.31
  6.9 0.1 fusion.67
  7.2 0.1 select_reduce_fusion.3
  7.3 0.1 select_reduce_fusion.4
  7.7 0.1 copy.33
  7.9 0.1 copy.34
  8.0 0.1 stack.32
  8.3 0.1 and.425
  8.5 0.1 copy.32
  8.7 0.2 convolution_convert_fusion
  8.9 0.1 select_reduce_fusion.1.idx_ref
  9.1 3.0 %pack.3 = bf16[60,128,128]{2,1,0:T(8,128)(2,1)S(1)} custom-call(s32[132]{0:T(256)S(1)} %select_reduce_fusion.1.idx_ref, bf16[240,128,128]{2,1,0:T(8,128)(2,1)} %bitcast.24), custom_call_target="tpu_custom_call" | custom-call | tf_op jit(solution)/shard_map/pack/pallas_call | solution.py:37
  12.1 0.1 collective-permute-start.6
  12.3 0.1 copy.36
  12.8 0.3 select_reduce_fusion
  13.3 1.5 %collective-permute-start.3 = (bf16[18,128,128]{2,1,0:T(8,128)(2,1)S(1)}, bf16[18,128,128]{2,1,0:T(8,128)(2,1)S(1)}, u32[]{:S(2)}, u32[]{:S(2)}) collective-permute-start(bf16[18,128,128]{2,1,0:T(8,128)(2,1)S(1)} %collective-permute-done.1.near0_ref), channel_id=1, source_target_pairs={{0,64},{64,128},{128,192},{192,0},{1,65},{65,129},{129,193},{193,1... | collective-permute-start | bytes 1769480 | tf_op jit(solution)/shard_map/ppermute | solution.py:448
  14.8 1.0 %collective-permute-start.4 = (bf16[18,128,128]{2,1,0:T(8,128)(2,1)S(1)}, bf16[18,128,128]{2,1,0:T(8,128)(2,1)}, u32[]{:S(2)}, u32[]{:S(2)}) collective-permute-start(bf16[18,128,128]{2,1,0:T(8,128)(2,1)S(1)} %collective-permute-done.1.near0_ref), channel_id=1, source_target_pairs={{0,128},{64,192},{128,0},{192,64},{1,129},{65,193},{129,1},{193,65... | collective-permute-start | bytes 1769480 | tf_op jit(solution)/shard_map/ppermute | solution.py:448
  16.1 0.1 pad_add_fusion.1
  16.4 0.1 fusion.155
  16.5 0.1 fusion.143
  16.6 1.0 %convolution_reduce_fusion = f32[]{:T(128)} fusion(bf16[768,64]{1,0:T(8,128)(2,1)S(1)} %copy-done.2, u32[4,780]{1,0:T(4,128)S(1)} %get-tuple-element.47, u32[4,780]{1,0:T(4,128)S(1)} %get-tuple-element.46, u32[768]{0:T(1024)S(1)} %not_select_fusion, u32[768]{0:T(1024)S(1)} %get-tuple-element.42, pred[768]{0:T(1024)(128)(4,1)S(1)} %get-tuple-element.69, ...), kind=kOutput, calls=%fused_computation.1 | convolution fusion | flops 623871 | bytes 525316 | tf_op jit(solution)/shard_map/dot_general | solution.py:363
  18.2 2.0 %collective-permute-start.5 = (bf16[18,128,128]{2,1,0:T(8,128)(2,1)S(1)}, bf16[18,128,128]{2,1,0:T(8,128)(2,1)S(1)}, u32[]{:S(2)}, u32[]{:S(2)}) collective-permute-start(bf16[18,128,128]{2,1,0:T(8,128)(2,1)S(1)} %collective-permute-done.1.near0_ref), channel_id=1, source_target_pairs={{0,192},{64,0},{128,64},{192,128},{1,193},{65,1},{129,65},{193,129... | collective-permute-start | bytes 1769480 | tf_op jit(solution)/shard_map/ppermute | solution.py:448
  20.3 14.8 %local_products.1 = (f32[61,128,128]{2,1,0:T(8,128)S(1)}, bf16[241,128,128]{2,1,0:T(8,128)(2,1)S(1)}, s32[1216]{0:T(1024)S(1)}, s32[1216]{0:T(1024)S(1)}, s32[8]{0:T(128)S(1)}) custom-call(s32[8]{0:T(128)S(1)} %broadcast_in_dim.231.start_ref, s32[2368]{0:T(1024)S(1)} %concatenate.78.table_ref, s32[240]{0:T(256)S(1)} %reshape.318.place_ref, ...), custom_call_target="tpu_custom_call" | custom-call | flops 10000000000 | bytes 24000000 | tf_op jit(solution)/shard_map/local_products/pallas_call | solution.py:157
  35.1 8.8 %collective-permute-done.5.near3_ref = bf16[18,128,128]{2,1,0:T(8,128)(2,1)S(1)} collective-permute-done((bf16[18,128,128]{2,1,0:T(8,128)(2,1)S(1)}, bf16[18,128,128]{2,1,0:T(8,128)(2,1)S(1)}, u32[]{:S(2)}, u32[]{:S(2)}) %collective-permute-start.5) | collective-permute-done | bytes 589856 | tf_op jit(solution)/shard_map/ppermute | solution.py:448
  43.9 3.5 %near_products.1.acc_in = f32[61,128,128]{2,1,0:T(8,128)S(1)} custom-call(s32[8]{0:T(128)S(1)} %broadcast_in_dim.235.layer_ref, s32[8]{0:T(128)S(1)} %get-tuple-element.25.size_ref, s32[1216]{0:T(1024)S(1)} %get-tuple-element.27.list_ref, f32[61,128,128]{2,1,0:T(8,128)S(1)} %get-tuple-element.28.acc_in, ...), custom_call_target="tpu_custom_call", output_to_operand_aliasing={{}: (3, {})} | custom-call | tf_op jit(solution)/shard_map/near_products/pallas_call | solution.py:215
  47.5 4.0 %far_products.1 = (bf16[60,128,128]{2,1,0:T(8,128)(2,1)}, f32[61,128,128]{2,1,0:T(8,128)S(1)}) custom-call(s32[8]{0:T(128)S(1)} %broadcast_in_dim.230.more_ref, s32[8]{0:T(128)S(1)} %get-tuple-element.25.size_ref, s32[1216]{0:T(1024)S(1)} %get-tuple-element.26.list_ref, f32[61,128,128]{2,1,0:T(8,128)S(1)} %near_products.1.acc_in, ...), custom_call_target="tpu_custom_call", output_to_operand_aliasing={{1}: (3, {})} | custom-call | tf_op jit(solution)/shard_map/far_products/pallas_call | solution.py:281
  (73 shorter events, 2.5 us)
Async XLA Ops:
  0.0 20.3 %collective-permute-start.2 = (bf16[240,128,128]{2,1,0:T(8,128)(2,1)}, bf16[240,128,128]{2,1,0:T(8,128)(2,1)}, u32[]{:S(2)}, u32[]{:S(2)}) collective-permute-start(bf16[240,128,128]{2,1,0:T(8,128)(2,1)} %bitcast.23), channel_id=1, source_target_pairs={{0,1},{1,0},{2,3},{3,2},{4,5},{5,4},{6,7},{7,6},{8,9},{9,8},{10,11... | collective-permute-start | bytes 23592968 | tf_op jit(solution)/shard_map/ppermute | solution.py:382
  1.8 11.6 %collective-permute-start.1 = (bf16[18,128,128]{2,1,0:T(8,128)(2,1)S(1)}, bf16[18,128,128]{2,1,0:T(8,128)(2,1)S(1)}, u32[]{:S(2)}, u32[]{:S(2)}) collective-permute-start(bf16[18,128,128]{2,1,0:T(8,128)(2,1)S(1)} %bitcast.27), channel_id=1, source_target_pairs={{0,63},{1,2},{2,1},{3,4},{4,3},{5,6},{6,5},{7,8},{8,7},{9,10},{10,... | collective-permute-start | bytes 1769480 | tf_op jit(solution)/shard_map/ppermute | solution.py:394
  9.0 6.8 %copy-start = (s32[768,20]{0,1:T(8,128)S(1)}, s32[768,20]{0,1:T(8,128)}, u32[]{:S(2)}) copy-start(s32[768,20]{0,1:T(8,128)} %param.7) | copy-start | bytes 184324
  9.0 6.8 %copy-start.1 = (s32[768]{0:T(1024)S(1)}, s32[768]{0:T(1024)}, u32[]{:S(2)}) copy-start(s32[768]{0:T(1024)} %param.8) | copy-start | bytes 9220
  9.1 7.5 %copy-start.2 = (bf16[768,64]{1,0:T(8,128)(2,1)S(1)}, bf16[768,64]{1,0:T(8,128)(2,1)}, u32[]{:S(2)}) copy-start(bf16[768,64]{1,0:T(8,128)(2,1)} %constant.250.clone) | copy-start | bytes 294916
  12.1 35.4 %collective-permute-start.6 = (bf16[60,128,128]{2,1,0:T(8,128)(2,1)S(1)}, bf16[60,128,128]{2,1,0:T(8,128)(2,1)}, u32[]{:S(2)}, u32[]{:S(2)}) collective-permute-start(bf16[60,128,128]{2,1,0:T(8,128)(2,1)S(1)} %pack.3), channel_id=1, source_target_pairs={{0,63},{1,2},{2,1},{3,4},{4,3},{5,6},{6,5},{7,8},{8,7},{9,10},{10,... | collective-permute-start | bytes 5898248 | tf_op jit(solution)/shard_map/ppermute | solution.py:451
  13.3 21.7 %collective-permute-start.3 = (bf16[18,128,128]{2,1,0:T(8,128)(2,1)S(1)}, bf16[18,128,128]{2,1,0:T(8,128)(2,1)S(1)}, u32[]{:S(2)}, u32[]{:S(2)}) collective-permute-start(bf16[18,128,128]{2,1,0:T(8,128)(2,1)S(1)} %collective-permute-done.1.near0_ref), channel_id=1, source_target_pairs={{0,64},{64,128},{128,192},{192,0},{1,65},{65,129},{129,193},{193,1... | collective-permute-start | bytes 1769480 | tf_op jit(solution)/shard_map/ppermute | solution.py:448
  14.8 20.3 %collective-permute-start.4 = (bf16[18,128,128]{2,1,0:T(8,128)(2,1)S(1)}, bf16[18,128,128]{2,1,0:T(8,128)(2,1)}, u32[]{:S(2)}, u32[]{:S(2)}) collective-permute-start(bf16[18,128,128]{2,1,0:T(8,128)(2,1)S(1)} %collective-permute-done.1.near0_ref), channel_id=1, source_target_pairs={{0,128},{64,192},{128,0},{192,64},{1,129},{65,193},{129,1},{193,65... | collective-permute-start | bytes 1769480 | tf_op jit(solution)/shard_map/ppermute | solution.py:448
  18.2 25.7 %collective-permute-start.5 = (bf16[18,128,128]{2,1,0:T(8,128)(2,1)S(1)}, bf16[18,128,128]{2,1,0:T(8,128)(2,1)S(1)}, u32[]{:S(2)}, u32[]{:S(2)}) collective-permute-start(bf16[18,128,128]{2,1,0:T(8,128)(2,1)S(1)} %collective-permute-done.1.near0_ref), channel_id=1, source_target_pairs={{0,192},{64,0},{128,64},{192,128},{1,193},{65,1},{129,65},{193,129... | collective-permute-start | bytes 1769480 | tf_op jit(solution)/shard_map/ppermute | solution.py:448

commit v6 on v5

--- a/solution.py
+++ b/solution.py
@@ -12,10 +12,10 @@
 STRIDE = 64
 WIDE = 16
 UNROLL = 4
-NEAR_ROWS = 6
+NEAR_ROWS = 5
 NEAR_SLOTS = 12
-FIRST = 60
-BOUND = 132
+FIRST = 68
+BOUND = 140
 ANY = pl.BlockSpec(memory_space=pl.ANY)
 SMEM = pl.BlockSpec(memory_space=pltpu.SMEM)
 VMEM = pl.BlockSpec(memory_space=pltpu.VMEM)
@@ -172,7 +172,7 @@
         ],
         compiler_params=pltpu.CompilerParams(vmem_limit_bytes=32 << 20),
         cost_estimate=pl.CostEstimate(
-            flops=10 * 10**9, bytes_accessed=24 * 10**6, transcendentals=0
+            flops=2 * 10**9, bytes_accessed=8 * 10**6, transcendentals=0
         ),
         name="local_products",
     )(start, table, place, blocks, inner)
@@ -473,6 +473,7 @@
     place = jnp.where(
         live[1], jnp.arange(rows, dtype=jnp.int32)[:, None] + off[1], 3 * rows
     ).reshape(-1)
+    inner, columns, counts = lax.optimization_barrier((inner, columns, counts))
     more = most_needed(columns, counts, layers) > FIRST
 
     def second():

time: 51.9 us -> 52 us (level)
  the two profiles are of different devices: /device:TPU:107 before, /device:TPU:2 now
where the time goes in v6:
time: 52 us; the launch traced here: 51.2 us
  Pallas kernels  26.1 us (50%)
  starting transfers between devices  13.7 us (26%)
  local copies, waits for them, and re-layouts  3.84 us (7%)
  other arithmetic  3.11 us (6%)
  waiting for transfers between devices  2.25 us (4%)
  matrix products  1.12 us (2%)
  between operations  1.05 us (2%)
    pallas_call x1, Pallas kernels, local_products(): pl.pallas_call(functools.partial(local_kernel, rows, slots, quarter), out...  15.5 us
    ppermute x1, starting transfers between devices, per_device(): near_mine = lax.ppermute(near_rows, ('row', 'col'), outer_pairs)  8.5 us
    ppermute x3, starting transfers between devices, per_device(): lax.ppermute(near_mine, 'layer', [(x, (x + d) % layers) for x in range(la...  5.12 us
    pallas_call x1, Pallas kernels, far_products(): pl.pallas_call(functools.partial(far_kernel, rows, quarter), out_shape=(j...  3.86 us
    pallas_call x1, Pallas kernels, near_products(): pl.pallas_call(near_kernel, out_shape=jax.ShapeDtypeStruct(acc.shape, acc...  3.83 us
    pallas_call x1, Pallas kernels, pack(): pl.pallas_call(functools.partial(pack_kernel, start, size), out_shape=jax...  2.96 us
    ppermute x1, waiting for transfers between devices, per_device(): outer = lax.ppermute(packed, ('row', 'col'), outer_pairs)  2.23 us
    dynamic_slice x1, local copies, waits for them, and re-layouts, per_device(): lax.dynamic_slice(values, (jnp.where(even, 0, rows - NEAR_ROWS), layer *...  1.06 us
  transfers between devices with their start and end apart: 6, of which 1 were waited for; matrix products, arithmetic and copies ran while one was open for 16% of the time, Pallas kernels for 43%

profile of v6, /device:TPU:2, one launch (start us, length us, event | category | flops | bytes accessed | tf_op | source)
XLA Modules:
  0.0 51.2 jit_solution(13058086551811101043)
XLA Ops:
  0.0 1.1 %constant_dynamic-slice_fusion = bf16[5,3,128,128]{3,2,1,0:T(8,128)(2,1)S(1)} fusion(bf16[12,20,128,128]{3,2,1,0:T(8,128)(2,1)} %param.6, s32[]{:T(128)S(6)} %select_n.443, s32[]{:T(128)S(6)} %select_n.444), kind=kLoop, calls=%fused_computation.295 | loop fusion | bytes 983048 | tf_op jit(solution)/shard_map/dynamic_slice | solution.py:389
  1.1 8.5 %collective-permute-start.2 = (bf16[15,128,128]{2,1,0:T(8,128)(2,1)S(1)}, bf16[15,128,128]{2,1,0:T(8,128)(2,1)S(1)}, u32[]{:S(2)}, u32[]{:S(2)}) collective-permute-start(bf16[15,128,128]{2,1,0:T(8,128)(2,1)S(1)} %bitcast.27), channel_id=1, source_target_pairs={{0,63},{1,2},{2,1},{3,4},{4,3},{5,6},{6,5},{7,8},{8,7},{9,10},{10,... | collective-permute-start | bytes 1474568 | tf_op jit(solution)/shard_map/ppermute | solution.py:394
  9.6 0.7 %broadcast_in_dim.197 = s32[1,768]{1,0:T(1,128)S(1)} reshape(s32[768]{0:T(1024)} %param.8) | data formatting | bytes 6144 | tf_op jit(solution)/shard_map/broadcast_in_dim | solution.py:395
  10.3 0.9 %pad_add_fusion = s32[21,768]{1,0:T(8,128)S(1)} fusion(s32[1,768]{1,0:T(1,128)S(1)} %broadcast_in_dim.197, s32[20,768]{1,0:T(8,128)} %bitcast.28), kind=kLoop, calls=%fused_computation.15 | loop fusion | flops 16128 | bytes 129024 | tf_op jit(solution)/shard_map/concatenate | solution.py:395
  11.6 0.1 copy.30
  11.7 0.1 copy.31
  11.9 0.1 fusion.67
  12.2 0.1 select_reduce_fusion.3
  12.3 0.1 select_reduce_fusion.4
  12.7 0.1 copy.33
  12.9 0.1 copy.34
  13.0 0.1 stack.32
  13.3 0.1 and.425
  13.5 0.1 copy.32
  13.7 0.2 convolution_convert_fusion
  13.9 0.1 select_reduce_fusion.1.idx_ref
  14.0 3.0 %pack.3 = bf16[68,128,128]{2,1,0:T(8,128)(2,1)S(1)} custom-call(s32[140]{0:T(256)S(1)} %select_reduce_fusion.1.idx_ref, bf16[240,128,128]{2,1,0:T(8,128)(2,1)} %bitcast.24), custom_call_target="tpu_custom_call" | custom-call | tf_op jit(solution)/shard_map/pack/pallas_call | solution.py:37
  17.0 0.1 collective-permute-start.6
  17.2 0.1 copy.36
  17.7 0.3 select_reduce_fusion
  18.0 0.1 copy.37
  18.2 1.7 %collective-permute-start.3 = (bf16[15,128,128]{2,1,0:T(8,128)(2,1)S(1)}, bf16[15,128,128]{2,1,0:T(8,128)(2,1)S(1)}, u32[]{:S(2)}, u32[]{:S(2)}) collective-permute-start(bf16[15,128,128]{2,1,0:T(8,128)(2,1)S(1)} %collective-permute-done.2.near0_ref), channel_id=1, source_target_pairs={{0,64},{64,128},{128,192},{192,0},{1,65},{65,129},{129,193},{193,1... | collective-permute-start | bytes 1474568 | tf_op jit(solution)/shard_map/ppermute | solution.py:448
  19.9 1.1 %collective-permute-start.4 = (bf16[15,128,128]{2,1,0:T(8,128)(2,1)S(1)}, bf16[15,128,128]{2,1,0:T(8,128)(2,1)}, u32[]{:S(2)}, u32[]{:S(2)}) collective-permute-start(bf16[15,128,128]{2,1,0:T(8,128)(2,1)S(1)} %collective-permute-done.2.near0_ref), channel_id=1, source_target_pairs={{0,128},{64,192},{128,0},{192,64},{1,129},{65,193},{129,1},{193,65... | collective-permute-start | bytes 1474568 | tf_op jit(solution)/shard_map/ppermute | solution.py:448
  21.0 2.4 %collective-permute-start.5 = (bf16[15,128,128]{2,1,0:T(8,128)(2,1)S(1)}, bf16[15,128,128]{2,1,0:T(8,128)(2,1)}, u32[]{:S(2)}, u32[]{:S(2)}) collective-permute-start(bf16[15,128,128]{2,1,0:T(8,128)(2,1)S(1)} %collective-permute-done.2.near0_ref), channel_id=1, source_target_pairs={{0,192},{64,0},{128,64},{192,128},{1,193},{65,1},{129,65},{193,129... | collective-permute-start | bytes 1474568 | tf_op jit(solution)/shard_map/ppermute | solution.py:448
  23.7 0.1 fusion.155
  23.8 0.1 fusion.143
  24.0 0.1 pad_add_fusion.1
  24.1 1.0 %convolution_reduce_fusion = f32[]{:T(128)} fusion(bf16[768,64]{1,0:T(8,128)(2,1)S(1)} %copy-done.2, u32[4,780]{1,0:T(4,128)S(1)} %get-tuple-element.53, u32[4,780]{1,0:T(4,128)S(1)} %get-tuple-element.52, u32[768]{0:T(1024)S(1)} %not_select_fusion, u32[768]{0:T(1024)S(1)} %get-tuple-element.48, pred[768]{0:T(1024)(128)(4,1)S(1)} %get-tuple-element.75, ...), kind=kOutput, calls=%fused_computation.1 | convolution fusion | flops 623871 | bytes 525316 | tf_op jit(solution)/shard_map/dot_general | solution.py:363
  25.8 15.5 %local_products.1 = (f32[61,128,128]{2,1,0:T(8,128)S(1)}, bf16[241,128,128]{2,1,0:T(8,128)(2,1)S(1)}, s32[1216]{0:T(1024)S(1)}, s32[1216]{0:T(1024)S(1)}, s32[8]{0:T(128)S(1)}) custom-call(s32[8]{0:T(128)S(1)} %broadcast_in_dim.231.start_ref, s32[2368]{0:T(1024)S(1)} %concatenate.78.table_ref, s32[240]{0:T(256)S(1)} %reshape.318.place_ref, ...), custom_call_target="tpu_custom_call" | custom-call | flops 2000000000 | bytes 8000000 | tf_op jit(solution)/shard_map/local_products/pallas_call | solution.py:157
  41.3 3.8 %near_products.1.acc_in = f32[61,128,128]{2,1,0:T(8,128)S(1)} custom-call(s32[8]{0:T(128)S(1)} %broadcast_in_dim.235.layer_ref, s32[8]{0:T(128)S(1)} %get-tuple-element.31.size_ref, s32[1216]{0:T(1024)S(1)} %get-tuple-element.33.list_ref, f32[61,128,128]{2,1,0:T(8,128)S(1)} %get-tuple-element.34.acc_in, ...), custom_call_target="tpu_custom_call", output_to_operand_aliasing={{}: (3, {})} | custom-call | tf_op jit(solution)/shard_map/near_products/pallas_call | solution.py:215
  45.1 2.2 %collective-permute-done.6.first_ref = bf16[68,128,128]{2,1,0:T(8,128)(2,1)} collective-permute-done((bf16[68,128,128]{2,1,0:T(8,128)(2,1)S(1)}, bf16[68,128,128]{2,1,0:T(8,128)(2,1)}, u32[]{:S(2)}, u32[]{:S(2)}) %collective-permute-start.6) | collective-permute-done | bytes 2228256 | tf_op jit(solution)/shard_map/ppermute | solution.py:451
  47.4 3.9 %far_products.1 = (bf16[60,128,128]{2,1,0:T(8,128)(2,1)}, f32[61,128,128]{2,1,0:T(8,128)S(1)}) custom-call(s32[8]{0:T(128)S(1)} %broadcast_in_dim.230.more_ref, s32[8]{0:T(128)S(1)} %get-tuple-element.31.size_ref, s32[1216]{0:T(1024)S(1)} %get-tuple-element.32.list_ref, f32[61,128,128]{2,1,0:T(8,128)S(1)} %near_products.1.acc_in, ...), custom_call_target="tpu_custom_call", output_to_operand_aliasing={{1}: (3, {})} | custom-call | tf_op jit(solution)/shard_map/far_products/pallas_call | solution.py:281
  (73 shorter events, 2.4 us)
Async XLA Ops:
  0.0 23.4 %collective-permute-start.1 = (bf16[240,128,128]{2,1,0:T(8,128)(2,1)}, bf16[240,128,128]{2,1,0:T(8,128)(2,1)}, u32[]{:S(2)}, u32[]{:S(2)}) collective-permute-start(bf16[240,128,128]{2,1,0:T(8,128)(2,1)} %bitcast.23), channel_id=1, source_target_pairs={{0,1},{1,0},{2,3},{3,2},{4,5},{5,4},{6,7},{7,6},{8,9},{9,8},{10,11... | collective-permute-start | bytes 23592968 | tf_op jit(solution)/shard_map/ppermute | solution.py:382
  1.1 17.2 %collective-permute-start.2 = (bf16[15,128,128]{2,1,0:T(8,128)(2,1)S(1)}, bf16[15,128,128]{2,1,0:T(8,128)(2,1)S(1)}, u32[]{:S(2)}, u32[]{:S(2)}) collective-permute-start(bf16[15,128,128]{2,1,0:T(8,128)(2,1)S(1)} %bitcast.27), channel_id=1, source_target_pairs={{0,63},{1,2},{2,1},{3,4},{4,3},{5,6},{6,5},{7,8},{8,7},{9,10},{10,... | collective-permute-start | bytes 1474568 | tf_op jit(solution)/shard_map/ppermute | solution.py:394
  14.0 9.4 %copy-start = (s32[768,20]{0,1:T(8,128)S(1)}, s32[768,20]{0,1:T(8,128)}, u32[]{:S(2)}) copy-start(s32[768,20]{0,1:T(8,128)} %param.7) | copy-start | bytes 184324
  14.0 9.4 %copy-start.1 = (s32[768]{0:T(1024)S(1)}, s32[768]{0:T(1024)}, u32[]{:S(2)}) copy-start(s32[768]{0:T(1024)} %param.8) | copy-start | bytes 9220
  14.0 10.1 %copy-start.2 = (bf16[768,64]{1,0:T(8,128)(2,1)S(1)}, bf16[768,64]{1,0:T(8,128)(2,1)}, u32[]{:S(2)}) copy-start(bf16[768,64]{1,0:T(8,128)(2,1)} %constant.250.clone) | copy-start | bytes 294916
  17.0 30.4 %collective-permute-start.6 = (bf16[68,128,128]{2,1,0:T(8,128)(2,1)S(1)}, bf16[68,128,128]{2,1,0:T(8,128)(2,1)}, u32[]{:S(2)}, u32[]{:S(2)}) collective-permute-start(bf16[68,128,128]{2,1,0:T(8,128)(2,1)S(1)} %pack.3), channel_id=1, source_target_pairs={{0,63},{1,2},{2,1},{3,4},{4,3},{5,6},{6,5},{7,8},{8,7},{9,10},{10,... | collective-permute-start | bytes 6684680 | tf_op jit(solution)/shard_map/ppermute | solution.py:451
  18.2 23.0 %collective-permute-start.3 = (bf16[15,128,128]{2,1,0:T(8,128)(2,1)S(1)}, bf16[15,128,128]{2,1,0:T(8,128)(2,1)S(1)}, u32[]{:S(2)}, u32[]{:S(2)}) collective-permute-start(bf16[15,128,128]{2,1,0:T(8,128)(2,1)S(1)} %collective-permute-done.2.near0_ref), channel_id=1, source_target_pairs={{0,64},{64,128},{128,192},{192,0},{1,65},{65,129},{129,193},{193,1... | collective-permute-start | bytes 1474568 | tf_op jit(solution)/shard_map/ppermute | solution.py:448
  19.9 21.3 %collective-permute-start.4 = (bf16[15,128,128]{2,1,0:T(8,128)(2,1)S(1)}, bf16[15,128,128]{2,1,0:T(8,128)(2,1)}, u32[]{:S(2)}, u32[]{:S(2)}) collective-permute-start(bf16[15,128,128]{2,1,0:T(8,128)(2,1)S(1)} %collective-permute-done.2.near0_ref), channel_id=1, source_target_pairs={{0,128},{64,192},{128,0},{192,64},{1,129},{65,193},{129,1},{193,65... | collective-permute-start | bytes 1474568 | tf_op jit(solution)/shard_map/ppermute | solution.py:448
  21.0 20.3 %collective-permute-start.5 = (bf16[15,128,128]{2,1,0:T(8,128)(2,1)S(1)}, bf16[15,128,128]{2,1,0:T(8,128)(2,1)}, u32[]{:S(2)}, u32[]{:S(2)}) collective-permute-start(bf16[15,128,128]{2,1,0:T(8,128)(2,1)S(1)} %collective-permute-done.2.near0_ref), channel_id=1, source_target_pairs={{0,192},{64,0},{128,64},{192,128},{1,193},{65,1},{129,65},{193,129... | collective-permute-start | bytes 1474568 | tf_op jit(solution)/shard_map/ppermute | solution.py:448

commit v7 on v6

--- a/solution.py
+++ b/solution.py
@@ -56,7 +56,7 @@
             )
             rhs = jnp.concatenate([v_ref[e0 & 1023], v_ref[e1 & 1023]], axis=0)
             parts.append(
-                (e0 >> 18, jnp.dot(lhs, rhs, preferred_element_type=jnp.float32))
+                ((e0 >> 18) & 63, jnp.dot(lhs, rhs, preferred_element_type=jnp.float32))
             )
         for out, part in parts:
             acc_ref[out] += part
@@ -90,12 +90,13 @@
     count = rows * slots
     outs = rows * quarter
     size = 2 * UNROLL
+    load_a = pltpu.make_async_copy(blocks_ref, a_ref.at[pl.ds(0, count)], sem.at[1])
+    load_a.start()
     load = pltpu.make_async_copy(inner_ref, inner_v.at[pl.ds(count, count)], sem.at[0])
     load.start()
-    load_own = pltpu.make_async_copy(blocks_ref, inner_v.at[pl.ds(0, count)], sem.at[1])
-    load_own.start()
-    load_a = pltpu.make_async_copy(blocks_ref, a_ref.at[pl.ds(0, count)], sem.at[2])
-    load_a.start()
+    move_own = pltpu.make_async_copy(
+        a_ref.at[pl.ds(0, count)], inner_v.at[pl.ds(0, count)], sem.at[2]
+    )
     a_ref[count] = jnp.zeros(a_ref.shape[1:], a_ref.dtype)
 
     def clear(o, carry):
@@ -118,13 +119,13 @@
                 e_own, e_near, e_far = ends
                 for m in range(slots):
                     code = table_ref[terms_at[m] + (j_at + 2 * BAND)]
-                    entry = (code & 1023) + (tag + (m << 10))
+                    entry = code + (tag + (m << 10))
                     own_ref[e_own] = entry
                     near_ref[e_near] = entry
                     far_ref[e_far] = entry
-                    e_own += (code >> 10) & 1
-                    e_near += (code >> 11) & 1
-                    e_far += code >> 12
+                    e_own += (code >> 25) & 1
+                    e_near += (code >> 26) & 1
+                    e_far += code >> 27
                 none = ((i * quarter + p) << 18) | (count << 10)
                 own_ref[e_own] = none
                 near_ref[e_near] = none
@@ -136,7 +137,10 @@
         return lax.fori_loop(0, quarter, one_output, ends)
 
     zero = jnp.int32(0)
-    e_own, e_near, e_far = lax.fori_loop(0, rows, one_row, (zero, zero, zero))
+    half = lax.fori_loop(0, rows // 2, one_row, (zero, zero, zero))
+    load_a.wait()
+    move_own.start()
+    e_own, e_near, e_far = lax.fori_loop(rows // 2, rows, one_row, half)
     for u in range(size):
         none = (outs << 18) | (count << 10)
         own_ref[e_own + u] = none
@@ -144,8 +148,7 @@
         far_ref[e_far + u] = none
     size_ref[0] = (e_near + size - 1) // size * size
     size_ref[1] = (e_far + size - 1) // size * size
-    load_own.wait()
-    load_a.wait()
+    move_own.wait()
     load.wait()
     run_list(own_ref, (e_own + size - 1) // size * size, a_ref, inner_v, acc_ref)
 
@@ -450,17 +453,17 @@
     ]
     outer = lax.ppermute(packed, ("row", "col"), outer_pairs)
 
-    code = jnp.where(get, (4 << 10) + get_pos, 0)
+    code = jnp.where(get, (4 << 25) + get_pos, 0)
     code = jnp.where(even, code.reshape(rows, slots)[::-1], code.reshape(rows, slots))
     row_at = jnp.arange(rows, dtype=jnp.int32)[:, None] - jnp.where(even, rows - NEAR_ROWS, 0)
     sent = (row_at >= 0) & (row_at < NEAR_ROWS) & (slot_ids < NEAR_SLOTS)
     sent_at = (slot_ids // share * NEAR_ROWS + row_at) * share + slot_ids % share
     far_live = jnp.where(even, live[0], live[2])
-    code = jnp.where(sent & far_live, (2 << 10) + sent_at, code)
+    code = jnp.where(sent & far_live, (2 << 25) + sent_at, code)
     ids = ids.reshape(rows, slots)
-    own = jnp.where(live[1], (1 << 10) + ids, 0)
+    own = jnp.where(live[1], (1 << 25) + ids, 0)
     near = jnp.where(even, live[2], live[0])
-    near = jnp.where(near, (1 << 10) + span + ids, 0)
+    near = jnp.where(near, (1 << 25) + span + ids, 0)
     codes = jnp.concatenate(
         [jnp.where(even, code, near), own, jnp.where(even, near, code)], axis=0
     )

time: 52 us -> 52.1 us (level)
  Pallas kernels: 26.1 us -> 26.7 us
where the time goes in v7:
time: 52.1 us; the launch traced here: 51.7 us
  Pallas kernels  26.7 us (51%)
  starting transfers between devices  13.7 us (26%)
  local copies, waits for them, and re-layouts  3.84 us (7%)
  other arithmetic  3.11 us (6%)
  waiting for transfers between devices  2.17 us (4%)
  matrix products  1.12 us (2%)
  between operations  1.05 us (2%)
    pallas_call x1, Pallas kernels, local_products(): pl.pallas_call(functools.partial(local_kernel, rows, slots, quarter), out...  15.6 us
    ppermute x1, starting transfers between devices, per_device(): near_mine = lax.ppermute(near_rows, ('row', 'col'), outer_pairs)  8.5 us
    ppermute x3, starting transfers between devices, per_device(): lax.ppermute(near_mine, 'layer', [(x, (x + d) % layers) for x in range(la...  5.06 us
    pallas_call x1, Pallas kernels, far_products(): pl.pallas_call(functools.partial(far_kernel, rows, quarter), out_shape=(j...  4.31 us
    pallas_call x1, Pallas kernels, near_products(): pl.pallas_call(near_kernel, out_shape=jax.ShapeDtypeStruct(acc.shape, acc...  3.83 us
    pallas_call x1, Pallas kernels, pack(): pl.pallas_call(functools.partial(pack_kernel, start, size), out_shape=jax...  2.95 us
    ppermute x1, waiting for transfers between devices, per_device(): outer = lax.ppermute(packed, ('row', 'col'), outer_pairs)  2.15 us
    dynamic_slice x1, local copies, waits for them, and re-layouts, per_device(): lax.dynamic_slice(values, (jnp.where(even, 0, rows - NEAR_ROWS), layer *...  1.06 us
  transfers between devices with their start and end apart: 6, of which 1 were waited for; matrix products, arithmetic and copies ran while one was open for 16% of the time, Pallas kernels for 43%

profile of v7, /device:TPU:2, one launch (start us, length us, event | category | flops | bytes accessed | tf_op | source)
XLA Modules:
  0.0 51.7 jit_solution(6312257739509956405)
XLA Ops:
  0.0 1.1 %constant_dynamic-slice_fusion = bf16[5,3,128,128]{3,2,1,0:T(8,128)(2,1)S(1)} fusion(bf16[12,20,128,128]{3,2,1,0:T(8,128)(2,1)} %param.6, s32[]{:T(128)S(6)} %select_n.443, s32[]{:T(128)S(6)} %select_n.444), kind=kLoop, calls=%fused_computation.295 | loop fusion | bytes 983048 | tf_op jit(solution)/shard_map/dynamic_slice | solution.py:392
  1.1 8.5 %collective-permute-start.2 = (bf16[15,128,128]{2,1,0:T(8,128)(2,1)S(1)}, bf16[15,128,128]{2,1,0:T(8,128)(2,1)S(1)}, u32[]{:S(2)}, u32[]{:S(2)}) collective-permute-start(bf16[15,128,128]{2,1,0:T(8,128)(2,1)S(1)} %bitcast.27), channel_id=1, source_target_pairs={{0,63},{1,2},{2,1},{3,4},{4,3},{5,6},{6,5},{7,8},{8,7},{9,10},{10,... | collective-permute-start | bytes 1474568 | tf_op jit(solution)/shard_map/ppermute | solution.py:397
  9.6 0.7 %broadcast_in_dim.197 = s32[1,768]{1,0:T(1,128)S(1)} reshape(s32[768]{0:T(1024)} %param.8) | data formatting | bytes 6144 | tf_op jit(solution)/shard_map/broadcast_in_dim | solution.py:398
  10.3 0.9 %pad_add_fusion = s32[21,768]{1,0:T(8,128)S(1)} fusion(s32[1,768]{1,0:T(1,128)S(1)} %broadcast_in_dim.197, s32[20,768]{1,0:T(8,128)} %bitcast.28), kind=kLoop, calls=%fused_computation.15 | loop fusion | flops 16128 | bytes 129024 | tf_op jit(solution)/shard_map/concatenate | solution.py:398
  11.6 0.1 copy.30
  11.7 0.1 copy.31
  11.9 0.1 fusion.67
  12.2 0.1 select_reduce_fusion.3
  12.3 0.1 select_reduce_fusion.4
  12.7 0.1 copy.33
  12.9 0.1 copy.34
  13.0 0.1 stack.32
  13.3 0.1 and.425
  13.5 0.1 copy.32
  13.7 0.2 convolution_convert_fusion
  13.9 0.1 select_reduce_fusion.1.idx_ref
  14.0 3.0 %pack.3 = bf16[68,128,128]{2,1,0:T(8,128)(2,1)S(1)} custom-call(s32[140]{0:T(256)S(1)} %select_reduce_fusion.1.idx_ref, bf16[240,128,128]{2,1,0:T(8,128)(2,1)} %bitcast.24), custom_call_target="tpu_custom_call" | custom-call | tf_op jit(solution)/shard_map/pack/pallas_call | solution.py:37
  17.0 0.1 collective-permute-start.6
  17.2 0.1 copy.36
  17.7 0.3 select_reduce_fusion
  18.0 0.1 copy.37
  18.2 1.8 %collective-permute-start.3 = (bf16[15,128,128]{2,1,0:T(8,128)(2,1)S(1)}, bf16[15,128,128]{2,1,0:T(8,128)(2,1)S(1)}, u32[]{:S(2)}, u32[]{:S(2)}) collective-permute-start(bf16[15,128,128]{2,1,0:T(8,128)(2,1)S(1)} %collective-permute-done.2.near0_ref), channel_id=1, source_target_pairs={{0,64},{64,128},{128,192},{192,0},{1,65},{65,129},{129,193},{193,1... | collective-permute-start | bytes 1474568 | tf_op jit(solution)/shard_map/ppermute | solution.py:451
  20.0 0.9 %collective-permute-start.4 = (bf16[15,128,128]{2,1,0:T(8,128)(2,1)S(1)}, bf16[15,128,128]{2,1,0:T(8,128)(2,1)}, u32[]{:S(2)}, u32[]{:S(2)}) collective-permute-start(bf16[15,128,128]{2,1,0:T(8,128)(2,1)S(1)} %collective-permute-done.2.near0_ref), channel_id=1, source_target_pairs={{0,128},{64,192},{128,0},{192,64},{1,129},{65,193},{129,1},{193,65... | collective-permute-start | bytes 1474568 | tf_op jit(solution)/shard_map/ppermute | solution.py:451
  20.9 2.4 %collective-permute-start.5 = (bf16[15,128,128]{2,1,0:T(8,128)(2,1)S(1)}, bf16[15,128,128]{2,1,0:T(8,128)(2,1)}, u32[]{:S(2)}, u32[]{:S(2)}) collective-permute-start(bf16[15,128,128]{2,1,0:T(8,128)(2,1)S(1)} %collective-permute-done.2.near0_ref), channel_id=1, source_target_pairs={{0,192},{64,0},{128,64},{192,128},{1,193},{65,1},{129,65},{193,129... | collective-permute-start | bytes 1474568 | tf_op jit(solution)/shard_map/ppermute | solution.py:451
  23.7 0.1 fusion.155
  23.8 0.1 fusion.143
  23.9 0.1 pad_add_fusion.1
  24.0 1.0 %convolution_reduce_fusion = f32[]{:T(128)} fusion(bf16[768,64]{1,0:T(8,128)(2,1)S(1)} %copy-done.2, u32[4,780]{1,0:T(4,128)S(1)} %get-tuple-element.53, u32[4,780]{1,0:T(4,128)S(1)} %get-tuple-element.52, u32[768]{0:T(1024)S(1)} %not_select_fusion, u32[768]{0:T(1024)S(1)} %get-tuple-element.48, pred[768]{0:T(1024)(128)(4,1)S(1)} %get-tuple-element.75, ...), kind=kOutput, calls=%fused_computation.1 | convolution fusion | flops 623871 | bytes 525316 | tf_op jit(solution)/shard_map/dot_general | solution.py:366
  25.7 15.6 %local_products.1 = (f32[61,128,128]{2,1,0:T(8,128)S(1)}, bf16[241,128,128]{2,1,0:T(8,128)(2,1)S(1)}, s32[1216]{0:T(1024)S(1)}, s32[1216]{0:T(1024)S(1)}, s32[8]{0:T(128)S(1)}) custom-call(s32[8]{0:T(128)S(1)} %broadcast_in_dim.231.start_ref, s32[2368]{0:T(1024)S(1)} %concatenate.78.table_ref, s32[240]{0:T(256)S(1)} %reshape.318.place_ref, ...), custom_call_target="tpu_custom_call" | custom-call | flops 2000000000 | bytes 8000000 | tf_op jit(solution)/shard_map/local_products/pallas_call | solution.py:160
  41.4 3.8 %near_products.1.acc_in = f32[61,128,128]{2,1,0:T(8,128)S(1)} custom-call(s32[8]{0:T(128)S(1)} %broadcast_in_dim.235.layer_ref, s32[8]{0:T(128)S(1)} %get-tuple-element.31.size_ref, s32[1216]{0:T(1024)S(1)} %get-tuple-element.33.list_ref, f32[61,128,128]{2,1,0:T(8,128)S(1)} %get-tuple-element.34.acc_in, ...), custom_call_target="tpu_custom_call", output_to_operand_aliasing={{}: (3, {})} | custom-call | tf_op jit(solution)/shard_map/near_products/pallas_call | solution.py:218
  45.2 2.2 %collective-permute-done.6.first_ref = bf16[68,128,128]{2,1,0:T(8,128)(2,1)} collective-permute-done((bf16[68,128,128]{2,1,0:T(8,128)(2,1)S(1)}, bf16[68,128,128]{2,1,0:T(8,128)(2,1)}, u32[]{:S(2)}, u32[]{:S(2)}) %collective-permute-start.6) | collective-permute-done | bytes 2228256 | tf_op jit(solution)/shard_map/ppermute | solution.py:454
  47.4 4.3 %far_products.1 = (bf16[60,128,128]{2,1,0:T(8,128)(2,1)}, f32[61,128,128]{2,1,0:T(8,128)S(1)}) custom-call(s32[8]{0:T(128)S(1)} %broadcast_in_dim.230.more_ref, s32[8]{0:T(128)S(1)} %get-tuple-element.31.size_ref, s32[1216]{0:T(1024)S(1)} %get-tuple-element.32.list_ref, f32[61,128,128]{2,1,0:T(8,128)S(1)} %near_products.1.acc_in, ...), custom_call_target="tpu_custom_call", output_to_operand_aliasing={{1}: (3, {})} | custom-call | tf_op jit(solution)/shard_map/far_products/pallas_call | solution.py:284
  (73 shorter events, 2.4 us)
Async XLA Ops:
  0.0 23.3 %collective-permute-start.1 = (bf16[240,128,128]{2,1,0:T(8,128)(2,1)}, bf16[240,128,128]{2,1,0:T(8,128)(2,1)}, u32[]{:S(2)}, u32[]{:S(2)}) collective-permute-start(bf16[240,128,128]{2,1,0:T(8,128)(2,1)} %bitcast.23), channel_id=1, source_target_pairs={{0,1},{1,0},{2,3},{3,2},{4,5},{5,4},{6,7},{7,6},{8,9},{9,8},{10,11... | collective-permute-start | bytes 23592968 | tf_op jit(solution)/shard_map/ppermute | solution.py:385
  1.1 17.2 %collective-permute-start.2 = (bf16[15,128,128]{2,1,0:T(8,128)(2,1)S(1)}, bf16[15,128,128]{2,1,0:T(8,128)(2,1)S(1)}, u32[]{:S(2)}, u32[]{:S(2)}) collective-permute-start(bf16[15,128,128]{2,1,0:T(8,128)(2,1)S(1)} %bitcast.27), channel_id=1, source_target_pairs={{0,63},{1,2},{2,1},{3,4},{4,3},{5,6},{6,5},{7,8},{8,7},{9,10},{10,... | collective-permute-start | bytes 1474568 | tf_op jit(solution)/shard_map/ppermute | solution.py:397
  14.0 9.3 %copy-start = (s32[768,20]{0,1:T(8,128)S(1)}, s32[768,20]{0,1:T(8,128)}, u32[]{:S(2)}) copy-start(s32[768,20]{0,1:T(8,128)} %param.7) | copy-start | bytes 184324
  14.0 9.3 %copy-start.1 = (s32[768]{0:T(1024)S(1)}, s32[768]{0:T(1024)}, u32[]{:S(2)}) copy-start(s32[768]{0:T(1024)} %param.8) | copy-start | bytes 9220
  14.0 10.0 %copy-start.2 = (bf16[768,64]{1,0:T(8,128)(2,1)S(1)}, bf16[768,64]{1,0:T(8,128)(2,1)}, u32[]{:S(2)}) copy-start(bf16[768,64]{1,0:T(8,128)(2,1)} %constant.250.clone) | copy-start | bytes 294916
  17.0 30.4 %collective-permute-start.6 = (bf16[68,128,128]{2,1,0:T(8,128)(2,1)S(1)}, bf16[68,128,128]{2,1,0:T(8,128)(2,1)}, u32[]{:S(2)}, u32[]{:S(2)}) collective-permute-start(bf16[68,128,128]{2,1,0:T(8,128)(2,1)S(1)} %pack.3), channel_id=1, source_target_pairs={{0,63},{1,2},{2,1},{3,4},{4,3},{5,6},{6,5},{7,8},{8,7},{9,10},{10,... | collective-permute-start | bytes 6684680 | tf_op jit(solution)/shard_map/ppermute | solution.py:454
  18.2 23.1 %collective-permute-start.3 = (bf16[15,128,128]{2,1,0:T(8,128)(2,1)S(1)}, bf16[15,128,128]{2,1,0:T(8,128)(2,1)S(1)}, u32[]{:S(2)}, u32[]{:S(2)}) collective-permute-start(bf16[15,128,128]{2,1,0:T(8,128)(2,1)S(1)} %collective-permute-done.2.near0_ref), channel_id=1, source_target_pairs={{0,64},{64,128},{128,192},{192,0},{1,65},{65,129},{129,193},{193,1... | collective-permute-start | bytes 1474568 | tf_op jit(solution)/shard_map/ppermute | solution.py:451
  20.0 21.4 %collective-permute-start.4 = (bf16[15,128,128]{2,1,0:T(8,128)(2,1)S(1)}, bf16[15,128,128]{2,1,0:T(8,128)(2,1)}, u32[]{:S(2)}, u32[]{:S(2)}) collective-permute-start(bf16[15,128,128]{2,1,0:T(8,128)(2,1)S(1)} %collective-permute-done.2.near0_ref), channel_id=1, source_target_pairs={{0,128},{64,192},{128,0},{192,64},{1,129},{65,193},{129,1},{193,65... | collective-permute-start | bytes 1474568 | tf_op jit(solution)/shard_map/ppermute | solution.py:451
  20.9 20.5 %collective-permute-start.5 = (bf16[15,128,128]{2,1,0:T(8,128)(2,1)S(1)}, bf16[15,128,128]{2,1,0:T(8,128)(2,1)}, u32[]{:S(2)}, u32[]{:S(2)}) collective-permute-start(bf16[15,128,128]{2,1,0:T(8,128)(2,1)S(1)} %collective-permute-done.2.near0_ref), channel_id=1, source_target_pairs={{0,192},{64,0},{128,64},{192,128},{1,193},{65,1},{129,65},{193,129... | collective-permute-start | bytes 1474568 | tf_op jit(solution)/shard_map/ppermute | solution.py:451
